TPU v7x, 512 devices: a whole 4x4x16 slice. The times are simulated.
512 devices in a mesh: ctx: 128 (over z, y, x_hi), tp: 4 (over x_lo, core).
Axes of the slice: x: 4 (x_hi: 2, x_lo: 2; x = x_hi * 2 + x_lo), y: 4, z: 16, core: 2. Of those that a mesh axis runs over, the one named last changes fastest.
Arguments:
- query_heads: bfloat16 [16384, 4096], P('ctx', 'tp'), may hold values from -16 to 16
- key_heads_wide: bfloat16 [16384, 512], P(('ctx', 'tp')), may hold values from -16 to 16
- value_heads_wide: bfloat16 [16384, 512], P(('ctx', 'tp')), may hold values from -6 to 6
- grad_output: bfloat16 [16384, 4096], P('ctx', 'tp'), may hold values from -48 to 48
Outputs:
- grad_query: float32 [16384, 4096], P('ctx', 'tp')
- key_gradient: float32 [16384, 512], P(('ctx', 'tp'))
- value_gradient: float32 [16384, 512], P(('ctx', 'tp'))
All inputs are finite; a program needn't handle non-finite values.
Results may differ from a plain program's by a relative error of at most 0.007.
Values may be sent and summed in bfloat16 or wider, within the bound.
No kernel may reach another device: no remote copies, remote signals or barrier semaphores. Data moves between devices by JAX's collectives and lax.ppermute only.
A program may use at most 64 MiB of HBM per device.

v0:
```python
import math

import jax
import jax.numpy as jnp
from jax import lax
from jax.sharding import PartitionSpec as P

HEAD_SIZE = 128
QUERY_HEADS = 32
KEY_VALUE_HEADS = 4


def shifted(block, axis, distance):
    devices = range(lax.axis_size(axis))
    route = [((i - distance) % len(devices), i) for i in devices]
    return lax.ppermute(block, axis, route)


def shards(query_heads, key_heads_wide, value_heads_wide, grad_output):
    ctx_count = lax.axis_size("ctx")
    group_devices = ctx_count // 4
    half_span = group_devices // 2
    position = lax.axis_index("ctx")
    head_position = lax.axis_index("tp")
    shared_head_local = KEY_VALUE_HEADS // lax.axis_size("tp")
    query_heads_per_group = QUERY_HEADS // KEY_VALUE_HEADS
    rows_here = query_heads.shape[0]
    kv_width = shared_head_local * HEAD_SIZE
    score_scale = 1.0 / math.sqrt(HEAD_SIZE)
    keys_local, values_local = (
        lax.all_to_all(key_heads_wide, "tp", split_axis=1, concat_axis=0, tiled=True),
        lax.all_to_all(value_heads_wide, "tp", split_axis=1, concat_axis=0, tiled=True),
    )
    own_block = jnp.concatenate([keys_local, values_local], axis=1)
    rolled_heads = head_position * shared_head_local >= KEY_VALUE_HEADS // 2
    offset = jnp.where(rolled_heads, half_span, 0)
    rank_in_group = jnp.mod(position - offset, ctx_count) % group_devices
    query_split = query_heads.reshape(
        rows_here, shared_head_local, query_heads_per_group, HEAD_SIZE
    )
    grad_split = grad_output.reshape(rows_here, shared_head_local, query_heads_per_group, HEAD_SIZE)
    query_index = lax.broadcasted_iota(jnp.int32, (rows_here, 1, 1, rows_here), 0)
    key_index = lax.broadcasted_iota(jnp.int32, (rows_here, 1, 1, rows_here), 3)
    causal = key_index <= query_index
    score_shape = (rows_here, shared_head_local, query_heads_per_group, rows_here)
    stat_shape = (rows_here, shared_head_local, query_heads_per_group)

    def split_block(kv_block):
        key_block = kv_block[:, :kv_width].reshape(rows_here, shared_head_local, HEAD_SIZE)
        value_block = kv_block[:, kv_width:].reshape(rows_here, shared_head_local, HEAD_SIZE)
        return (key_block, value_block)

    def scores_of(key_block, distance):
        products = (
            jnp.einsum("thrd,uhd->thru", query_split, key_block, preferred_element_type=jnp.float32)
            * score_scale
        )
        return jnp.where(jnp.logical_or(distance > 0, causal), products, -jnp.inf)

    def first_visit(moments, kv_block, distance):

        def first_active(unused):
            running, totals, weighted = moments
            key_block, value_block = split_block(kv_block)
            masked = scores_of(key_block, distance)
            slopes = jnp.einsum(
                "thrd,uhd->thru", grad_split, value_block, preferred_element_type=jnp.float32
            )
            highest = jnp.maximum(running, jnp.max(masked, axis=3))
            factor = jnp.exp(running - highest)
            weights = jnp.exp(masked - highest[..., None])
            totals = factor * totals + jnp.sum(weights, axis=3)
            weighted = factor * weighted + jnp.sum(weights * slopes, axis=3)
            return ((highest, totals, weighted), slopes)

        def first_passive(unused):
            return (moments, jnp.zeros(score_shape, jnp.float32))

        return lax.cond(distance <= rank_in_group, first_active, first_passive, None)

    start_moments = (
        jnp.full(stat_shape, -jnp.inf, jnp.float32),
        jnp.zeros(stat_shape, jnp.float32),
        jnp.zeros(stat_shape, jnp.float32),
    )
    moments, slopes = first_visit(start_moments, own_block, 0)
    stored = jnp.zeros((group_devices,) + score_shape, jnp.float32)
    stored = lax.dynamic_update_index_in_dim(stored, slopes, 0, 0)
    kept_blocks = jnp.zeros((1,), jnp.bfloat16)

    def cycle_forward(distance, loop_state):
        moments, kv_block, stored, kept_blocks = loop_state
        kv_block = shifted(kv_block, "ctx", 1)
        moments, slopes = first_visit(moments, kv_block, distance)
        stored = lax.dynamic_update_index_in_dim(stored, slopes, distance, 0)
        return (moments, kv_block, stored, kept_blocks)

    moments, unused_block, stored, kept_blocks = lax.fori_loop(
        1, group_devices, cycle_forward, (moments, own_block, stored, kept_blocks)
    )
    running, totals, weighted = moments
    log_norm = running + jnp.log(totals)
    centre = weighted / totals

    def slopes_at(distance):
        return lax.dynamic_index_in_dim(stored, distance, 0, keepdims=False)

    def second_visit(kv_block, slopes, distance):

        def second_active(unused):
            key_block, value_block = split_block(kv_block)
            masked = scores_of(key_block, distance)
            soft_weights = jnp.exp(masked - log_norm[..., None])
            soft_low = soft_weights.astype(jnp.bfloat16)
            score_grad = (soft_weights * (slopes - centre[..., None])).astype(jnp.bfloat16)
            query_part = (
                jnp.einsum(
                    "thru,uhd->thrd", score_grad, key_block, preferred_element_type=jnp.float32
                )
                * score_scale
            )
            key_part = (
                jnp.einsum(
                    "thru,thrd->uhd", score_grad, query_split, preferred_element_type=jnp.float32
                )
                * score_scale
            )
            value_part = jnp.einsum(
                "thru,thrd->uhd", soft_low, grad_split, preferred_element_type=jnp.float32
            )
            grad_part = jnp.concatenate(
                [key_part.reshape(rows_here, kv_width), value_part.reshape(rows_here, kv_width)],
                axis=1,
            )
            return (query_part, grad_part)

        def second_passive(unused):
            return (
                jnp.zeros(
                    (rows_here, shared_head_local, query_heads_per_group, HEAD_SIZE), jnp.float32
                ),
                jnp.zeros((rows_here, 2 * kv_width), jnp.float32),
            )

        return lax.cond(distance <= rank_in_group, second_active, second_passive, None)

    query_grad, kv_grads = second_visit(own_block, slopes_at(0), 0)

    def visit_again(distance, loop_state):
        query_grad, kv_block, kv_grads = loop_state
        kv_block = shifted(kv_block, "ctx", 1)
        kv_grads = shifted(kv_grads, "ctx", 1)
        query_part, grad_part = second_visit(kv_block, slopes_at(distance), distance)
        return (query_grad + query_part, kv_block, kv_grads + grad_part)

    query_grad, unused_block, kv_grads = lax.fori_loop(
        1, group_devices, visit_again, (query_grad, own_block, kv_grads)
    )
    kv_grads = shifted(kv_grads, "ctx", 1 - group_devices)
    grad_query = query_grad.reshape(
        rows_here, shared_head_local * query_heads_per_group * HEAD_SIZE
    )
    key_grad = kv_grads[:, :kv_width]
    value_grad = kv_grads[:, kv_width:]
    key_gradient, value_gradient = (
        lax.all_to_all(key_grad, "tp", split_axis=0, concat_axis=1, tiled=True),
        lax.all_to_all(value_grad, "tp", split_axis=0, concat_axis=1, tiled=True),
    )
    return (grad_query, key_gradient, value_gradient)


def solution(mesh):
    return jax.shard_map(
        shards,
        mesh=mesh,
        in_specs=(P("ctx", "tp"), P(("ctx", "tp"), None), P(("ctx", "tp"), None), P("ctx", "tp")),
        out_specs=(P("ctx", "tp"), P(("ctx", "tp"), None), P(("ctx", "tp"), None)),
        check_vma=False,
    )
```

profile of v0, /device:TPU:1, one launch (start us, length us, event | category | flops | bytes accessed | tf_op | source)
XLA Modules:
  0.0 978.3 jit_solution(901979938268220464)
XLA Ops:
  2.0 10.1 %all-to-all-start = ((bf16[32,4,128]{2,0,1:T(8,128)(2,1)}), bf16[32,4,128]{2,0,1:T(8,128)(2,1)S(1)}, u32[]{:S(2)}, u32[]{:S(2)}) async-start(bf16[32,4,128]{2,0,1:T(8,128)(2,1)} %copy_bitcast_fusion.4), calls=%async_computation | async-start | bytes 65536 | tf_op jit(solution)/shard_map/all_to_all | solution.py:31
  32.8 370.1 %while.42 = (s32[]{:T(128)}, f32[128,1,8]{0,2,1:T(8,128)}, f32[128,1,8]{0,2,1:T(8,128)S(1)}, f32[128,1,8]{0,2,1:T(8,128)S(1)}, bf16[128,256]{1,0:T(8,128)(2,1)S(...) while((s32[]{:T(128)}, f32[128,1,8]{0,2,1:T(8,128)}, ...), condition=%wide.region_11.12_spmd.clone, body=%wide.region_5.11_spmd.clone.sunk | while | flops 68062208 | bytes 3969371 | solution.py:98
  34.8 10.4 %collective-permute-done = bf16[128,256]{1,0:T(8,128)(2,1)S(1)} collective-permute-done((bf16[128,256]{1,0:T(8,128)(2,1)S(1)}, bf16[128,256]{1,0:T(8,128)(2,1)S(1)}, u32[]{:S(2)}, u32[]{:S(2)}) %collective-permute-start) | collective-permute-done | bytes 65568 | tf_op jit(solution)/shard_map/while/body/eval_jaxpr/ppermute | solution.py:16
  48.0 8.8 collective-permute-done
  59.7 8.8 collective-permute-done
  83.0 8.8 collective-permute-done
  94.7 8.8 collective-permute-done
  153.1 9.1 collective-permute-done
  281.8 9.0 collective-permute-done
  340.4 9.0 collective-permute-done
  352.3 10.9 %collective-permute-done = bf16[128,256]{1,0:T(8,128)(2,1)S(1)} collective-permute-done((bf16[128,256]{1,0:T(8,128)(2,1)S(1)}, bf16[128,256]{1,0:T(8,128)(2,1)S(1)}, u32[]{:S(2)}, u32[]{:S(2)}) %collective-permute-start) | collective-permute-done | bytes 65568 | tf_op jit(solution)/shard_map/while/body/eval_jaxpr/ppermute | solution.py:16
  366.0 9.5 collective-permute-done
  378.5 10.1 %collective-permute-done = bf16[128,256]{1,0:T(8,128)(2,1)S(1)} collective-permute-done((bf16[128,256]{1,0:T(8,128)(2,1)S(1)}, bf16[128,256]{1,0:T(8,128)(2,1)S(1)}, u32[]{:S(2)}, u32[]{:S(2)}) %collective-permute-start) | collective-permute-done | bytes 65568 | tf_op jit(solution)/shard_map/while/body/eval_jaxpr/ppermute | solution.py:16
  391.5 10.5 %collective-permute-done = bf16[128,256]{1,0:T(8,128)(2,1)S(1)} collective-permute-done((bf16[128,256]{1,0:T(8,128)(2,1)S(1)}, bf16[128,256]{1,0:T(8,128)(2,1)S(1)}, u32[]{:S(2)}, u32[]{:S(2)}) %collective-permute-start) | collective-permute-done | bytes 65568 | tf_op jit(solution)/shard_map/while/body/eval_jaxpr/ppermute | solution.py:16
  405.7 427.1 %while.43 = (s32[]{:T(128)}, f32[128,1,8,128]{3,0,2,1:T(8,128)S(1)}, bf16[128,256]{1,0:T(8,128)(2,1)S(1)}, f32[128,256]{0,1:T(8,128)S(1)}, s32[]{:T(128)}, /*ind...) while((s32[]{:T(128)}, ...), condition=%wide.region_17.18_spmd.clone, body=%wide.region_14.17_spmd.clone.sunk | while | flops 135512064 | bytes 7840083 | solution.py:156
  409.6 9.5 collective-permute-done.1
  423.3 8.8 collective-permute-done.1
  436.2 8.8 collective-permute-done.1
  449.2 8.8 collective-permute-done.1
  462.1 8.8 collective-permute-done.1
  475.1 8.8 collective-permute-done.1
  488.1 10.0 %collective-permute-done.1 = bf16[128,256]{1,0:T(8,128)(2,1)S(1)} collective-permute-done((bf16[128,256]{1,0:T(8,128)(2,1)S(1)}, bf16[128,256]{1,0:T(8,128)(2,1)S(1)}, u32[]{:S(2)}, u32[]{:S(2)}) %collective-permute-start.1) | collective-permute-done | bytes 65568 | tf_op jit(solution)/shard_map/while/body/eval_jaxpr/ppermute | solution.py:16
  502.2 9.9 %collective-permute-done.1 = bf16[128,256]{1,0:T(8,128)(2,1)S(1)} collective-permute-done((bf16[128,256]{1,0:T(8,128)(2,1)S(1)}, bf16[128,256]{1,0:T(8,128)(2,1)S(1)}, u32[]{:S(2)}, u32[]{:S(2)}) %collective-permute-start.1) | collective-permute-done | bytes 65568 | tf_op jit(solution)/shard_map/while/body/eval_jaxpr/ppermute | solution.py:16
  516.3 9.8 %collective-permute-done.1 = bf16[128,256]{1,0:T(8,128)(2,1)S(1)} collective-permute-done((bf16[128,256]{1,0:T(8,128)(2,1)S(1)}, bf16[128,256]{1,0:T(8,128)(2,1)S(1)}, u32[]{:S(2)}, u32[]{:S(2)}) %collective-permute-start.1) | collective-permute-done | bytes 65568 | tf_op jit(solution)/shard_map/while/body/eval_jaxpr/ppermute | solution.py:16
  530.2 9.7 collective-permute-done.1
  544.1 9.5 collective-permute-done.1
  557.8 8.8 collective-permute-done.1
  570.7 8.8 collective-permute-done.1
  583.7 8.8 collective-permute-done.1
  596.6 8.8 collective-permute-done.1
  609.6 8.8 collective-permute-done.1
  622.5 9.5 collective-permute-done.1
  636.2 11.6 %collective-permute-done.1 = bf16[128,256]{1,0:T(8,128)(2,1)S(1)} collective-permute-done((bf16[128,256]{1,0:T(8,128)(2,1)S(1)}, bf16[128,256]{1,0:T(8,128)(2,1)S(1)}, u32[]{:S(2)}, u32[]{:S(2)}) %collective-permute-start.1) | collective-permute-done | bytes 65568 | tf_op jit(solution)/shard_map/while/body/eval_jaxpr/ppermute | solution.py:16
  652.0 8.8 collective-permute-done.1
  665.0 8.8 collective-permute-done.1
  677.9 8.8 collective-permute-done.1
  690.9 8.8 collective-permute-done.1
  703.8 9.0 collective-permute-done.1
  717.0 10.5 %collective-permute-done.1 = bf16[128,256]{1,0:T(8,128)(2,1)S(1)} collective-permute-done((bf16[128,256]{1,0:T(8,128)(2,1)S(1)}, bf16[128,256]{1,0:T(8,128)(2,1)S(1)}, u32[]{:S(2)}, u32[]{:S(2)}) %collective-permute-start.1) | collective-permute-done | bytes 65568 | tf_op jit(solution)/shard_map/while/body/eval_jaxpr/ppermute | solution.py:16
  731.6 9.8 collective-permute-done.1
  745.6 11.5 %collective-permute-done.1 = bf16[128,256]{1,0:T(8,128)(2,1)S(1)} collective-permute-done((bf16[128,256]{1,0:T(8,128)(2,1)S(1)}, bf16[128,256]{1,0:T(8,128)(2,1)S(1)}, u32[]{:S(2)}, u32[]{:S(2)}) %collective-permute-start.1) | collective-permute-done | bytes 65568 | tf_op jit(solution)/shard_map/while/body/eval_jaxpr/ppermute | solution.py:16
  761.2 10.7 %collective-permute-done.1 = bf16[128,256]{1,0:T(8,128)(2,1)S(1)} collective-permute-done((bf16[128,256]{1,0:T(8,128)(2,1)S(1)}, bf16[128,256]{1,0:T(8,128)(2,1)S(1)}, u32[]{:S(2)}, u32[]{:S(2)}) %collective-permute-start.1) | collective-permute-done | bytes 65568 | tf_op jit(solution)/shard_map/while/body/eval_jaxpr/ppermute | solution.py:16
  776.1 11.4 %collective-permute-done.1 = bf16[128,256]{1,0:T(8,128)(2,1)S(1)} collective-permute-done((bf16[128,256]{1,0:T(8,128)(2,1)S(1)}, bf16[128,256]{1,0:T(8,128)(2,1)S(1)}, u32[]{:S(2)}, u32[]{:S(2)}) %collective-permute-start.1) | collective-permute-done | bytes 65568 | tf_op jit(solution)/shard_map/while/body/eval_jaxpr/ppermute | solution.py:16
  791.7 10.7 %collective-permute-done.1 = bf16[128,256]{1,0:T(8,128)(2,1)S(1)} collective-permute-done((bf16[128,256]{1,0:T(8,128)(2,1)S(1)}, bf16[128,256]{1,0:T(8,128)(2,1)S(1)}, u32[]{:S(2)}, u32[]{:S(2)}) %collective-permute-start.1) | collective-permute-done | bytes 65568 | tf_op jit(solution)/shard_map/while/body/eval_jaxpr/ppermute | solution.py:16
  806.6 10.8 %collective-permute-done.1 = bf16[128,256]{1,0:T(8,128)(2,1)S(1)} collective-permute-done((bf16[128,256]{1,0:T(8,128)(2,1)S(1)}, bf16[128,256]{1,0:T(8,128)(2,1)S(1)}, u32[]{:S(2)}, u32[]{:S(2)}) %collective-permute-start.1) | collective-permute-done | bytes 65568 | tf_op jit(solution)/shard_map/while/body/eval_jaxpr/ppermute | solution.py:16
  821.5 11.1 %collective-permute-done.1 = bf16[128,256]{1,0:T(8,128)(2,1)S(1)} collective-permute-done((bf16[128,256]{1,0:T(8,128)(2,1)S(1)}, bf16[128,256]{1,0:T(8,128)(2,1)S(1)}, u32[]{:S(2)}, u32[]{:S(2)}) %collective-permute-start.1) | collective-permute-done | bytes 65568 | tf_op jit(solution)/shard_map/while/body/eval_jaxpr/ppermute | solution.py:16
  834.9 10.1 %collective-permute-done.3 = f32[128,256]{1,0:T(8,128)S(1)} collective-permute-done((f32[128,256]{1,0:T(8,128)S(1)}, f32[128,256]{1,0:T(8,128)S(1)}, u32[]{:S(2)}, u32[]{:S(2)}) %collective-permute-start.3) | collective-permute-done | bytes 131104 | tf_op jit(solution)/shard_map/ppermute | solution.py:16
  845.7 121.3 %all-to-all-start.2 = ((f32[4,32,128]{2,1,0:T(8,128)}), f32[4,32,128]{2,1,0:T(8,128)S(1)}, u32[]{:S(2)}, u32[]{:S(2)}) async-start(f32[4,32,128]{2,1,0:T(8,128)} %bitcast.69), calls=%async_computation.2 | async-start | bytes 131072 | tf_op jit(solution)/shard_map/all_to_all | solution.py:166
  (616 shorter events, 429.9 us)
Async XLA Ops:
  2.0 13.3 %all-to-all-start = ((bf16[32,4,128]{2,0,1:T(8,128)(2,1)}), bf16[32,4,128]{2,0,1:T(8,128)(2,1)S(1)}, u32[]{:S(2)}, u32[]{:S(2)}) async-start(bf16[32,4,128]{2,0,1:T(8,128)(2,1)} %copy_bitcast_fusion.4), calls=%async_computation | async-start | bytes 65536 | tf_op jit(solution)/shard_map/all_to_all | solution.py:31
  32.8 12.3 %collective-permute-start = (bf16[128,256]{1,0:T(8,128)(2,1)S(1)}, bf16[128,256]{1,0:T(8,128)(2,1)S(1)}, u32[]{:S(2)}, u32[]{:S(2)}) collective-permute-start(bf16[128,256]{1,0:T(8,128)(2,1)S(1)} %get-tuple-element.941), channel_id=1, source_target_pairs={{508,0},{0,4},{4,8},{8,12},{12,16},{16,20},{20,24},{24,28},{28,32}... | collective-permute-start | bytes 196616 | tf_op jit(solution)/shard_map/while/body/eval_jaxpr/ppermute | solution.py:16
  350.3 12.8 %collective-permute-start = (bf16[128,256]{1,0:T(8,128)(2,1)S(1)}, bf16[128,256]{1,0:T(8,128)(2,1)S(1)}, u32[]{:S(2)}, u32[]{:S(2)}) collective-permute-start(bf16[128,256]{1,0:T(8,128)(2,1)S(1)} %get-tuple-element.941), channel_id=1, source_target_pairs={{508,0},{0,4},{4,8},{8,12},{12,16},{16,20},{20,24},{24,28},{28,32}... | collective-permute-start | bytes 196616 | tf_op jit(solution)/shard_map/while/body/eval_jaxpr/ppermute | solution.py:16
  376.5 12.1 %collective-permute-start = (bf16[128,256]{1,0:T(8,128)(2,1)S(1)}, bf16[128,256]{1,0:T(8,128)(2,1)S(1)}, u32[]{:S(2)}, u32[]{:S(2)}) collective-permute-start(bf16[128,256]{1,0:T(8,128)(2,1)S(1)} %get-tuple-element.941), channel_id=1, source_target_pairs={{508,0},{0,4},{4,8},{8,12},{12,16},{16,20},{20,24},{24,28},{28,32}... | collective-permute-start | bytes 196616 | tf_op jit(solution)/shard_map/while/body/eval_jaxpr/ppermute | solution.py:16
  389.6 12.4 %collective-permute-start = (bf16[128,256]{1,0:T(8,128)(2,1)S(1)}, bf16[128,256]{1,0:T(8,128)(2,1)S(1)}, u32[]{:S(2)}, u32[]{:S(2)}) collective-permute-start(bf16[128,256]{1,0:T(8,128)(2,1)S(1)} %get-tuple-element.941), channel_id=1, source_target_pairs={{508,0},{0,4},{4,8},{8,12},{12,16},{16,20},{20,24},{24,28},{28,32}... | collective-permute-start | bytes 196616 | tf_op jit(solution)/shard_map/while/body/eval_jaxpr/ppermute | solution.py:16
  405.8 13.6 %collective-permute-start.2 = (f32[128,256]{0,1:T(8,128)S(1)}, f32[128,256]{0,1:T(8,128)S(1)}, u32[]{:S(2)}, u32[]{:S(2)}) collective-permute-start(f32[128,256]{0,1:T(8,128)S(1)} %get-tuple-element.979), channel_id=1, source_target_pairs={{508,0},{0,4},{4,8},{8,12},{12,16},{16,20},{20,24},{24,28},{28,32}... | collective-permute-start | bytes 393224 | tf_op jit(solution)/shard_map/while/body/eval_jaxpr/ppermute | solution.py:16
  419.4 12.9 %collective-permute-start.2 = (f32[128,256]{0,1:T(8,128)S(1)}, f32[128,256]{0,1:T(8,128)S(1)}, u32[]{:S(2)}, u32[]{:S(2)}) collective-permute-start(f32[128,256]{0,1:T(8,128)S(1)} %get-tuple-element.979), channel_id=1, source_target_pairs={{508,0},{0,4},{4,8},{8,12},{12,16},{16,20},{20,24},{24,28},{28,32}... | collective-permute-start | bytes 393224 | tf_op jit(solution)/shard_map/while/body/eval_jaxpr/ppermute | solution.py:16
  432.4 12.9 %collective-permute-start.2 = (f32[128,256]{0,1:T(8,128)S(1)}, f32[128,256]{0,1:T(8,128)S(1)}, u32[]{:S(2)}, u32[]{:S(2)}) collective-permute-start(f32[128,256]{0,1:T(8,128)S(1)} %get-tuple-element.979), channel_id=1, source_target_pairs={{508,0},{0,4},{4,8},{8,12},{12,16},{16,20},{20,24},{24,28},{28,32}... | collective-permute-start | bytes 393224 | tf_op jit(solution)/shard_map/while/body/eval_jaxpr/ppermute | solution.py:16
  445.3 12.9 %collective-permute-start.2 = (f32[128,256]{0,1:T(8,128)S(1)}, f32[128,256]{0,1:T(8,128)S(1)}, u32[]{:S(2)}, u32[]{:S(2)}) collective-permute-start(f32[128,256]{0,1:T(8,128)S(1)} %get-tuple-element.979), channel_id=1, source_target_pairs={{508,0},{0,4},{4,8},{8,12},{12,16},{16,20},{20,24},{24,28},{28,32}... | collective-permute-start | bytes 393224 | tf_op jit(solution)/shard_map/while/body/eval_jaxpr/ppermute | solution.py:16
  458.3 12.9 %collective-permute-start.2 = (f32[128,256]{0,1:T(8,128)S(1)}, f32[128,256]{0,1:T(8,128)S(1)}, u32[]{:S(2)}, u32[]{:S(2)}) collective-permute-start(f32[128,256]{0,1:T(8,128)S(1)} %get-tuple-element.979), channel_id=1, source_target_pairs={{508,0},{0,4},{4,8},{8,12},{12,16},{16,20},{20,24},{24,28},{28,32}... | collective-permute-start | bytes 393224 | tf_op jit(solution)/shard_map/while/body/eval_jaxpr/ppermute | solution.py:16
  471.2 12.9 %collective-permute-start.2 = (f32[128,256]{0,1:T(8,128)S(1)}, f32[128,256]{0,1:T(8,128)S(1)}, u32[]{:S(2)}, u32[]{:S(2)}) collective-permute-start(f32[128,256]{0,1:T(8,128)S(1)} %get-tuple-element.979), channel_id=1, source_target_pairs={{508,0},{0,4},{4,8},{8,12},{12,16},{16,20},{20,24},{24,28},{28,32}... | collective-permute-start | bytes 393224 | tf_op jit(solution)/shard_map/while/body/eval_jaxpr/ppermute | solution.py:16
  484.2 14.1 %collective-permute-start.2 = (f32[128,256]{0,1:T(8,128)S(1)}, f32[128,256]{0,1:T(8,128)S(1)}, u32[]{:S(2)}, u32[]{:S(2)}) collective-permute-start(f32[128,256]{0,1:T(8,128)S(1)} %get-tuple-element.979), channel_id=1, source_target_pairs={{508,0},{0,4},{4,8},{8,12},{12,16},{16,20},{20,24},{24,28},{28,32}... | collective-permute-start | bytes 393224 | tf_op jit(solution)/shard_map/while/body/eval_jaxpr/ppermute | solution.py:16
  486.1 11.9 %collective-permute-start.1 = (bf16[128,256]{1,0:T(8,128)(2,1)S(1)}, bf16[128,256]{1,0:T(8,128)(2,1)S(1)}, u32[]{:S(2)}, u32[]{:S(2)}) collective-permute-start(bf16[128,256]{1,0:T(8,128)(2,1)S(1)} %get-tuple-element.978), channel_id=1, source_target_pairs={{508,0},{0,4},{4,8},{8,12},{12,16},{16,20},{20,24},{24,28},{28,32}... | collective-permute-start | bytes 196616 | tf_op jit(solution)/shard_map/while/body/eval_jaxpr/ppermute | solution.py:16
  498.3 14.0 %collective-permute-start.2 = (f32[128,256]{0,1:T(8,128)S(1)}, f32[128,256]{0,1:T(8,128)S(1)}, u32[]{:S(2)}, u32[]{:S(2)}) collective-permute-start(f32[128,256]{0,1:T(8,128)S(1)} %get-tuple-element.979), channel_id=1, source_target_pairs={{508,0},{0,4},{4,8},{8,12},{12,16},{16,20},{20,24},{24,28},{28,32}... | collective-permute-start | bytes 393224 | tf_op jit(solution)/shard_map/while/body/eval_jaxpr/ppermute | solution.py:16
  500.3 11.8 %collective-permute-start.1 = (bf16[128,256]{1,0:T(8,128)(2,1)S(1)}, bf16[128,256]{1,0:T(8,128)(2,1)S(1)}, u32[]{:S(2)}, u32[]{:S(2)}) collective-permute-start(bf16[128,256]{1,0:T(8,128)(2,1)S(1)} %get-tuple-element.978), channel_id=1, source_target_pairs={{508,0},{0,4},{4,8},{8,12},{12,16},{16,20},{20,24},{24,28},{28,32}... | collective-permute-start | bytes 196616 | tf_op jit(solution)/shard_map/while/body/eval_jaxpr/ppermute | solution.py:16
  512.4 13.9 %collective-permute-start.2 = (f32[128,256]{0,1:T(8,128)S(1)}, f32[128,256]{0,1:T(8,128)S(1)}, u32[]{:S(2)}, u32[]{:S(2)}) collective-permute-start(f32[128,256]{0,1:T(8,128)S(1)} %get-tuple-element.979), channel_id=1, source_target_pairs={{508,0},{0,4},{4,8},{8,12},{12,16},{16,20},{20,24},{24,28},{28,32}... | collective-permute-start | bytes 393224 | tf_op jit(solution)/shard_map/while/body/eval_jaxpr/ppermute | solution.py:16
  526.3 13.9 %collective-permute-start.2 = (f32[128,256]{0,1:T(8,128)S(1)}, f32[128,256]{0,1:T(8,128)S(1)}, u32[]{:S(2)}, u32[]{:S(2)}) collective-permute-start(f32[128,256]{0,1:T(8,128)S(1)} %get-tuple-element.979), channel_id=1, source_target_pairs={{508,0},{0,4},{4,8},{8,12},{12,16},{16,20},{20,24},{24,28},{28,32}... | collective-permute-start | bytes 393224 | tf_op jit(solution)/shard_map/while/body/eval_jaxpr/ppermute | solution.py:16
  540.2 13.6 %collective-permute-start.2 = (f32[128,256]{0,1:T(8,128)S(1)}, f32[128,256]{0,1:T(8,128)S(1)}, u32[]{:S(2)}, u32[]{:S(2)}) collective-permute-start(f32[128,256]{0,1:T(8,128)S(1)} %get-tuple-element.979), channel_id=1, source_target_pairs={{508,0},{0,4},{4,8},{8,12},{12,16},{16,20},{20,24},{24,28},{28,32}... | collective-permute-start | bytes 393224 | tf_op jit(solution)/shard_map/while/body/eval_jaxpr/ppermute | solution.py:16
  553.9 12.9 %collective-permute-start.2 = (f32[128,256]{0,1:T(8,128)S(1)}, f32[128,256]{0,1:T(8,128)S(1)}, u32[]{:S(2)}, u32[]{:S(2)}) collective-permute-start(f32[128,256]{0,1:T(8,128)S(1)} %get-tuple-element.979), channel_id=1, source_target_pairs={{508,0},{0,4},{4,8},{8,12},{12,16},{16,20},{20,24},{24,28},{28,32}... | collective-permute-start | bytes 393224 | tf_op jit(solution)/shard_map/while/body/eval_jaxpr/ppermute | solution.py:16
  566.8 12.9 %collective-permute-start.2 = (f32[128,256]{0,1:T(8,128)S(1)}, f32[128,256]{0,1:T(8,128)S(1)}, u32[]{:S(2)}, u32[]{:S(2)}) collective-permute-start(f32[128,256]{0,1:T(8,128)S(1)} %get-tuple-element.979), channel_id=1, source_target_pairs={{508,0},{0,4},{4,8},{8,12},{12,16},{16,20},{20,24},{24,28},{28,32}... | collective-permute-start | bytes 393224 | tf_op jit(solution)/shard_map/while/body/eval_jaxpr/ppermute | solution.py:16
  579.8 12.9 %collective-permute-start.2 = (f32[128,256]{0,1:T(8,128)S(1)}, f32[128,256]{0,1:T(8,128)S(1)}, u32[]{:S(2)}, u32[]{:S(2)}) collective-permute-start(f32[128,256]{0,1:T(8,128)S(1)} %get-tuple-element.979), channel_id=1, source_target_pairs={{508,0},{0,4},{4,8},{8,12},{12,16},{16,20},{20,24},{24,28},{28,32}... | collective-permute-start | bytes 393224 | tf_op jit(solution)/shard_map/while/body/eval_jaxpr/ppermute | solution.py:16
  592.8 12.9 %collective-permute-start.2 = (f32[128,256]{0,1:T(8,128)S(1)}, f32[128,256]{0,1:T(8,128)S(1)}, u32[]{:S(2)}, u32[]{:S(2)}) collective-permute-start(f32[128,256]{0,1:T(8,128)S(1)} %get-tuple-element.979), channel_id=1, source_target_pairs={{508,0},{0,4},{4,8},{8,12},{12,16},{16,20},{20,24},{24,28},{28,32}... | collective-permute-start | bytes 393224 | tf_op jit(solution)/shard_map/while/body/eval_jaxpr/ppermute | solution.py:16
  605.7 12.9 %collective-permute-start.2 = (f32[128,256]{0,1:T(8,128)S(1)}, f32[128,256]{0,1:T(8,128)S(1)}, u32[]{:S(2)}, u32[]{:S(2)}) collective-permute-start(f32[128,256]{0,1:T(8,128)S(1)} %get-tuple-element.979), channel_id=1, source_target_pairs={{508,0},{0,4},{4,8},{8,12},{12,16},{16,20},{20,24},{24,28},{28,32}... | collective-permute-start | bytes 393224 | tf_op jit(solution)/shard_map/while/body/eval_jaxpr/ppermute | solution.py:16
  618.7 13.7 %collective-permute-start.2 = (f32[128,256]{0,1:T(8,128)S(1)}, f32[128,256]{0,1:T(8,128)S(1)}, u32[]{:S(2)}, u32[]{:S(2)}) collective-permute-start(f32[128,256]{0,1:T(8,128)S(1)} %get-tuple-element.979), channel_id=1, source_target_pairs={{508,0},{0,4},{4,8},{8,12},{12,16},{16,20},{20,24},{24,28},{28,32}... | collective-permute-start | bytes 393224 | tf_op jit(solution)/shard_map/while/body/eval_jaxpr/ppermute | solution.py:16
  632.4 15.7 %collective-permute-start.2 = (f32[128,256]{0,1:T(8,128)S(1)}, f32[128,256]{0,1:T(8,128)S(1)}, u32[]{:S(2)}, u32[]{:S(2)}) collective-permute-start(f32[128,256]{0,1:T(8,128)S(1)} %get-tuple-element.979), channel_id=1, source_target_pairs={{508,0},{0,4},{4,8},{8,12},{12,16},{16,20},{20,24},{24,28},{28,32}... | collective-permute-start | bytes 393224 | tf_op jit(solution)/shard_map/while/body/eval_jaxpr/ppermute | solution.py:16
  634.3 13.5 %collective-permute-start.1 = (bf16[128,256]{1,0:T(8,128)(2,1)S(1)}, bf16[128,256]{1,0:T(8,128)(2,1)S(1)}, u32[]{:S(2)}, u32[]{:S(2)}) collective-permute-start(bf16[128,256]{1,0:T(8,128)(2,1)S(1)} %get-tuple-element.978), channel_id=1, source_target_pairs={{508,0},{0,4},{4,8},{8,12},{12,16},{16,20},{20,24},{24,28},{28,32}... | collective-permute-start | bytes 196616 | tf_op jit(solution)/shard_map/while/body/eval_jaxpr/ppermute | solution.py:16
  648.1 12.9 %collective-permute-start.2 = (f32[128,256]{0,1:T(8,128)S(1)}, f32[128,256]{0,1:T(8,128)S(1)}, u32[]{:S(2)}, u32[]{:S(2)}) collective-permute-start(f32[128,256]{0,1:T(8,128)S(1)} %get-tuple-element.979), channel_id=1, source_target_pairs={{508,0},{0,4},{4,8},{8,12},{12,16},{16,20},{20,24},{24,28},{28,32}... | collective-permute-start | bytes 393224 | tf_op jit(solution)/shard_map/while/body/eval_jaxpr/ppermute | solution.py:16
  661.1 12.9 %collective-permute-start.2 = (f32[128,256]{0,1:T(8,128)S(1)}, f32[128,256]{0,1:T(8,128)S(1)}, u32[]{:S(2)}, u32[]{:S(2)}) collective-permute-start(f32[128,256]{0,1:T(8,128)S(1)} %get-tuple-element.979), channel_id=1, source_target_pairs={{508,0},{0,4},{4,8},{8,12},{12,16},{16,20},{20,24},{24,28},{28,32}... | collective-permute-start | bytes 393224 | tf_op jit(solution)/shard_map/while/body/eval_jaxpr/ppermute | solution.py:16
  674.0 12.9 %collective-permute-start.2 = (f32[128,256]{0,1:T(8,128)S(1)}, f32[128,256]{0,1:T(8,128)S(1)}, u32[]{:S(2)}, u32[]{:S(2)}) collective-permute-start(f32[128,256]{0,1:T(8,128)S(1)} %get-tuple-element.979), channel_id=1, source_target_pairs={{508,0},{0,4},{4,8},{8,12},{12,16},{16,20},{20,24},{24,28},{28,32}... | collective-permute-start | bytes 393224 | tf_op jit(solution)/shard_map/while/body/eval_jaxpr/ppermute | solution.py:16
  687.0 12.9 %collective-permute-start.2 = (f32[128,256]{0,1:T(8,128)S(1)}, f32[128,256]{0,1:T(8,128)S(1)}, u32[]{:S(2)}, u32[]{:S(2)}) collective-permute-start(f32[128,256]{0,1:T(8,128)S(1)} %get-tuple-element.979), channel_id=1, source_target_pairs={{508,0},{0,4},{4,8},{8,12},{12,16},{16,20},{20,24},{24,28},{28,32}... | collective-permute-start | bytes 393224 | tf_op jit(solution)/shard_map/while/body/eval_jaxpr/ppermute | solution.py:16
  700.0 13.1 %collective-permute-start.2 = (f32[128,256]{0,1:T(8,128)S(1)}, f32[128,256]{0,1:T(8,128)S(1)}, u32[]{:S(2)}, u32[]{:S(2)}) collective-permute-start(f32[128,256]{0,1:T(8,128)S(1)} %get-tuple-element.979), channel_id=1, source_target_pairs={{508,0},{0,4},{4,8},{8,12},{12,16},{16,20},{20,24},{24,28},{28,32}... | collective-permute-start | bytes 393224 | tf_op jit(solution)/shard_map/while/body/eval_jaxpr/ppermute | solution.py:16
  713.1 14.6 %collective-permute-start.2 = (f32[128,256]{0,1:T(8,128)S(1)}, f32[128,256]{0,1:T(8,128)S(1)}, u32[]{:S(2)}, u32[]{:S(2)}) collective-permute-start(f32[128,256]{0,1:T(8,128)S(1)} %get-tuple-element.979), channel_id=1, source_target_pairs={{508,0},{0,4},{4,8},{8,12},{12,16},{16,20},{20,24},{24,28},{28,32}... | collective-permute-start | bytes 393224 | tf_op jit(solution)/shard_map/while/body/eval_jaxpr/ppermute | solution.py:16
  715.0 12.4 %collective-permute-start.1 = (bf16[128,256]{1,0:T(8,128)(2,1)S(1)}, bf16[128,256]{1,0:T(8,128)(2,1)S(1)}, u32[]{:S(2)}, u32[]{:S(2)}) collective-permute-start(bf16[128,256]{1,0:T(8,128)(2,1)S(1)} %get-tuple-element.978), channel_id=1, source_target_pairs={{508,0},{0,4},{4,8},{8,12},{12,16},{16,20},{20,24},{24,28},{28,32}... | collective-permute-start | bytes 196616 | tf_op jit(solution)/shard_map/while/body/eval_jaxpr/ppermute | solution.py:16
  727.8 13.9 %collective-permute-start.2 = (f32[128,256]{0,1:T(8,128)S(1)}, f32[128,256]{0,1:T(8,128)S(1)}, u32[]{:S(2)}, u32[]{:S(2)}) collective-permute-start(f32[128,256]{0,1:T(8,128)S(1)} %get-tuple-element.979), channel_id=1, source_target_pairs={{508,0},{0,4},{4,8},{8,12},{12,16},{16,20},{20,24},{24,28},{28,32}... | collective-permute-start | bytes 393224 | tf_op jit(solution)/shard_map/while/body/eval_jaxpr/ppermute | solution.py:16
  741.7 15.6 %collective-permute-start.2 = (f32[128,256]{0,1:T(8,128)S(1)}, f32[128,256]{0,1:T(8,128)S(1)}, u32[]{:S(2)}, u32[]{:S(2)}) collective-permute-start(f32[128,256]{0,1:T(8,128)S(1)} %get-tuple-element.979), channel_id=1, source_target_pairs={{508,0},{0,4},{4,8},{8,12},{12,16},{16,20},{20,24},{24,28},{28,32}... | collective-permute-start | bytes 393224 | tf_op jit(solution)/shard_map/while/body/eval_jaxpr/ppermute | solution.py:16
  743.6 13.4 %collective-permute-start.1 = (bf16[128,256]{1,0:T(8,128)(2,1)S(1)}, bf16[128,256]{1,0:T(8,128)(2,1)S(1)}, u32[]{:S(2)}, u32[]{:S(2)}) collective-permute-start(bf16[128,256]{1,0:T(8,128)(2,1)S(1)} %get-tuple-element.978), channel_id=1, source_target_pairs={{508,0},{0,4},{4,8},{8,12},{12,16},{16,20},{20,24},{24,28},{28,32}... | collective-permute-start | bytes 196616 | tf_op jit(solution)/shard_map/while/body/eval_jaxpr/ppermute | solution.py:16
  757.4 14.8 %collective-permute-start.2 = (f32[128,256]{0,1:T(8,128)S(1)}, f32[128,256]{0,1:T(8,128)S(1)}, u32[]{:S(2)}, u32[]{:S(2)}) collective-permute-start(f32[128,256]{0,1:T(8,128)S(1)} %get-tuple-element.979), channel_id=1, source_target_pairs={{508,0},{0,4},{4,8},{8,12},{12,16},{16,20},{20,24},{24,28},{28,32}... | collective-permute-start | bytes 393224 | tf_op jit(solution)/shard_map/while/body/eval_jaxpr/ppermute | solution.py:16
  759.3 12.7 %collective-permute-start.1 = (bf16[128,256]{1,0:T(8,128)(2,1)S(1)}, bf16[128,256]{1,0:T(8,128)(2,1)S(1)}, u32[]{:S(2)}, u32[]{:S(2)}) collective-permute-start(bf16[128,256]{1,0:T(8,128)(2,1)S(1)} %get-tuple-element.978), channel_id=1, source_target_pairs={{508,0},{0,4},{4,8},{8,12},{12,16},{16,20},{20,24},{24,28},{28,32}... | collective-permute-start | bytes 196616 | tf_op jit(solution)/shard_map/while/body/eval_jaxpr/ppermute | solution.py:16
  772.2 15.6 %collective-permute-start.2 = (f32[128,256]{0,1:T(8,128)S(1)}, f32[128,256]{0,1:T(8,128)S(1)}, u32[]{:S(2)}, u32[]{:S(2)}) collective-permute-start(f32[128,256]{0,1:T(8,128)S(1)} %get-tuple-element.979), channel_id=1, source_target_pairs={{508,0},{0,4},{4,8},{8,12},{12,16},{16,20},{20,24},{24,28},{28,32}... | collective-permute-start | bytes 393224 | tf_op jit(solution)/shard_map/while/body/eval_jaxpr/ppermute | solution.py:16
  774.2 13.4 %collective-permute-start.1 = (bf16[128,256]{1,0:T(8,128)(2,1)S(1)}, bf16[128,256]{1,0:T(8,128)(2,1)S(1)}, u32[]{:S(2)}, u32[]{:S(2)}) collective-permute-start(bf16[128,256]{1,0:T(8,128)(2,1)S(1)} %get-tuple-element.978), channel_id=1, source_target_pairs={{508,0},{0,4},{4,8},{8,12},{12,16},{16,20},{20,24},{24,28},{28,32}... | collective-permute-start | bytes 196616 | tf_op jit(solution)/shard_map/while/body/eval_jaxpr/ppermute | solution.py:16
  787.8 14.8 %collective-permute-start.2 = (f32[128,256]{0,1:T(8,128)S(1)}, f32[128,256]{0,1:T(8,128)S(1)}, u32[]{:S(2)}, u32[]{:S(2)}) collective-permute-start(f32[128,256]{0,1:T(8,128)S(1)} %get-tuple-element.979), channel_id=1, source_target_pairs={{508,0},{0,4},{4,8},{8,12},{12,16},{16,20},{20,24},{24,28},{28,32}... | collective-permute-start | bytes 393224 | tf_op jit(solution)/shard_map/while/body/eval_jaxpr/ppermute | solution.py:16
  789.8 12.6 %collective-permute-start.1 = (bf16[128,256]{1,0:T(8,128)(2,1)S(1)}, bf16[128,256]{1,0:T(8,128)(2,1)S(1)}, u32[]{:S(2)}, u32[]{:S(2)}) collective-permute-start(bf16[128,256]{1,0:T(8,128)(2,1)S(1)} %get-tuple-element.978), channel_id=1, source_target_pairs={{508,0},{0,4},{4,8},{8,12},{12,16},{16,20},{20,24},{24,28},{28,32}... | collective-permute-start | bytes 196616 | tf_op jit(solution)/shard_map/while/body/eval_jaxpr/ppermute | solution.py:16
  802.7 14.9 %collective-permute-start.2 = (f32[128,256]{0,1:T(8,128)S(1)}, f32[128,256]{0,1:T(8,128)S(1)}, u32[]{:S(2)}, u32[]{:S(2)}) collective-permute-start(f32[128,256]{0,1:T(8,128)S(1)} %get-tuple-element.979), channel_id=1, source_target_pairs={{508,0},{0,4},{4,8},{8,12},{12,16},{16,20},{20,24},{24,28},{28,32}... | collective-permute-start | bytes 393224 | tf_op jit(solution)/shard_map/while/body/eval_jaxpr/ppermute | solution.py:16
  804.6 12.7 %collective-permute-start.1 = (bf16[128,256]{1,0:T(8,128)(2,1)S(1)}, bf16[128,256]{1,0:T(8,128)(2,1)S(1)}, u32[]{:S(2)}, u32[]{:S(2)}) collective-permute-start(bf16[128,256]{1,0:T(8,128)(2,1)S(1)} %get-tuple-element.978), channel_id=1, source_target_pairs={{508,0},{0,4},{4,8},{8,12},{12,16},{16,20},{20,24},{24,28},{28,32}... | collective-permute-start | bytes 196616 | tf_op jit(solution)/shard_map/while/body/eval_jaxpr/ppermute | solution.py:16
  817.7 15.2 %collective-permute-start.2 = (f32[128,256]{0,1:T(8,128)S(1)}, f32[128,256]{0,1:T(8,128)S(1)}, u32[]{:S(2)}, u32[]{:S(2)}) collective-permute-start(f32[128,256]{0,1:T(8,128)S(1)} %get-tuple-element.979), channel_id=1, source_target_pairs={{508,0},{0,4},{4,8},{8,12},{12,16},{16,20},{20,24},{24,28},{28,32}... | collective-permute-start | bytes 393224 | tf_op jit(solution)/shard_map/while/body/eval_jaxpr/ppermute | solution.py:16
  819.6 13.0 %collective-permute-start.1 = (bf16[128,256]{1,0:T(8,128)(2,1)S(1)}, bf16[128,256]{1,0:T(8,128)(2,1)S(1)}, u32[]{:S(2)}, u32[]{:S(2)}) collective-permute-start(bf16[128,256]{1,0:T(8,128)(2,1)S(1)} %get-tuple-element.978), channel_id=1, source_target_pairs={{508,0},{0,4},{4,8},{8,12},{12,16},{16,20},{20,24},{24,28},{28,32}... | collective-permute-start | bytes 196616 | tf_op jit(solution)/shard_map/while/body/eval_jaxpr/ppermute | solution.py:16
  833.0 12.0 %collective-permute-start.3 = (f32[128,256]{1,0:T(8,128)S(1)}, f32[128,256]{1,0:T(8,128)S(1)}, u32[]{:S(2)}, u32[]{:S(2)}) collective-permute-start(f32[128,256]{1,0:T(8,128)S(1)} %copy.61), channel_id=1, source_target_pairs={{124,0},{128,4},{132,8},{136,12},{140,16},{144,20},{148,24},{152,2... | collective-permute-start | bytes 393224 | tf_op jit(solution)/shard_map/ppermute | solution.py:16
  845.7 124.6 %all-to-all-start.2 = ((f32[4,32,128]{2,1,0:T(8,128)}), f32[4,32,128]{2,1,0:T(8,128)S(1)}, u32[]{:S(2)}, u32[]{:S(2)}) async-start(f32[4,32,128]{2,1,0:T(8,128)} %bitcast.69), calls=%async_computation.2 | async-start | bytes 131072 | tf_op jit(solution)/shard_map/all_to_all | solution.py:166
  (52 other events, 542.7 us)
where the time goes:
time: 985 us; the launch traced here: 978 us
  waiting for transfers between devices  596 us (61%)
  starting transfers between devices  320 us (32%)
  local copies, waits for them, and re-layouts  46.7 us (5%)
    ppermute x94, waiting for transfers between devices, shifted(): return lax.ppermute(block, axis, route)  589 us
    ppermute x94, starting transfers between devices, shifted(): return lax.ppermute(block, axis, route)  180 us
    all_to_all x1, starting transfers between devices, shards(): lax.all_to_all(key_grad, 'tp', split_axis=0, concat_axis=1, tiled=True)  121 us
    dynamic_update_slice x31, local copies, waits for them, and re-layouts, cycle_forward(): stored = lax.dynamic_update_index_in_dim(stored, slopes, distance, 0)  26.4 us
  transfers between devices with their start and end apart: 98, of which 67 were waited for; matrix products, arithmetic and copies ran while one was open for 1% of the time, Pallas kernels for 0%

commit v1 on v0

v1 whole, which is shorter than its diff:
```python
import functools
import math

import jax
import jax.numpy as jnp
from jax import lax
from jax.experimental import pallas as pl
from jax.experimental.pallas import tpu as pltpu
from jax.sharding import PartitionSpec as P

HEAD_SIZE = 128
GROUPS = 4
SLABS = 4
KEYS = 512
ROWS = 512
AXES = ("ctx", "tp")
BF16, F32 = jnp.bfloat16, jnp.float32


def product(a, b):
    return jnp.dot(a, b, preferred_element_type=F32)


def attention_kernel(
    rank_ref, q_ref, do_ref, kv_ref, dq_ref, dkv_ref,
    q_rows, do_rows, q_cols, do_cols, k_cols, weights, slopes, maxima, total,
):
    tokens = q_ref.shape[0]
    heads = q_ref.shape[1] // HEAD_SIZE
    blocks, slabs = kv_ref.shape[0], kv_ref.shape[1]
    per_step = KEYS // tokens
    steps_per_slab = blocks // per_step
    rank = rank_ref[0]
    steps = lax.div(rank, jnp.int32(per_step)) + 1
    scale = 1.0 / math.sqrt(HEAD_SIZE)

    for h in range(heads):
        across = slice(h * HEAD_SIZE, (h + 1) * HEAD_SIZE)
        down = slice(h * tokens, (h + 1) * tokens)
        q_rows[down, :] = q_ref[:, across]
        do_rows[down, :] = do_ref[:, across]
        q_cols[:, down] = q_ref[:, across].T
        do_cols[:, down] = do_ref[:, across].T

    def block(step, column):
        slab = lax.div(step, jnp.int32(steps_per_slab))
        first = lax.rem(step, jnp.int32(steps_per_slab)) * per_step
        part = kv_ref[pl.ds(first, per_step), slab, :, column * HEAD_SIZE : (column + 1) * HEAD_SIZE]
        return part.reshape(KEYS, HEAD_SIZE)

    @pl.loop(0, steps)
    def _(step):
        k_cols[:, pl.ds(pl.multiple_of(step * KEYS, KEYS), KEYS)] = block(step, 0).T

    for tile in range(heads * tokens // ROWS):
        rows = slice(tile * ROWS, (tile + 1) * ROWS)

        def statistics(step, carry, masked):
            highest, norm, weighted = carry
            first = pl.multiple_of(step * KEYS, KEYS)
            scores = product(block(step, 0), q_cols[:, rows]) * (scale * math.log2(math.e))
            if masked:
                key = lax.broadcasted_iota(jnp.int32, (KEYS, ROWS), 0) + (first - rank * tokens)
                query = lax.rem(lax.broadcasted_iota(jnp.int32, (KEYS, ROWS), 1), tokens)
                scores = jnp.where(key <= query, scores, -jnp.inf)
            higher = jnp.maximum(highest, jnp.max(scores, axis=0, keepdims=True))
            weight = jnp.exp2(scores - higher)
            factor = jnp.exp2(highest - higher)
            slope = product(block(step, 1), do_cols[:, rows])
            weights[pl.ds(first, KEYS), :] = weight
            slopes[pl.ds(first, KEYS), :] = slope
            maxima[pl.ds(step * 8, 8), :] = jnp.broadcast_to(higher, (8, ROWS))
            norm = norm * factor + jnp.sum(weight, axis=0, keepdims=True)
            weighted = weighted * factor + jnp.sum(weight * slope, axis=0, keepdims=True)
            return higher, norm, weighted

        zeros = jnp.zeros((1, ROWS), F32)
        carry = lax.fori_loop(
            0, steps - 1, functools.partial(statistics, masked=False),
            (jnp.full((1, ROWS), -jnp.inf, F32), zeros, zeros),
        )
        highest, norm, weighted = statistics(steps - 1, carry, True)
        inverse = 1.0 / norm
        centre = weighted * inverse

        def gradients(step, dq_cols):
            keys = pl.ds(pl.multiple_of(step * KEYS, KEYS), KEYS)
            factor = jnp.exp2(maxima[pl.ds(step * 8, 8), :][0:1] - highest) * inverse
            soft = weights[keys, :] * factor
            score_grad = (soft * (slopes[keys, :] - centre)).astype(BF16)
            dk = product(score_grad, q_rows[rows, :])
            dv = product(soft.astype(BF16), do_rows[rows, :])
            if tile == 0:
                total[keys, 0:HEAD_SIZE] = dk
                total[keys, HEAD_SIZE:] = dv
            else:
                total[keys, 0:HEAD_SIZE] += dk
                total[keys, HEAD_SIZE:] += dv
            return dq_cols + product(k_cols[:, keys], score_grad)

        dq_cols = lax.fori_loop(0, steps, gradients, jnp.zeros((HEAD_SIZE, ROWS), F32)) * scale
        for i in range(ROWS // tokens):
            h = tile * (ROWS // tokens) + i
            dq_ref[:, h * HEAD_SIZE : (h + 1) * HEAD_SIZE] = dq_cols[:, i * tokens : (i + 1) * tokens].T

    @pl.loop(0, slabs * steps_per_slab)
    def _(step):
        slab = lax.div(step, jnp.int32(steps_per_slab))
        first = lax.rem(step, jnp.int32(steps_per_slab)) * per_step
        keys = pl.ds(pl.multiple_of(step * KEYS, KEYS), KEYS)
        there = pl.ds(first, per_step)

        @pl.when(step < steps)
        def _():
            dk = (total[keys, 0:HEAD_SIZE] * scale).astype(BF16)
            dv = total[keys, HEAD_SIZE:].astype(BF16)
            dkv_ref[there, slab, :, 0:HEAD_SIZE] = dk.reshape(per_step, tokens, HEAD_SIZE)
            dkv_ref[there, slab, :, HEAD_SIZE:] = dv.reshape(per_step, tokens, HEAD_SIZE)

        @pl.when(step >= steps)
        def _():
            dkv_ref[there, slab] = jnp.zeros((per_step, tokens, 2 * HEAD_SIZE), BF16)


def attention_gradients(rank, q, do, kv):
    tokens, width = q.shape
    rows = tokens * (width // HEAD_SIZE)
    keys = kv.shape[0] * kv.shape[1] * kv.shape[2]
    whole = pl.BlockSpec(memory_space=pltpu.VMEM)
    return pl.pallas_call(
        attention_kernel,
        out_shape=(jax.ShapeDtypeStruct(q.shape, F32), jax.ShapeDtypeStruct(kv.shape, BF16)),
        in_specs=[pl.BlockSpec(memory_space=pltpu.SMEM), whole, whole, whole],
        out_specs=(whole, whole),
        scratch_shapes=[
            pltpu.VMEM((rows, HEAD_SIZE), BF16),
            pltpu.VMEM((rows, HEAD_SIZE), BF16),
            pltpu.VMEM((HEAD_SIZE, rows), BF16),
            pltpu.VMEM((HEAD_SIZE, rows), BF16),
            pltpu.VMEM((HEAD_SIZE, keys), BF16),
            pltpu.VMEM((keys, ROWS), F32),
            pltpu.VMEM((keys, ROWS), F32),
            pltpu.VMEM((8 * keys // KEYS, ROWS), F32),
            pltpu.VMEM((keys, 2 * HEAD_SIZE), F32),
        ],
        compiler_params=pltpu.CompilerParams(vmem_limit_bytes=48 * 2**20),
        cost_estimate=pl.CostEstimate(
            flops=10 * rows * keys * HEAD_SIZE, bytes_accessed=6 * 2**20, transcendentals=rows * keys
        ),
        name="attention_gradients",
    )(rank, q, do, kv)


def slab_lists(ctx_count, tp_count):
    span = ctx_count // GROUPS
    plane = span // SLABS
    lists = []
    for t in range(tp_count):
        first = span // 2 if t >= tp_count // 2 else 0
        for g in range(GROUPS):
            for p in range(plane):
                column = [(first + g * span + s * plane + p) % ctx_count for s in range(SLABS)]
                lists.append([c * tp_count + t for c in column])
    return lists


def plane_lists(ctx_count, tp_count):
    plane = ctx_count // GROUPS // SLABS
    return [
        [(s * plane + p) * tp_count + t for p in range(plane)]
        for t in range(tp_count)
        for s in range(ctx_count // plane)
    ]


def exchange(parts, lists):
    return lax.all_to_all(parts, AXES, 0, 0, axis_index_groups=lists, tiled=True)


def shards(query_heads, key_heads_wide, value_heads_wide, grad_output):
    ctx_count = lax.axis_size("ctx")
    tp_count = lax.axis_size("tp")
    span = ctx_count // GROUPS
    plane = span // SLABS
    here = key_heads_wide.shape[0]
    rows = query_heads.shape[0]
    columns = slab_lists(ctx_count, tp_count)
    planes = plane_lists(ctx_count, tp_count)
    offset = jnp.where(lax.axis_index("tp") >= tp_count // 2, span // 2, 0)
    rank = jnp.mod(lax.axis_index("ctx") - offset, ctx_count) % span

    both = jnp.stack(
        [a.reshape(here, tp_count, HEAD_SIZE) for a in (key_heads_wide, value_heads_wide)], axis=2
    ).transpose(1, 0, 2, 3).reshape(tp_count, here, 2 * HEAD_SIZE)
    own = lax.all_to_all(both, "tp", 0, 0, tiled=True).reshape(rows, 2 * HEAD_SIZE)
    column = exchange(jnp.broadcast_to(own, (SLABS,) + own.shape), columns)
    kv = exchange(jnp.broadcast_to(column, (plane,) + column.shape), planes)
    grad_query, dkv = attention_gradients(rank.astype(jnp.int32).reshape(1), query_heads, grad_output, kv)
    partial = jnp.sum(exchange(dkv, planes).astype(F32), axis=0).astype(BF16)
    mine = jnp.sum(exchange(partial, columns).astype(F32), axis=0)
    back = lax.all_to_all(mine.reshape(tp_count, here, 2 * HEAD_SIZE), "tp", 0, 0, tiled=True)
    back = back.reshape(tp_count, here, 2, HEAD_SIZE).transpose(2, 1, 0, 3)
    back = back.reshape(2, here, tp_count * HEAD_SIZE)
    return grad_query, back[0], back[1]


def solution(mesh):
    return jax.shard_map(
        shards,
        mesh=mesh,
        in_specs=(P("ctx", "tp"), P(AXES, None), P(AXES, None), P("ctx", "tp")),
        out_specs=(P("ctx", "tp"), P(AXES, None), P(AXES, None)),
        check_vma=False,
    )
```

time: 985 us -> 134 us (0.14)
  waiting for transfers between devices: 596 us -> 24.3 us
  starting transfers between devices: 320 us -> 3.73 us
  blocking collectives: 0 us -> 96.4 us
  local copies, waits for them, and re-layouts: 46.7 us -> 4.23 us
    ppermute x94 -> x0, waiting for transfers between devices: 589 us -> none  [shifted(): return lax.ppermute(block, axis, route)]
    ppermute x94 -> x0, starting transfers between devices: 180 us -> none  [shifted(): return lax.ppermute(block, axis, route)]
    all_to_all x4 -> x1, starting transfers between devices: 140 us -> 3.73 us  [exchange(): lax.all_to_all(parts, AXES, 0, 0, axis_index_groups=lists, tiled=True)]
    all_to_all x0 -> x5, blocking collectives: none -> 96.4 us  [the longest x3 70.2 us: exchange(): lax.all_to_all(parts, AXES, 0, 0, axis_index_groups=lists, tiled=True)]
    dynamic_update_slice x32 -> x0, local copies, waits for them, and re-layouts: 28.5 us -> none  [the longest x31 26.4 us: cycle_forward(): stored = lax.dynamic_update_index_in_dim(stored, slopes, distance, 0)]
    all_to_all x4 -> x1, waiting for transfers between devices: 6.97 us -> 24.3 us  [exchange(): lax.all_to_all(parts, AXES, 0, 0, axis_index_groups=lists, tiled=True)]
    unnamed x10 -> x4, local copies, waits for them, and re-layouts: 9.99 us -> 0.01 us
  transfers between devices with their start and end apart: 98 -> 1, of which waited for: 67 -> 1; matrix products, arithmetic and copies ran while one was open for 1% -> 0% of each run, Pallas kernels for 0% -> 0%
where the time goes in v1:
time: 134 us
  blocking collectives  96.4 us (72%)
  waiting for transfers between devices  24.3 us (18%)
  local copies, waits for them, and re-layouts  4.23 us (3%)
  Pallas kernels  3.86 us (3%)
  starting transfers between devices  3.73 us (3%)
    all_to_all x3, blocking collectives, exchange(): lax.all_to_all(parts, AXES, 0, 0, axis_index_groups=lists, tiled=True)  70.2 us
    all_to_all x1, waiting for transfers between devices, exchange(): lax.all_to_all(parts, AXES, 0, 0, axis_index_groups=lists, tiled=True)  24.3 us
    all_to_all x1, blocking collectives, shards(): lax.all_to_all(mine.reshape(tp_count, here, 2 * HEAD_SIZE), 'tp', 0, 0, t...  13.7 us
    all_to_all x1, blocking collectives, shards(): lax.all_to_all(both, 'tp', 0, 0, tiled=True).reshape(rows, 2 * HEAD_SIZE)  12.5 us
    pallas_call x1, Pallas kernels, attention_gradients(): pl.pallas_call(attention_kernel, out_shape=(jax.ShapeDtypeStruct(q.shape,...  3.86 us
    all_to_all x1, starting transfers between devices, exchange(): lax.all_to_all(parts, AXES, 0, 0, axis_index_groups=lists, tiled=True)  3.73 us
  transfers between devices with their start and end apart: 1, of which 1 were waited for; matrix products, arithmetic and copies ran while one was open for 0% of the time, Pallas kernels for 0%

profile of v1, /device:TPU:1, one launch (start us, length us, event | category | flops | bytes accessed | tf_op | source)
XLA Modules:
  0.0 133.8 jit_solution(17685256283150566682)
XLA Ops:
  0.6 0.8 stack_reshape.6
  1.4 0.1 copy.13
  1.5 0.8 stack_reshape.7
  2.2 0.1 copy.14
  2.3 0.1 maximum_bitcast_fusion
  2.5 12.5 %all_to_all.30 = bf16[4,32,256]{2,1,0:T(8,128)(2,1)S(1)} all-to-all(bf16[4,32,256]{2,1,0:T(8,128)(2,1)S(1)} %reshape.27), channel_id=1, replica_groups=mesh['ctx'=128,'tp'=4] {'tp'}, dimensions={0} | all-to-all | bytes 131072 | tf_op jit(solution)/shard_map/all_to_all | solution.py:195
  15.0 9.5 %all_to_all.31 = bf16[4,128,256]{2,1,0:T(8,128)(2,1)S(1)} all-to-all(bf16[4,128,256]{2,1,0:T(8,128)(2,1)S(1)} %broadcast_in_dim.6), channel_id=1, replica_groups={{0,32,64,96},{4,36,68,100},{8,40,72,104},{12,44,76,108},{16,48,80,112},..., dimensions={0} | all-to-all | bytes 524288 | tf_op jit(solution)/shard_map/all_to_all | solution.py:177
  24.5 1.6 %broadcast_in_dim.7 = bf16[8,4,128,256]{3,2,1,0:T(8,128)(2,1)} broadcast(bf16[4,128,256]{2,1,0:T(8,128)(2,1)S(1)} %all_to_all.31), dimensions={1,2,3} | broadcast | bytes 2359296 | tf_op jit(solution)/shard_map/broadcast_in_dim | solution.py:197
  26.1 0.0 copy-start
  26.1 0.0 copy-start.1
  26.1 3.7 %all-to-all-start.2 = ((bf16[8,4,128,256]{3,2,1,0:T(8,128)(2,1)}), bf16[8,4,128,256]{3,2,1,0:T(8,128)(2,1)S(1)}, u32[]{:S(2)}, u32[]{:S(2)}) async-start(bf16[8,4,128,256]{3,2,1,0:T(8,128)(2,1)} %broadcast_in_dim.7), calls=%async_computation.2 | async-start | bytes 4194304 | tf_op jit(solution)/shard_map/all_to_all | solution.py:177
  29.9 24.3 %all-to-all-done.2.kv_ref = bf16[8,4,128,256]{3,2,1,0:T(8,128)(2,1)S(1)} async-done(((bf16[8,4,128,256]{3,2,1,0:T(8,128)(2,1)}), bf16[8,4,128,256]{3,2,1,0:T(8,128)(2,1)S(1)}, u32[]{:S(2)}, u32[]{:S(2)}) %all-to-all-start.2) | async-done | bytes 2097184 | tf_op jit(solution)/shard_map/all_to_all | solution.py:177
  54.2 0.0 copy-done
  54.2 0.0 copy-done.1
  54.2 3.9 %attention_gradients.1 = (f32[128,1024]{1,0:T(8,128)}, bf16[8,4,128,256]{3,2,1,0:T(8,128)(2,1)S(1)}) custom-call(s32[1]{0:T(128)} %bitcast.rank_ref, bf16[128,1024]{1,0:T(8,128)(2,1)S(1)} %copy-done, bf16[128,1024]{1,0:T(8,128)(2,1)S(1)} %copy-done.1, bf16[8,4,128,256]{3,2,1,0:T(8,128)(2,1)S(1)} %all-to-all-done.2.kv_ref), custom_call_target="tpu_custom_call" | custom-call | flops 5368709120 | bytes 6291456 | tf_op jit(solution)/shard_map/attention_gradients/pallas_call | solution.py:130
  58.0 33.6 %all_to_all.32 = bf16[8,4,128,256]{3,2,1,0:T(8,128)(2,1)S(1)} all-to-all(bf16[8,4,128,256]{3,2,1,0:T(8,128)(2,1)S(1)} %get-tuple-element.6), channel_id=1, replica_groups={{0,4,8,12,16,20,24,28},{32,36,40,44,48,52,56,60},{64,68,72,76,80,84,88,..., dimensions={0} | all-to-all | bytes 4194304 | tf_op jit(solution)/shard_map/all_to_all | solution.py:177
  91.7 0.3 reduce_sum.21
  92.0 27.0 %all_to_all.33 = bf16[4,128,256]{2,1,0:T(8,128)(2,1)S(1)} all-to-all(bf16[4,128,256]{2,1,0:T(8,128)(2,1)S(1)} %reduce_sum.21), channel_id=1, replica_groups={{0,32,64,96},{4,36,68,100},{8,40,72,104},{12,44,76,108},{16,48,80,112},..., dimensions={0} | all-to-all | bytes 524288 | tf_op jit(solution)/shard_map/all_to_all | solution.py:177
  119.1 13.7 %all_to_all.34 = f32[4,32,256]{2,1,0:T(8,128)S(1)} all-to-all(f32[4,32,256]{2,1,0:T(8,128)S(1)} %bitcast.14), channel_id=1, replica_groups=mesh['ctx'=128,'tp'=4] {'tp'}, dimensions={0} | all-to-all | bytes 262144 | tf_op jit(solution)/shard_map/all_to_all | solution.py:201
  132.8 0.1 reshape.30
  132.9 0.1 fusion
  133.1 0.7 copy_bitcast_fusion
  (5 shorter events, 0.2 us)
Async XLA Ops:
  26.1 28.1 %copy-start = (bf16[128,1024]{1,0:T(8,128)(2,1)S(1)}, bf16[128,1024]{1,0:T(8,128)(2,1)}, u32[]{:S(2)}) copy-start(bf16[128,1024]{1,0:T(8,128)(2,1)} %q_ref.1) | copy-start | bytes 786436
  26.1 28.1 %copy-start.1 = (bf16[128,1024]{1,0:T(8,128)(2,1)S(1)}, bf16[128,1024]{1,0:T(8,128)(2,1)}, u32[]{:S(2)}) copy-start(bf16[128,1024]{1,0:T(8,128)(2,1)} %do_ref.1) | copy-start | bytes 786436
  26.1 28.1 %all-to-all-start.2 = ((bf16[8,4,128,256]{3,2,1,0:T(8,128)(2,1)}), bf16[8,4,128,256]{3,2,1,0:T(8,128)(2,1)S(1)}, u32[]{:S(2)}, u32[]{:S(2)}) async-start(bf16[8,4,128,256]{3,2,1,0:T(8,128)(2,1)} %broadcast_in_dim.7), calls=%async_computation.2 | async-start | bytes 4194304 | tf_op jit(solution)/shard_map/all_to_all | solution.py:177

commit v2 on v1

v2 whole, which is shorter than its diff:
```python
import functools
import math

import jax
import jax.numpy as jnp
from jax import lax
from jax.experimental import pallas as pl
from jax.experimental.pallas import tpu as pltpu
from jax.sharding import PartitionSpec as P

HEAD_SIZE = 128
GROUPS = 4
SLABS = 4
PAIR = 2
ROWS = 512
LOWEST = -1e30
AXES = ("ctx", "tp")
BF16, F32 = jnp.bfloat16, jnp.float32
SCALE = 1.0 / math.sqrt(HEAD_SIZE)


def product(a, b):
    return jnp.dot(a, b, preferred_element_type=F32)


def keys_of(kv_ref, slab, column):
    part = kv_ref[:, slab, :, column * HEAD_SIZE : (column + 1) * HEAD_SIZE]
    return part.reshape(part.shape[0] * part.shape[1], HEAD_SIZE)


def statistics_kernel(
    place_ref, q_ref, do_ref, peer_ref, kv_ref, stats_ref, weights_ref, slopes_ref, q_cols, do_cols
):
    tokens, width = q_ref.shape
    heads = width // HEAD_SIZE
    mine = heads * tokens
    keys = kv_ref.shape[0] * kv_ref.shape[2]
    slab, along_y, along_x = place_ref[0], place_ref[1], place_ref[2]

    for owner in range(PAIR):
        q = q_ref if owner == 0 else peer_ref.at[0]
        do = do_ref if owner == 0 else peer_ref.at[1]
        for h in range(heads):
            across = slice(h * HEAD_SIZE, (h + 1) * HEAD_SIZE)
            down = slice(owner * mine + h * tokens, owner * mine + (h + 1) * tokens)
            q_cols[:, down] = q[:, across].T
            do_cols[:, down] = do[:, across].T

    for tile in range(PAIR * mine // ROWS):
        rows = slice(tile * ROWS, (tile + 1) * ROWS)

        def step(s, carry, masked):
            highest, norm, weighted = carry
            scores = product(keys_of(kv_ref, s, 0), q_cols[:, rows]) * (SCALE * math.log2(math.e))
            if masked:
                key = lax.broadcasted_iota(jnp.int32, (keys, ROWS), 0)
                if tile * ROWS < mine:
                    last = along_y * tokens + lax.rem(
                        lax.broadcasted_iota(jnp.int32, (keys, ROWS), 1), jnp.int32(tokens)
                    )
                else:
                    last = (along_y + 1 - along_x) * tokens - 1
                scores = jnp.where(key <= last, scores, LOWEST)
            higher = jnp.maximum(highest, jnp.max(scores, axis=0, keepdims=True))
            weight = jnp.exp2(scores - higher)
            factor = jnp.exp2(highest - higher)
            slope = product(keys_of(kv_ref, s, 1), do_cols[:, rows])
            weights_ref[s, :, rows] = weight.astype(weights_ref.dtype)
            slopes_ref[s, :, rows] = slope.astype(slopes_ref.dtype)
            stats_ref[pl.ds(s, 1), rows] = higher
            norm = norm * factor + jnp.sum(weight, axis=0, keepdims=True)
            weighted = weighted * factor + jnp.sum(weight * slope, axis=0, keepdims=True)
            return higher, norm, weighted

        zeros = jnp.zeros((1, ROWS), F32)
        carry = lax.fori_loop(
            0, slab, functools.partial(step, masked=False),
            (jnp.full((1, ROWS), LOWEST, F32), zeros, zeros),
        )
        highest, norm, weighted = step(slab, carry, True)
        stats_ref[SLABS : SLABS + 1, rows] = highest
        stats_ref[SLABS + 1 : SLABS + 2, rows] = norm
        stats_ref[SLABS + 2 : SLABS + 3, rows] = weighted


def gradients_kernel(
    place_ref, q_ref, do_ref, peer_ref, kv_ref, stats_ref, other_ref, weights_ref, slopes_ref,
    dq_ref, dq_peer_ref, dkv_ref,
    q_rows, do_rows, k_cols, total,
):
    tokens, width = q_ref.shape
    heads = width // HEAD_SIZE
    mine = heads * tokens
    along_y = kv_ref.shape[0]
    keys = along_y * tokens
    slab = place_ref[0]

    for owner in range(PAIR):
        q = q_ref if owner == 0 else peer_ref.at[0]
        do = do_ref if owner == 0 else peer_ref.at[1]
        for h in range(heads):
            across = slice(h * HEAD_SIZE, (h + 1) * HEAD_SIZE)
            down = slice(owner * mine + h * tokens, owner * mine + (h + 1) * tokens)
            q_rows[down, :] = q[:, across]
            do_rows[down, :] = do[:, across]

    @pl.loop(0, slab + 1)
    def _(s):
        k_cols[s] = keys_of(kv_ref, s, 0).T

    for tile in range(PAIR * mine // ROWS):
        rows = slice(tile * ROWS, (tile + 1) * ROWS)
        there = slice((tile * ROWS + mine) % (PAIR * mine), (tile * ROWS + mine) % (PAIR * mine) + ROWS)
        here_highest = stats_ref[SLABS : SLABS + 1, rows]
        there_highest = other_ref[SLABS : SLABS + 1, there]
        highest = jnp.maximum(here_highest, there_highest)
        here_factor = jnp.exp2(here_highest - highest)
        there_factor = jnp.exp2(there_highest - highest)

        def merged(i):
            at = slice(SLABS + i, SLABS + i + 1)
            return stats_ref[at, rows] * here_factor + other_ref[at, there] * there_factor

        inverse = 1.0 / merged(1)
        centre = merged(2) * inverse

        def step(s, dq_cols):
            factor = jnp.exp2(stats_ref[pl.ds(s, 1), rows] - highest) * inverse
            soft = weights_ref[s, :, rows].astype(F32) * factor
            score_grad = (soft * (slopes_ref[s, :, rows].astype(F32) - centre)).astype(BF16)
            dk = product(score_grad, q_rows[rows, :])
            dv = product(soft.astype(BF16), do_rows[rows, :])
            if tile == 0:
                total[s, :, 0:HEAD_SIZE] = dk
                total[s, :, HEAD_SIZE:] = dv
            else:
                total[s, :, 0:HEAD_SIZE] += dk
                total[s, :, HEAD_SIZE:] += dv
            return dq_cols + product(k_cols[s], score_grad)

        dq_cols = lax.fori_loop(0, slab + 1, step, jnp.zeros((HEAD_SIZE, ROWS), F32)) * SCALE
        for i in range(ROWS // tokens):
            h = tile * (ROWS // tokens) + i
            out = dq_ref if h < heads else dq_peer_ref
            across = slice(h % heads * HEAD_SIZE, (h % heads + 1) * HEAD_SIZE)
            out[:, across] = dq_cols[:, i * tokens : (i + 1) * tokens].T.astype(out.dtype)

    @pl.loop(0, SLABS)
    def _(s):
        @pl.when(s <= slab)
        def _():
            dk = (total[s, :, 0:HEAD_SIZE] * SCALE).astype(BF16)
            dv = total[s, :, HEAD_SIZE:].astype(BF16)
            dkv_ref[:, s, :, 0:HEAD_SIZE] = dk.reshape(along_y, tokens, HEAD_SIZE)
            dkv_ref[:, s, :, HEAD_SIZE:] = dv.reshape(along_y, tokens, HEAD_SIZE)

        @pl.when(s > slab)
        def _():
            dkv_ref[:, s] = jnp.zeros((along_y, tokens, 2 * HEAD_SIZE), BF16)


WHOLE = pl.BlockSpec(memory_space=pltpu.VMEM)
SCALARS = pl.BlockSpec(memory_space=pltpu.SMEM)


def row_statistics(place, q, do, peer, kv):
    tokens, width = q.shape
    rows = PAIR * tokens * (width // HEAD_SIZE)
    keys = kv.shape[0] * kv.shape[2]
    return pl.pallas_call(
        statistics_kernel,
        out_shape=(
            jax.ShapeDtypeStruct((8, rows), F32),
            jax.ShapeDtypeStruct((SLABS, keys, rows), F32),
            jax.ShapeDtypeStruct((SLABS, keys, rows), F32),
        ),
        in_specs=[SCALARS, WHOLE, WHOLE, WHOLE, WHOLE],
        out_specs=(WHOLE, WHOLE, WHOLE),
        scratch_shapes=[pltpu.VMEM((HEAD_SIZE, rows), BF16), pltpu.VMEM((HEAD_SIZE, rows), BF16)],
        compiler_params=pltpu.CompilerParams(vmem_limit_bytes=12 * 2**20),
        cost_estimate=pl.CostEstimate(
            flops=4 * rows * SLABS * keys * HEAD_SIZE, bytes_accessed=2 * 2**20, transcendentals=rows * SLABS * keys
        ),
        name="row_statistics",
    )(place, q, do, peer, kv)


def attention_gradients(place, q, do, peer, kv, stats, other, weights, slopes):
    tokens, width = q.shape
    rows = PAIR * tokens * (width // HEAD_SIZE)
    keys = kv.shape[0] * kv.shape[2]
    return pl.pallas_call(
        gradients_kernel,
        out_shape=(
            jax.ShapeDtypeStruct(q.shape, F32),
            jax.ShapeDtypeStruct(q.shape, BF16),
            jax.ShapeDtypeStruct(kv.shape, BF16),
        ),
        in_specs=[SCALARS] + [WHOLE] * 8,
        out_specs=(WHOLE, WHOLE, WHOLE),
        scratch_shapes=[
            pltpu.VMEM((rows, HEAD_SIZE), BF16),
            pltpu.VMEM((rows, HEAD_SIZE), BF16),
            pltpu.VMEM((SLABS, HEAD_SIZE, keys), BF16),
            pltpu.VMEM((SLABS, keys, 2 * HEAD_SIZE), F32),
        ],
        compiler_params=pltpu.CompilerParams(vmem_limit_bytes=12 * 2**20),
        cost_estimate=pl.CostEstimate(
            flops=6 * rows * SLABS * keys * HEAD_SIZE, bytes_accessed=4 * 2**20, transcendentals=rows
        ),
        name="attention_gradients",
    )(place, q, do, peer, kv, stats, other, weights, slopes)


def line_lists(ctx_count, tp_count, along_z):
    span = ctx_count // GROUPS
    plane = span // SLABS
    lists = []
    for t in range(tp_count):
        first = span // 2 if t >= tp_count // 2 and along_z else 0
        for g in range(GROUPS):
            if along_z:
                lines = [[first + g * span + s * plane + p for s in range(SLABS)] for p in range(plane)]
            else:
                lines = [
                    [g * span + s * plane + y * PAIR + x for y in range(plane // PAIR)]
                    for s in range(SLABS)
                    for x in range(PAIR)
                ]
            lists += [[c % ctx_count * tp_count + t for c in line] for line in lines]
    return lists


def exchange(parts, lists):
    return lax.all_to_all(parts, AXES, 0, 0, axis_index_groups=lists, tiled=True)


def to_peer(array):
    return lax.ppermute(array, "ctx", [(c, c ^ 1) for c in range(lax.axis_size("ctx"))])


def shards(query_heads, key_heads_wide, value_heads_wide, grad_output):
    ctx_count = lax.axis_size("ctx")
    tp_count = lax.axis_size("tp")
    span = ctx_count // GROUPS
    plane = span // SLABS
    lines = plane // PAIR
    here = key_heads_wide.shape[0]
    rows = query_heads.shape[0]
    along_z = line_lists(ctx_count, tp_count, True)
    along_y = line_lists(ctx_count, tp_count, False)
    offset = jnp.where(lax.axis_index("tp") >= tp_count // 2, span // 2, 0)
    rank = (jnp.mod(lax.axis_index("ctx") - offset, ctx_count) % span).astype(jnp.int32)
    place = jnp.stack([rank // plane, rank % plane // PAIR, rank % PAIR])

    peer = to_peer(jnp.stack([query_heads, grad_output]))
    both = jnp.stack(
        [a.reshape(here, tp_count, HEAD_SIZE) for a in (key_heads_wide, value_heads_wide)], axis=2
    ).transpose(1, 0, 2, 3).reshape(tp_count, here, 2 * HEAD_SIZE)
    own = lax.all_to_all(both, "tp", 0, 0, tiled=True).reshape(rows, 2 * HEAD_SIZE)
    column = exchange(jnp.broadcast_to(own, (SLABS,) + own.shape), along_z)
    kv = exchange(jnp.broadcast_to(column, (lines,) + column.shape), along_y)
    stats, weights, slopes = row_statistics(place, query_heads, grad_output, peer, kv)
    other = to_peer(stats)
    dq, dq_peer, dkv = attention_gradients(
        place, query_heads, grad_output, peer, kv, stats, other, weights, slopes
    )
    grad_query = dq + to_peer(dq_peer).astype(F32)
    partial = jnp.sum(exchange(dkv, along_y).astype(F32), axis=0).astype(BF16)
    mine = jnp.sum(exchange(partial, along_z).astype(F32), axis=0)
    back = lax.all_to_all(mine.reshape(tp_count, here, 2 * HEAD_SIZE), "tp", 0, 0, tiled=True)
    back = back.reshape(tp_count, here, 2, HEAD_SIZE).transpose(2, 1, 0, 3)
    back = back.reshape(2, here, tp_count * HEAD_SIZE)
    return grad_query, back[0], back[1]


def solution(mesh):
    return jax.shard_map(
        shards,
        mesh=mesh,
        in_specs=(P("ctx", "tp"), P(AXES, None), P(AXES, None), P("ctx", "tp")),
        out_specs=(P("ctx", "tp"), P(AXES, None), P(AXES, None)),
        check_vma=False,
    )
```

time: 134 us -> 118 us (0.88)
  blocking collectives: 96.4 us -> 35.4 us
  starting transfers between devices: 3.73 us -> 41.9 us
  other arithmetic: 0.52 us -> 3.73 us
  Pallas kernels: 3.86 us -> 6.78 us
  waiting for transfers between devices: 24.3 us -> 22.8 us
  local copies, waits for them, and re-layouts: 4.23 us -> 5.61 us
    all_to_all x3 -> x2, blocking collectives: 70.2 us -> 22.9 us  [exchange(): lax.all_to_all(parts, AXES, 0, 0, axis_index_groups=lists, tiled=True)]
    all_to_all x1 -> x2, waiting for transfers between devices: 24.3 us -> 3.51 us  [exchange(): lax.all_to_all(parts, AXES, 0, 0, axis_index_groups=lists, tiled=True)]
    all_to_all x1 -> x2, starting transfers between devices: 3.73 us -> 24.1 us  [exchange(): lax.all_to_all(parts, AXES, 0, 0, axis_index_groups=lists, tiled=True)]
    ppermute x0 -> x3, waiting for transfers between devices: none -> 16.6 us  [to_peer(): lax.ppermute(array, 'ctx', [(c, c ^ 1) for c in range(lax.axis_size('ctx'...]
    all_to_all x1 -> x0, blocking collectives: 13.7 us -> none  [shards(): lax.all_to_all(mine.reshape(tp_count, here, 2 * HEAD_SIZE), 'tp', 0, 0, t...]
    all_to_all x0 -> x1, starting transfers between devices: none -> 11.8 us  [shards(): lax.all_to_all(mine.reshape(tp_count, here, 2 * HEAD_SIZE), 'tp', 0, 0, t...]
    ppermute x0 -> x3, starting transfers between devices: none -> 5.97 us  [to_peer(): lax.ppermute(array, 'ctx', [(c, c ^ 1) for c in range(lax.axis_size('ctx'...]
    pallas_call x1 -> x2, Pallas kernels: 3.86 us -> 6.78 us  [the longest x1 3.72 us: attention_gradients(): pl.pallas_call(gradients_kernel, out_shape=(jax.ShapeDtypeStruct(q.shape,...]
  transfers between devices with their start and end apart: 1 -> 6, of which waited for: 1 -> 4; matrix products, arithmetic and copies ran while one was open for 0% -> 2% of each run, Pallas kernels for 0% -> 0%
where the time goes in v2:
time: 118 us; the launch traced here: 117 us
  starting transfers between devices  41.9 us (36%)
  blocking collectives  35.4 us (30%)
  waiting for transfers between devices  22.8 us (19%)
  Pallas kernels  6.78 us (6%)
  local copies, waits for them, and re-layouts  5.61 us (5%)
  other arithmetic  3.73 us (3%)
    all_to_all x2, starting transfers between devices, exchange(): lax.all_to_all(parts, AXES, 0, 0, axis_index_groups=lists, tiled=True)  24.1 us
    all_to_all x2, blocking collectives, exchange(): lax.all_to_all(parts, AXES, 0, 0, axis_index_groups=lists, tiled=True)  22.9 us
    ppermute x3, waiting for transfers between devices, to_peer(): lax.ppermute(array, 'ctx', [(c, c ^ 1) for c in range(lax.axis_size('ctx'...  16.6 us
    all_to_all x1, blocking collectives, shards(): lax.all_to_all(both, 'tp', 0, 0, tiled=True).reshape(rows, 2 * HEAD_SIZE)  12.5 us
    all_to_all x1, starting transfers between devices, shards(): lax.all_to_all(mine.reshape(tp_count, here, 2 * HEAD_SIZE), 'tp', 0, 0, t...  11.8 us
    ppermute x3, starting transfers between devices, to_peer(): lax.ppermute(array, 'ctx', [(c, c ^ 1) for c in range(lax.axis_size('ctx'...  5.97 us
    pallas_call x1, Pallas kernels, attention_gradients(): pl.pallas_call(gradients_kernel, out_shape=(jax.ShapeDtypeStruct(q.shape,...  3.72 us
    all_to_all x2, waiting for transfers between devices, exchange(): lax.all_to_all(parts, AXES, 0, 0, axis_index_groups=lists, tiled=True)  3.51 us
  transfers between devices with their start and end apart: 6, of which 4 were waited for; matrix products, arithmetic and copies ran while one was open for 2% of the time, Pallas kernels for 0%

profile of v2, /device:TPU:1, one launch (start us, length us, event | category | flops | bytes accessed | tf_op | source)
XLA Modules:
  0.0 117.1 jit_solution(9514686200265888710)
XLA Ops:
  0.6 0.8 stack_reshape.6
  1.4 0.1 copy.13
  1.5 0.8 stack_reshape.7
  2.2 0.1 copy.14
  2.3 0.1 maximum_bitcast_fusion
  2.5 12.5 %all_to_all.30 = bf16[4,32,256]{2,1,0:T(8,128)(2,1)S(1)} all-to-all(bf16[4,32,256]{2,1,0:T(8,128)(2,1)S(1)} %reshape.23), channel_id=1, replica_groups=mesh['ctx'=128,'tp'=4] {'tp'}, dimensions={0} | all-to-all | bytes 131072 | tf_op jit(solution)/shard_map/all_to_all | solution.py:260
  15.0 9.5 %all_to_all.31 = bf16[4,128,256]{2,1,0:T(8,128)(2,1)S(1)} all-to-all(bf16[4,128,256]{2,1,0:T(8,128)(2,1)S(1)} %broadcast_in_dim.6), channel_id=1, replica_groups={{0,32,64,96},{4,36,68,100},{8,40,72,104},{12,44,76,108},{16,48,80,112},..., dimensions={0} | all-to-all | bytes 524288 | tf_op jit(solution)/shard_map/all_to_all | solution.py:235
  24.5 1.1 broadcast_in_dim.7
  25.6 3.5 %all-to-all-start.2 = ((bf16[4,4,128,256]{3,2,1,0:T(8,128)(2,1)}), bf16[4,4,128,256]{3,2,1,0:T(8,128)(2,1)S(1)}, u32[]{:S(2)}, u32[]{:S(2)}) async-start(bf16[4,4,128,256]{3,2,1,0:T(8,128)(2,1)} %broadcast_in_dim.7), calls=%async_computation.2 | async-start | bytes 2097152 | tf_op jit(solution)/shard_map/all_to_all | solution.py:235
  29.1 1.1 pad_maximum_fusion
  30.2 1.9 %collective-permute-start = (bf16[2,128,1024]{2,1,0:T(8,128)(2,1)S(1)}, bf16[2,128,1024]{2,1,0:T(8,128)(2,1)S(1)}, u32[]{:S(2)}, u32[]{:S(2)}) collective-permute-start(bf16[2,128,1024]{2,1,0:T(8,128)(2,1)S(1)} %pad_maximum_fusion), channel_id=1, source_target_pairs={{0,4},{4,0},{8,12},{12,8},{16,20},{20,16},{24,28},{28,24},{32,36},... | collective-permute-start | bytes 1572872 | tf_op jit(solution)/shard_map/ppermute | solution.py:239
  32.2 0.1 pad_add_fusion.place_ref
  32.3 12.0 %collective-permute-done.peer_ref = bf16[2,128,1024]{2,1,0:T(8,128)(2,1)S(1)} collective-permute-done((bf16[2,128,1024]{2,1,0:T(8,128)(2,1)S(1)}, bf16[2,128,1024]{2,1,0:T(8,128)(2,1)S(1)}, u32[]{:S(2)}, u32[]{:S(2)}) %collective-permute-start) | collective-permute-done | bytes 524320 | tf_op jit(solution)/shard_map/ppermute | solution.py:239
  44.3 0.0 all-to-all-done.2.kv_ref
  44.3 0.0 copy-start
  44.3 0.9 copy-done
  45.2 0.0 copy-start.1
  45.2 0.9 copy-done.1
  46.2 3.1 %row_statistics.1 = (f32[8,2048]{1,0:T(8,128)S(1)}, f32[4,512,2048]{2,1,0:T(8,128)S(1)}, f32[4,512,2048]{2,1,0:T(8,128)S(1)}) custom-call(s32[3]{0:T(128)S(1)} %pad_add_fusion.place_ref, bf16[128,1024]{1,0:T(8,128)(2,1)S(1)} %copy-done, bf16[128,1024]{1,0:T(8,128)(2,1)S(1)} %copy-done.1, bf16[2,128,1024]{2,1,0:T(8,128)(2,1)S(1)} %collective-permute-done.peer_ref, ...), custom_call_target="tpu_custom_call" | custom-call | flops 2147483648 | bytes 2097152 | tf_op jit(solution)/shard_map/row_statistics/pallas_call | solution.py:170
  49.2 1.9 %collective-permute-start.1 = (f32[8,2048]{1,0:T(8,128)S(1)}, f32[8,2048]{1,0:T(8,128)S(1)}, u32[]{:S(2)}, u32[]{:S(2)}) collective-permute-start(f32[8,2048]{1,0:T(8,128)S(1)} %get-tuple-element.9.stats_ref), channel_id=1, source_target_pairs={{0,4},{4,0},{8,12},{12,8},{16,20},{20,16},{24,28},{28,24},{32,36},... | collective-permute-start | bytes 196616 | tf_op jit(solution)/shard_map/ppermute | solution.py:239
  51.2 4.6 %collective-permute-done.1.other_ref = f32[8,2048]{1,0:T(8,128)S(1)} collective-permute-done((f32[8,2048]{1,0:T(8,128)S(1)}, f32[8,2048]{1,0:T(8,128)S(1)}, u32[]{:S(2)}, u32[]{:S(2)}) %collective-permute-start.1) | collective-permute-done | bytes 65568 | tf_op jit(solution)/shard_map/ppermute | solution.py:239
  55.7 3.7 %attention_gradients.1 = (f32[128,1024]{1,0:T(8,128)S(1)}, bf16[128,1024]{1,0:T(8,128)(2,1)S(1)}, bf16[4,4,128,256]{3,2,1,0:T(8,128)(2,1)S(1)}) custom-call(s32[3]{0:T(128)S(1)} %pad_add_fusion.place_ref, bf16[128,1024]{1,0:T(8,128)(2,1)S(1)} %copy-done, bf16[128,1024]{1,0:T(8,128)(2,1)S(1)} %copy-done.1, ...), custom_call_target="tpu_custom_call" | custom-call | flops 3221225472 | bytes 4194304 | tf_op jit(solution)/shard_map/attention_gradients/pallas_call | solution.py:192
  59.5 13.5 %all_to_all.32 = bf16[4,4,128,256]{3,2,1,0:T(8,128)(2,1)S(1)} all-to-all(bf16[4,4,128,256]{3,2,1,0:T(8,128)(2,1)S(1)} %get-tuple-element.14), channel_id=1, replica_groups={{0,8,16,24},{4,12,20,28},{32,40,48,56},{36,44,52,60},{64,72,80,88},{68,..., dimensions={0} | all-to-all | bytes 2097152 | tf_op jit(solution)/shard_map/all_to_all | solution.py:235
  72.9 0.9 reduce_sum.21
  73.9 20.6 %all-to-all-start.4 = ((bf16[4,128,256]{2,1,0:T(8,128)(2,1)}), bf16[4,128,256]{2,1,0:T(8,128)(2,1)S(1)}, u32[]{:S(2)}, u32[]{:S(2)}) async-start(bf16[4,128,256]{2,1,0:T(8,128)(2,1)} %reduce_sum.21), calls=%async_computation.4 | async-start | bytes 524288 | tf_op jit(solution)/shard_map/all_to_all | solution.py:235
  94.5 2.1 %collective-permute-start.2 = (bf16[128,1024]{1,0:T(8,128)(2,1)S(1)}, bf16[128,1024]{1,0:T(8,128)(2,1)S(1)}, u32[]{:S(2)}, u32[]{:S(2)}) collective-permute-start(bf16[128,1024]{1,0:T(8,128)(2,1)S(1)} %get-tuple-element.13), channel_id=1, source_target_pairs={{0,4},{4,0},{8,12},{12,8},{16,20},{20,16},{24,28},{28,24},{32,36},... | collective-permute-start | bytes 786440 | tf_op jit(solution)/shard_map/ppermute | solution.py:239
  96.6 3.5 %all-to-all-done.4 = bf16[4,128,256]{2,1,0:T(8,128)(2,1)S(1)} async-done(((bf16[4,128,256]{2,1,0:T(8,128)(2,1)}), bf16[4,128,256]{2,1,0:T(8,128)(2,1)S(1)}, u32[]{:S(2)}, u32[]{:S(2)}) %all-to-all-start.4) | async-done | bytes 262176 | tf_op jit(solution)/shard_map/all_to_all | solution.py:235
  100.1 0.7 convert_reduce_fusion
  100.8 11.8 %all-to-all-start.5 = ((f32[4,32,256]{2,1,0:T(8,128)}), f32[4,32,256]{2,1,0:T(8,128)S(1)}, u32[]{:S(2)}, u32[]{:S(2)}) async-start(f32[4,32,256]{2,1,0:T(8,128)} %bitcast.7), calls=%async_computation.5 | async-start | bytes 262144 | tf_op jit(solution)/shard_map/all_to_all | solution.py:271
  112.5 0.0 collective-permute-done.2
  112.6 0.8 convert_add_fusion
  113.4 2.7 %all-to-all-done.5 = f32[4,32,256]{2,1,0:T(8,128)S(1)} async-done(((f32[4,32,256]{2,1,0:T(8,128)}), f32[4,32,256]{2,1,0:T(8,128)S(1)}, u32[]{:S(2)}, u32[]{:S(2)}) %all-to-all-start.5) | async-done | bytes 131104 | tf_op jit(solution)/shard_map/all_to_all | solution.py:271
  116.1 0.1 reshape.26
  116.2 0.1 fusion
  116.4 0.7 copy_bitcast_fusion
  (4 shorter events, 0.2 us)
Async XLA Ops:
  25.6 18.7 %all-to-all-start.2 = ((bf16[4,4,128,256]{3,2,1,0:T(8,128)(2,1)}), bf16[4,4,128,256]{3,2,1,0:T(8,128)(2,1)S(1)}, u32[]{:S(2)}, u32[]{:S(2)}) async-start(bf16[4,4,128,256]{3,2,1,0:T(8,128)(2,1)} %broadcast_in_dim.7), calls=%async_computation.2 | async-start | bytes 2097152 | tf_op jit(solution)/shard_map/all_to_all | solution.py:235
  30.2 14.1 %collective-permute-start = (bf16[2,128,1024]{2,1,0:T(8,128)(2,1)S(1)}, bf16[2,128,1024]{2,1,0:T(8,128)(2,1)S(1)}, u32[]{:S(2)}, u32[]{:S(2)}) collective-permute-start(bf16[2,128,1024]{2,1,0:T(8,128)(2,1)S(1)} %pad_maximum_fusion), channel_id=1, source_target_pairs={{0,4},{4,0},{8,12},{12,8},{16,20},{20,16},{24,28},{28,24},{32,36},... | collective-permute-start | bytes 1572872 | tf_op jit(solution)/shard_map/ppermute | solution.py:239
  44.3 1.0 copy-start
  45.2 0.9 copy-start.1
  49.2 6.5 %collective-permute-start.1 = (f32[8,2048]{1,0:T(8,128)S(1)}, f32[8,2048]{1,0:T(8,128)S(1)}, u32[]{:S(2)}, u32[]{:S(2)}) collective-permute-start(f32[8,2048]{1,0:T(8,128)S(1)} %get-tuple-element.9.stats_ref), channel_id=1, source_target_pairs={{0,4},{4,0},{8,12},{12,8},{16,20},{20,16},{24,28},{28,24},{32,36},... | collective-permute-start | bytes 196616 | tf_op jit(solution)/shard_map/ppermute | solution.py:239
  73.9 26.2 %all-to-all-start.4 = ((bf16[4,128,256]{2,1,0:T(8,128)(2,1)}), bf16[4,128,256]{2,1,0:T(8,128)(2,1)S(1)}, u32[]{:S(2)}, u32[]{:S(2)}) async-start(bf16[4,128,256]{2,1,0:T(8,128)(2,1)} %reduce_sum.21), calls=%async_computation.4 | async-start | bytes 524288 | tf_op jit(solution)/shard_map/all_to_all | solution.py:235
  94.5 18.1 %collective-permute-start.2 = (bf16[128,1024]{1,0:T(8,128)(2,1)S(1)}, bf16[128,1024]{1,0:T(8,128)(2,1)S(1)}, u32[]{:S(2)}, u32[]{:S(2)}) collective-permute-start(bf16[128,1024]{1,0:T(8,128)(2,1)S(1)} %get-tuple-element.13), channel_id=1, source_target_pairs={{0,4},{4,0},{8,12},{12,8},{16,20},{20,16},{24,28},{28,24},{32,36},... | collective-permute-start | bytes 786440 | tf_op jit(solution)/shard_map/ppermute | solution.py:239
  100.8 15.4 %all-to-all-start.5 = ((f32[4,32,256]{2,1,0:T(8,128)}), f32[4,32,256]{2,1,0:T(8,128)S(1)}, u32[]{:S(2)}, u32[]{:S(2)}) async-start(f32[4,32,256]{2,1,0:T(8,128)} %bitcast.7), calls=%async_computation.5 | async-start | bytes 262144 | tf_op jit(solution)/shard_map/all_to_all | solution.py:271

commit v3 on v2

v3 whole, which is shorter than its diff:
```python
import functools
import math

import jax
import jax.numpy as jnp
from jax import lax
from jax.experimental import pallas as pl
from jax.experimental.pallas import tpu as pltpu
from jax.sharding import PartitionSpec as P

HEAD_SIZE = 128
GROUPS = 4
SLABS = 4
PAIR = 2
ROWS = 1024
LOWEST = -1e30
AXES = ("ctx", "tp")
BF16, F32 = jnp.bfloat16, jnp.float32
SCALE = 1.0 / math.sqrt(HEAD_SIZE)


def product(a, b):
    return jnp.dot(a, b, preferred_element_type=F32)


def product_of_rows(a, b):
    return lax.dot_general(a, b, (((1,), (1,)), ((), ())), preferred_element_type=F32)


def keys_of(kv_ref, slab, column):
    part = kv_ref[:, slab, :, column * HEAD_SIZE : (column + 1) * HEAD_SIZE]
    return part.reshape(part.shape[0] * part.shape[1], HEAD_SIZE)


def by_head(ref, out):
    tokens = ref.shape[0]
    for h in range(ref.shape[1] // HEAD_SIZE):
        out[h * tokens : (h + 1) * tokens, :] = ref[:, h * HEAD_SIZE : (h + 1) * HEAD_SIZE]


def row_of(ref, i, tile):
    width = ref.shape[1]
    first = 8 * i + tile * (ROWS // width)
    return jnp.concatenate([ref[r : r + 1, :] for r in range(first, first + ROWS // width)], axis=1)


def rows_kernel(q_ref, do_ref, q_rows, do_rows):
    by_head(q_ref, q_rows)
    by_head(do_ref, do_rows)


def statistics_kernel(of_peer, place_ref, *refs):
    if of_peer:
        q_ref, do_ref, kv_ref, own_stats, stats_ref, maxima_ref, weights_ref, slopes_ref, q_rows, do_rows = refs
        rows_kernel(q_ref, do_ref, q_rows, do_rows)
        stats_ref[...] = own_stats[...]
    else:
        q_rows, do_rows, kv_ref, stats_ref, maxima_ref, weights_ref, slopes_ref = refs
    tokens = kv_ref.shape[2]
    keys = kv_ref.shape[0] * kv_ref.shape[2]
    slab, along_y, along_x = place_ref[0], place_ref[1], place_ref[2]

    def step(s, carry, masked):
        highest, norm, weighted = carry
        scores = product_of_rows(keys_of(kv_ref, s, 0), q_rows[...]) * (SCALE * math.log2(math.e))
        if masked:
            key = lax.broadcasted_iota(jnp.int32, (keys, ROWS), 0)
            if of_peer:
                last = (along_y + 1 - along_x) * tokens - 1
            else:
                token = lax.rem(lax.broadcasted_iota(jnp.int32, (keys, ROWS), 1), jnp.int32(tokens))
                last = along_y * tokens + token
            scores = jnp.where(key <= last, scores, LOWEST)
        higher = jnp.maximum(highest, jnp.max(scores, axis=0, keepdims=True))
        weight = jnp.exp2(scores - higher)
        factor = jnp.exp2(highest - higher)
        slope = product_of_rows(keys_of(kv_ref, s, 1), do_rows[...])
        weights_ref[s] = weight.astype(BF16)
        slopes_ref[s] = slope
        maxima_ref[pl.ds(s, 1), :] = higher
        norm = norm * factor + jnp.sum(weight, axis=0, keepdims=True)
        weighted = weighted * factor + jnp.sum(weight * slope, axis=0, keepdims=True)
        return higher, norm, weighted

    zeros = jnp.zeros((1, ROWS), F32)
    carry = lax.fori_loop(
        0, slab, functools.partial(step, masked=False), (jnp.full((1, ROWS), LOWEST, F32), zeros, zeros)
    )
    width = stats_ref.shape[1]
    for i, row in enumerate(step(slab, carry, True)):
        for j in range(ROWS // width):
            at = 8 * i + of_peer * (ROWS // width) + j
            stats_ref[at : at + 1, :] = row[:, j * width : (j + 1) * width]


def gradients_kernel(
    place_ref, own_q, own_do, peer_q, peer_do, kv_ref, stats_ref, other_ref,
    own_maxima, own_weights, own_slopes, peer_maxima, peer_weights, peer_slopes,
    dq_ref, dq_peer_ref, dkv_ref,
    there_q, there_do, k_cols, total,
):
    tokens, width = peer_q.shape
    heads = width // HEAD_SIZE
    along_y = kv_ref.shape[0]
    slab = place_ref[0]
    rows_kernel(peer_q, peer_do, there_q, there_do)

    @pl.loop(0, slab + 1)
    def _(s):
        k_cols[s] = keys_of(kv_ref, s, 0).T

    for owner in range(PAIR):
        q_rows, do_rows = (there_q, there_do) if owner else (own_q, own_do)
        maxima = peer_maxima if owner else own_maxima
        weights = peer_weights if owner else own_weights
        slopes = peer_slopes if owner else own_slopes
        here_highest, there_highest = row_of(stats_ref, 0, owner), row_of(other_ref, 0, 1 - owner)
        highest = jnp.maximum(here_highest, there_highest)
        here_factor, there_factor = jnp.exp2(here_highest - highest), jnp.exp2(there_highest - highest)
        inverse = 1.0 / (row_of(stats_ref, 1, owner) * here_factor + row_of(other_ref, 1, 1 - owner) * there_factor)
        centre = row_of(stats_ref, 2, owner) * here_factor + row_of(other_ref, 2, 1 - owner) * there_factor
        centre = centre * inverse

        def step(s, dq_cols):
            factor = jnp.exp2(maxima[pl.ds(s, 1), :] - highest) * inverse
            soft = weights[s].astype(F32) * factor
            score_grad = (soft * (slopes[s] - centre)).astype(BF16)
            dk = product(score_grad, q_rows[...])
            dv = product(soft.astype(BF16), do_rows[...])
            if owner == 0:
                total[s, :, 0:HEAD_SIZE] = dk
                total[s, :, HEAD_SIZE:] = dv
            else:
                total[s, :, 0:HEAD_SIZE] += dk
                total[s, :, HEAD_SIZE:] += dv
            return dq_cols + product(k_cols[s], score_grad)

        dq_cols = lax.fori_loop(0, slab + 1, step, jnp.zeros((HEAD_SIZE, ROWS), F32)) * SCALE
        out = dq_peer_ref if owner else dq_ref
        for h in range(heads):
            part = dq_cols[:, h * tokens : (h + 1) * tokens].T
            out[:, h * HEAD_SIZE : (h + 1) * HEAD_SIZE] = part.astype(out.dtype)

    @pl.loop(0, SLABS)
    def _(s):
        @pl.when(s <= slab)
        def _():
            dk = (total[s, :, 0:HEAD_SIZE] * SCALE).astype(BF16)
            dv = total[s, :, HEAD_SIZE:].astype(BF16)
            dkv_ref[:, s, :, 0:HEAD_SIZE] = dk.reshape(along_y, tokens, HEAD_SIZE)
            dkv_ref[:, s, :, HEAD_SIZE:] = dv.reshape(along_y, tokens, HEAD_SIZE)

        @pl.when(s > slab)
        def _():
            dkv_ref[:, s] = jnp.zeros((along_y, tokens, 2 * HEAD_SIZE), BF16)


def pack_kernel(key_ref, value_ref, out_ref):
    for h in range(out_ref.shape[0]):
        across = slice(h * HEAD_SIZE, (h + 1) * HEAD_SIZE)
        out_ref[h, :, 0:HEAD_SIZE] = key_ref[:, across]
        out_ref[h, :, HEAD_SIZE:] = value_ref[:, across]


def unpack_kernel(both_ref, key_ref, value_ref, sems):
    copies = [
        pltpu.make_async_copy(
            both_ref.at[h, :, i * HEAD_SIZE : (i + 1) * HEAD_SIZE],
            ref.at[:, h * HEAD_SIZE : (h + 1) * HEAD_SIZE],
            sems.at[i, h],
        )
        for i, ref in enumerate((key_ref, value_ref))
        for h in range(both_ref.shape[0])
    ]
    for copy in copies:
        copy.start()
    for copy in copies:
        copy.wait()


def sum_kernel(parts_ref, out_ref):
    total = parts_ref[0].astype(F32)
    for i in range(1, parts_ref.shape[0]):
        total += parts_ref[i].astype(F32)
    out_ref[...] = total.astype(out_ref.dtype)


WHOLE = pl.BlockSpec(memory_space=pltpu.VMEM)
IN_HBM = pl.BlockSpec(memory_space=pltpu.HBM)


def small(kernel, name, out, in_specs, out_specs, scratch, room, *args):
    moved = sum(a.size * a.dtype.itemsize for a in args)
    return pl.pallas_call(
        kernel,
        out_shape=out,
        in_specs=in_specs,
        out_specs=out_specs,
        scratch_shapes=scratch,
        compiler_params=pltpu.CompilerParams(vmem_limit_bytes=room * 2**20),
        cost_estimate=pl.CostEstimate(flops=0, bytes_accessed=2 * moved, transcendentals=0),
        name=name,
    )(*args)


def summed(parts, dtype):
    shape = jax.ShapeDtypeStruct(parts.shape[1:], dtype)
    return small(sum_kernel, "sum_of_parts", shape, [WHOLE], WHOLE, [], 4, parts)
SCALARS = pl.BlockSpec(memory_space=pltpu.SMEM)


def row_statistics(of_peer, place, q, do, kv, *own_stats):
    keys = kv.shape[0] * kv.shape[2]
    return pl.pallas_call(
        functools.partial(statistics_kernel, of_peer),
        out_shape=(
            jax.ShapeDtypeStruct((24, PAIR * ROWS // 8), F32),
            jax.ShapeDtypeStruct((8, ROWS), F32),
            jax.ShapeDtypeStruct((SLABS, keys, ROWS), BF16),
            jax.ShapeDtypeStruct((SLABS, keys, ROWS), F32),
        ),
        in_specs=[SCALARS] + [WHOLE] * (3 + len(own_stats)),
        out_specs=(WHOLE,) * 4,
        scratch_shapes=[pltpu.VMEM((ROWS, HEAD_SIZE), BF16)] * 2 if of_peer else [],
        compiler_params=pltpu.CompilerParams(vmem_limit_bytes=12 * 2**20),
        cost_estimate=pl.CostEstimate(
            flops=4 * ROWS * SLABS * keys * HEAD_SIZE, bytes_accessed=2**20, transcendentals=ROWS * SLABS * keys
        ),
        name="row_statistics",
    )(place, q, do, kv, *own_stats)


def attention_gradients(place, *args):
    q, kv = args[2], args[4]
    keys = kv.shape[0] * kv.shape[2]
    return pl.pallas_call(
        gradients_kernel,
        out_shape=(
            jax.ShapeDtypeStruct(q.shape, F32),
            jax.ShapeDtypeStruct(q.shape, BF16),
            jax.ShapeDtypeStruct(kv.shape, BF16),
        ),
        in_specs=[SCALARS] + [WHOLE] * len(args),
        out_specs=(WHOLE, WHOLE, WHOLE),
        scratch_shapes=[
            pltpu.VMEM((ROWS, HEAD_SIZE), BF16),
            pltpu.VMEM((ROWS, HEAD_SIZE), BF16),
            pltpu.VMEM((SLABS, HEAD_SIZE, keys), BF16),
            pltpu.VMEM((SLABS, keys, 2 * HEAD_SIZE), F32),
        ],
        compiler_params=pltpu.CompilerParams(vmem_limit_bytes=18 * 2**20),
        cost_estimate=pl.CostEstimate(
            flops=12 * ROWS * SLABS * keys * HEAD_SIZE, bytes_accessed=4 * 2**20, transcendentals=ROWS
        ),
        name="attention_gradients",
    )(place, *args)


def line_lists(ctx_count, tp_count, along_z):
    span = ctx_count // GROUPS
    plane = span // SLABS
    lists = []
    for t in range(tp_count):
        first = span // 2 if t >= tp_count // 2 and along_z else 0
        for g in range(GROUPS):
            if along_z:
                lines = [[first + g * span + s * plane + p for s in range(SLABS)] for p in range(plane)]
            else:
                lines = [
                    [g * span + s * plane + y * PAIR + x for y in range(plane // PAIR)]
                    for s in range(SLABS)
                    for x in range(PAIR)
                ]
            lists += [[c % ctx_count * tp_count + t for c in line] for line in lines]
    return lists


def exchange(parts, lists):
    return lax.all_to_all(parts, AXES, 0, 0, axis_index_groups=lists, tiled=True)


def to_peer(array):
    return lax.ppermute(array, "ctx", [(c, c ^ 1) for c in range(lax.axis_size("ctx"))])


def shards(query_heads, key_heads_wide, value_heads_wide, grad_output):
    ctx_count = lax.axis_size("ctx")
    tp_count = lax.axis_size("tp")
    span = ctx_count // GROUPS
    plane = span // SLABS
    lines = plane // PAIR
    here = key_heads_wide.shape[0]
    rows = query_heads.shape[0]
    along_z = line_lists(ctx_count, tp_count, True)
    along_y = line_lists(ctx_count, tp_count, False)
    offset = jnp.where(lax.axis_index("tp") >= tp_count // 2, span // 2, 0)
    rank = (jnp.mod(lax.axis_index("ctx") - offset, ctx_count) % span).astype(jnp.int32)
    place = jnp.stack([rank // plane, rank % plane // PAIR, rank % PAIR])

    peer_q, peer_do = to_peer(query_heads), to_peer(grad_output)
    shape = jax.ShapeDtypeStruct((ROWS, HEAD_SIZE), BF16)
    own_q, own_do = small(
        rows_kernel, "queries_by_head", (shape, shape), [WHOLE] * 2, (WHOLE, WHOLE), [], 4, query_heads, grad_output
    )
    both = small(
        pack_kernel, "keys_and_values_by_head", jax.ShapeDtypeStruct((tp_count, here, 2 * HEAD_SIZE), BF16),
        [WHOLE, WHOLE], WHOLE, [], 4, key_heads_wide, value_heads_wide,
    )
    own = lax.all_to_all(both, "tp", 0, 0, tiled=True).reshape(rows, 2 * HEAD_SIZE)
    column = exchange(jnp.broadcast_to(own, (SLABS,) + own.shape), along_z)
    kv = exchange(jnp.broadcast_to(column, (lines,) + column.shape), along_y)
    own_stats, *own_held = row_statistics(False, place, own_q, own_do, kv)
    stats, *peer_held = row_statistics(True, place, peer_q, peer_do, kv, own_stats)
    dq, dq_peer, dkv = attention_gradients(
        place, own_q, own_do, peer_q, peer_do, kv, stats, to_peer(stats), *own_held, *peer_held
    )
    grad_query = dq + to_peer(dq_peer).astype(F32)
    partial = summed(exchange(dkv, along_y), BF16)
    mine = summed(exchange(partial, along_z), F32)
    back = lax.all_to_all(mine.reshape(tp_count, here, 2 * HEAD_SIZE), "tp", 0, 0, tiled=True)
    shape = jax.ShapeDtypeStruct(key_heads_wide.shape, F32)
    key_gradient, value_gradient = small(
        unpack_kernel, "gradients_by_token", (shape, shape), [WHOLE], (IN_HBM, IN_HBM),
        [pltpu.SemaphoreType.DMA((2, tp_count))], 4, back
    )
    return grad_query, key_gradient, value_gradient


def solution(mesh):
    return jax.shard_map(
        shards,
        mesh=mesh,
        in_specs=(P("ctx", "tp"), P(AXES, None), P(AXES, None), P("ctx", "tp")),
        out_specs=(P("ctx", "tp"), P(AXES, None), P(AXES, None)),
        check_vma=False,
    )
```

time: 118 us -> 109 us (0.924)
  waiting for transfers between devices: 22.8 us -> 11.7 us
  starting transfers between devices: 41.9 us -> 45.7 us
  other arithmetic: 3.73 us -> 0.93 us
  Pallas kernels: 6.78 us -> 8.75 us
    ppermute x3 -> x4, waiting for transfers between devices: 16.6 us -> 2.1 us  [to_peer(): lax.ppermute(array, 'ctx', [(c, c ^ 1) for c in range(lax.axis_size('ctx'...]
    ppermute x3 -> x4, starting transfers between devices: 5.97 us -> 13.3 us  [to_peer(): lax.ppermute(array, 'ctx', [(c, c ^ 1) for c in range(lax.axis_size('ctx'...]
    all_to_all x2, waiting for transfers between devices: 3.51 us -> 6.83 us  [exchange(): lax.all_to_all(parts, AXES, 0, 0, axis_index_groups=lists, tiled=True)]
    all_to_all x2, starting transfers between devices: 24.1 us -> 21.2 us  [exchange(): lax.all_to_all(parts, AXES, 0, 0, axis_index_groups=lists, tiled=True)]
    pallas_call x1 -> x7, Pallas kernels: 3.05 us -> 5.43 us  [the longest x2 3.08 us: row_statistics(): pl.pallas_call(functools.partial(statistics_kernel, of_peer), out_shape=(...]
    another operation x4 -> x0, local copies, waits for them, and re-layouts: 1.65 us -> none  [shards(): jnp.stack([a.reshape(here, tp_count, HEAD_SIZE) for a in (key_heads_wide,...]
    reduce_sum x2 -> x0, other arithmetic: 1.58 us -> none  [the longest x1 0.91 us: shards(): partial = jnp.sum(exchange(dkv, along_y).astype(F32), axis=0).astype(BF16)]
    unnamed x4 -> x8, local copies, waits for them, and re-layouts: 1.9 us -> 3.4 us
  transfers between devices with their start and end apart: 6 -> 7, of which waited for: 4 -> 5; matrix products, arithmetic and copies ran while one was open for 2% -> 1% of each run, Pallas kernels for 0% -> 2%
where the time goes in v3:
time: 109 us; the launch traced here: 108 us
  starting transfers between devices  45.7 us (42%)
  blocking collectives  35.4 us (32%)
  waiting for transfers between devices  11.7 us (11%)
  Pallas kernels  8.75 us (8%)
  local copies, waits for them, and re-layouts  4.51 us (4%)
    all_to_all x2, blocking collectives, exchange(): lax.all_to_all(parts, AXES, 0, 0, axis_index_groups=lists, tiled=True)  22.9 us
    all_to_all x2, starting transfers between devices, exchange(): lax.all_to_all(parts, AXES, 0, 0, axis_index_groups=lists, tiled=True)  21.2 us
    ppermute x4, starting transfers between devices, to_peer(): lax.ppermute(array, 'ctx', [(c, c ^ 1) for c in range(lax.axis_size('ctx'...  13.3 us
    all_to_all x1, blocking collectives, shards(): lax.all_to_all(both, 'tp', 0, 0, tiled=True).reshape(rows, 2 * HEAD_SIZE)  12.5 us
    all_to_all x1, starting transfers between devices, shards(): lax.all_to_all(mine.reshape(tp_count, here, 2 * HEAD_SIZE), 'tp', 0, 0, t...  11.2 us
    all_to_all x2, waiting for transfers between devices, exchange(): lax.all_to_all(parts, AXES, 0, 0, axis_index_groups=lists, tiled=True)  6.83 us
    unnamed x8, local copies, waits for them, and re-layouts  3.4 us
    pallas_call x1, Pallas kernels, attention_gradients(): pl.pallas_call(gradients_kernel, out_shape=(jax.ShapeDtypeStruct(q.shape,...  3.31 us
  transfers between devices with their start and end apart: 7, of which 5 were waited for; matrix products, arithmetic and copies ran while one was open for 1% of the time, Pallas kernels for 2%

profile of v3, /device:TPU:1, one launch (start us, length us, event | category | flops | bytes accessed | tf_op | source)
XLA Modules:
  0.0 107.8 jit_solution(5117048317594009049)
XLA Ops:
  0.6 0.0 copy-start.2
  0.6 0.7 copy-done.2
  1.4 0.0 copy-start.3
  1.4 0.8 copy-done.3
  2.2 12.5 %all_to_all.30 = bf16[4,32,256]{2,1,0:T(8,128)(2,1)S(1)} all-to-all(bf16[4,32,256]{2,1,0:T(8,128)(2,1)S(1)} %keys_and_values_by_head.1), channel_id=1, replica_groups=mesh['ctx'=128,'tp'=4] {'tp'}, dimensions={0} | all-to-all | bytes 131072 | tf_op jit(solution)/shard_map/all_to_all | solution.py:309
  14.7 9.5 %all_to_all.31 = bf16[4,128,256]{2,1,0:T(8,128)(2,1)S(1)} all-to-all(bf16[4,128,256]{2,1,0:T(8,128)(2,1)S(1)} %broadcast_in_dim.6), channel_id=1, replica_groups={{0,32,64,96},{4,36,68,100},{8,40,72,104},{12,44,76,108},{16,48,80,112},..., dimensions={0} | all-to-all | bytes 524288 | tf_op jit(solution)/shard_map/all_to_all | solution.py:279
  24.2 1.1 %broadcast_in_dim.7 = bf16[4,4,128,256]{3,2,1,0:T(8,128)(2,1)} broadcast(bf16[4,128,256]{2,1,0:T(8,128)(2,1)S(1)} %all_to_all.31), dimensions={1,2,3} | broadcast | bytes 1310720 | tf_op jit(solution)/shard_map/broadcast_in_dim | solution.py:311
  25.3 3.5 %all-to-all-start.2 = ((bf16[4,4,128,256]{3,2,1,0:T(8,128)(2,1)}), bf16[4,4,128,256]{3,2,1,0:T(8,128)(2,1)S(1)}, u32[]{:S(2)}, u32[]{:S(2)}) async-start(bf16[4,4,128,256]{3,2,1,0:T(8,128)(2,1)} %broadcast_in_dim.7), calls=%async_computation.2 | async-start | bytes 2097152 | tf_op jit(solution)/shard_map/all_to_all | solution.py:279
  28.8 1.9 %collective-permute-start = (bf16[128,1024]{1,0:T(8,128)(2,1)}, bf16[128,1024]{1,0:T(8,128)(2,1)S(1)}, u32[]{:S(2)}, u32[]{:S(2)}) collective-permute-start(bf16[128,1024]{1,0:T(8,128)(2,1)} %q_ref.1), channel_id=1, source_target_pairs={{0,4},{4,0},{8,12},{12,8},{16,20},{20,16},{24,28},{28,24},{32,36},... | collective-permute-start | bytes 786440 | tf_op jit(solution)/shard_map/ppermute | solution.py:283
  30.7 4.9 %collective-permute-start.1 = (bf16[128,1024]{1,0:T(8,128)(2,1)}, bf16[128,1024]{1,0:T(8,128)(2,1)S(1)}, u32[]{:S(2)}, u32[]{:S(2)}) collective-permute-start(bf16[128,1024]{1,0:T(8,128)(2,1)} %do_ref.1), channel_id=1, source_target_pairs={{0,4},{4,0},{8,12},{12,8},{16,20},{20,16},{24,28},{28,24},{32,36},... | collective-permute-start | bytes 786440 | tf_op jit(solution)/shard_map/ppermute | solution.py:283
  35.7 0.0 copy-start
  35.7 0.9 copy-done
  36.6 0.0 copy-start.1
  36.6 0.9 copy-done.1
  37.6 0.1 queries_by_head.1
  37.7 0.1 pad_add_fusion.place_ref
  37.8 3.3 %all-to-all-done.2.refs_2_.kv_ref = bf16[4,4,128,256]{3,2,1,0:T(8,128)(2,1)S(1)} async-done(((bf16[4,4,128,256]{3,2,1,0:T(8,128)(2,1)}), bf16[4,4,128,256]{3,2,1,0:T(8,128)(2,1)S(1)}, u32[]{:S(2)}, u32[]{:S(2)}) %all-to-all-start.2) | async-done | bytes 1048608 | tf_op jit(solution)/shard_map/all_to_all | solution.py:279
  41.1 1.6 %row_statistics.2 = (f32[24,256]{1,0:T(8,128)S(1)}, f32[8,1024]{1,0:T(8,128)S(1)}, bf16[4,512,1024]{2,1,0:T(8,128)(2,1)S(1)}, f32[4,512,1024]{2,1,0:T(8,128)S(1)}) custom-call(s32[3]{0:T(128)S(1)} %pad_add_fusion.place_ref, bf16[1024,128]{1,0:T(8,128)(2,1)S(1)} %get-tuple-element.18.refs_0_.own_q, bf16[1024,128]{1,0:T(8,128)(2,1)S(1)} %get-tuple-element.19.refs_1_.own_do, ...), custom_call_target="tpu_custom_call" | custom-call | flops 1073741824 | bytes 1048576 | tf_op jit(solution)/shard_map/row_statistics/pallas_call | solution.py:214
  42.7 0.0 collective-permute-done.refs_0_.peer_q
  42.7 0.4 collective-permute-done.1.refs_1_.peer_do
  43.1 1.5 %row_statistics.3 = (f32[24,256]{1,0:T(8,128)S(1)}, f32[8,1024]{1,0:T(8,128)S(1)}, bf16[4,512,1024]{2,1,0:T(8,128)(2,1)S(1)}, f32[4,512,1024]{2,1,0:T(8,128)S(1)}) custom-call(s32[3]{0:T(128)S(1)} %pad_add_fusion.place_ref, bf16[128,1024]{1,0:T(8,128)(2,1)S(1)} %collective-permute-done.refs_0_.peer_q, ...), custom_call_target="tpu_custom_call" | custom-call | flops 1073741824 | bytes 1048576 | tf_op jit(solution)/shard_map/row_statistics/pallas_call | solution.py:214
  44.6 4.3 %collective-permute-start.2 = (f32[24,256]{1,0:T(8,128)S(1)}, f32[24,256]{1,0:T(8,128)S(1)}, u32[]{:S(2)}, u32[]{:S(2)}) collective-permute-start(f32[24,256]{1,0:T(8,128)S(1)} %get-tuple-element.21.stats_ref), channel_id=1, source_target_pairs={{0,4},{4,0},{8,12},{12,8},{16,20},{20,16},{24,28},{28,24},{32,36},... | collective-permute-start | bytes 73736 | tf_op jit(solution)/shard_map/ppermute | solution.py:283
  49.0 1.7 %collective-permute-done.2.other_ref = f32[24,256]{1,0:T(8,128)S(1)} collective-permute-done((f32[24,256]{1,0:T(8,128)S(1)}, f32[24,256]{1,0:T(8,128)S(1)}, u32[]{:S(2)}, u32[]{:S(2)}) %collective-permute-start.2) | collective-permute-done | bytes 24608 | tf_op jit(solution)/shard_map/ppermute | solution.py:283
  50.7 3.3 %attention_gradients.1 = (f32[128,1024]{1,0:T(8,128)S(1)}, bf16[128,1024]{1,0:T(8,128)(2,1)S(1)}, bf16[4,4,128,256]{3,2,1,0:T(8,128)(2,1)S(1)}) custom-call(s32[3]{0:T(128)S(1)} %pad_add_fusion.place_ref, bf16[1024,128]{1,0:T(8,128)(2,1)S(1)} %get-tuple-element.18.refs_0_.own_q, bf16[1024,128]{1,0:T(8,128)(2,1)S(1)} %get-tuple-element.19.refs_1_.own_do, ...), custom_call_target="tpu_custom_call" | custom-call | flops 3221225472 | bytes 4194304 | tf_op jit(solution)/shard_map/attention_gradients/pallas_call | solution.py:236
  54.0 13.5 %all_to_all.32.parts_ref = bf16[4,4,128,256]{3,2,1,0:T(8,128)(2,1)S(1)} all-to-all(bf16[4,4,128,256]{3,2,1,0:T(8,128)(2,1)S(1)} %get-tuple-element.30), channel_id=1, replica_groups={{0,8,16,24},{4,12,20,28},{32,40,48,56},{36,44,52,60},{64,72,80,88},{68,..., dimensions={0} | all-to-all | bytes 2097152 | tf_op jit(solution)/shard_map/all_to_all | solution.py:279
  67.5 0.8 sum_of_parts.2
  68.3 17.7 %all-to-all-start.4 = ((bf16[4,128,256]{2,1,0:T(8,128)(2,1)}), bf16[4,128,256]{2,1,0:T(8,128)(2,1)S(1)}, u32[]{:S(2)}, u32[]{:S(2)}) async-start(bf16[4,128,256]{2,1,0:T(8,128)(2,1)} %sum_of_parts.2), calls=%async_computation.4 | async-start | bytes 524288 | tf_op jit(solution)/shard_map/all_to_all | solution.py:279
  85.9 2.1 %collective-permute-start.3 = (bf16[128,1024]{1,0:T(8,128)(2,1)S(1)}, bf16[128,1024]{1,0:T(8,128)(2,1)S(1)}, u32[]{:S(2)}, u32[]{:S(2)}) collective-permute-start(bf16[128,1024]{1,0:T(8,128)(2,1)S(1)} %get-tuple-element.29), channel_id=1, source_target_pairs={{0,4},{4,0},{8,12},{12,8},{16,20},{20,16},{24,28},{28,24},{32,36},... | collective-permute-start | bytes 786440 | tf_op jit(solution)/shard_map/ppermute | solution.py:283
  88.1 3.5 %all-to-all-done.4.parts_ref = bf16[4,128,256]{2,1,0:T(8,128)(2,1)S(1)} async-done(((bf16[4,128,256]{2,1,0:T(8,128)(2,1)}), bf16[4,128,256]{2,1,0:T(8,128)(2,1)S(1)}, u32[]{:S(2)}, u32[]{:S(2)}) %all-to-all-start.4) | async-done | bytes 262176 | tf_op jit(solution)/shard_map/all_to_all | solution.py:279
  91.6 0.7 sum_of_parts.3
  92.3 11.2 %all-to-all-start.5 = ((f32[4,32,256]{2,1,0:T(8,128)}), f32[4,32,256]{2,1,0:T(8,128)S(1)}, u32[]{:S(2)}, u32[]{:S(2)}) async-start(f32[4,32,256]{2,1,0:T(8,128)} %bitcast.4), calls=%async_computation.5 | async-start | bytes 262144 | tf_op jit(solution)/shard_map/all_to_all | solution.py:320
  103.5 0.0 collective-permute-done.3
  103.5 0.8 convert_add_fusion
  104.4 2.7 %all-to-all-done.5.both_ref = f32[4,32,256]{2,1,0:T(8,128)S(1)} async-done(((f32[4,32,256]{2,1,0:T(8,128)}), f32[4,32,256]{2,1,0:T(8,128)S(1)}, u32[]{:S(2)}, u32[]{:S(2)}) %all-to-all-start.5) | async-done | bytes 131104 | tf_op jit(solution)/shard_map/all_to_all | solution.py:320
  107.1 0.7 gradients_by_token.1
  (2 shorter events, 0.0 us)
Async XLA Ops:
  0.6 0.8 copy-start.2
  1.4 0.8 copy-start.3
  25.3 15.9 %all-to-all-start.2 = ((bf16[4,4,128,256]{3,2,1,0:T(8,128)(2,1)}), bf16[4,4,128,256]{3,2,1,0:T(8,128)(2,1)S(1)}, u32[]{:S(2)}, u32[]{:S(2)}) async-start(bf16[4,4,128,256]{3,2,1,0:T(8,128)(2,1)} %broadcast_in_dim.7), calls=%async_computation.2 | async-start | bytes 2097152 | tf_op jit(solution)/shard_map/all_to_all | solution.py:279
  28.8 13.9 %collective-permute-start = (bf16[128,1024]{1,0:T(8,128)(2,1)}, bf16[128,1024]{1,0:T(8,128)(2,1)S(1)}, u32[]{:S(2)}, u32[]{:S(2)}) collective-permute-start(bf16[128,1024]{1,0:T(8,128)(2,1)} %q_ref.1), channel_id=1, source_target_pairs={{0,4},{4,0},{8,12},{12,8},{16,20},{20,16},{24,28},{28,24},{32,36},... | collective-permute-start | bytes 786440 | tf_op jit(solution)/shard_map/ppermute | solution.py:283
  30.7 12.4 %collective-permute-start.1 = (bf16[128,1024]{1,0:T(8,128)(2,1)}, bf16[128,1024]{1,0:T(8,128)(2,1)S(1)}, u32[]{:S(2)}, u32[]{:S(2)}) collective-permute-start(bf16[128,1024]{1,0:T(8,128)(2,1)} %do_ref.1), channel_id=1, source_target_pairs={{0,4},{4,0},{8,12},{12,8},{16,20},{20,16},{24,28},{28,24},{32,36},... | collective-permute-start | bytes 786440 | tf_op jit(solution)/shard_map/ppermute | solution.py:283
  35.7 1.0 copy-start
  36.6 0.9 copy-start.1
  44.6 6.1 %collective-permute-start.2 = (f32[24,256]{1,0:T(8,128)S(1)}, f32[24,256]{1,0:T(8,128)S(1)}, u32[]{:S(2)}, u32[]{:S(2)}) collective-permute-start(f32[24,256]{1,0:T(8,128)S(1)} %get-tuple-element.21.stats_ref), channel_id=1, source_target_pairs={{0,4},{4,0},{8,12},{12,8},{16,20},{20,16},{24,28},{28,24},{32,36},... | collective-permute-start | bytes 73736 | tf_op jit(solution)/shard_map/ppermute | solution.py:283
  68.3 23.3 %all-to-all-start.4 = ((bf16[4,128,256]{2,1,0:T(8,128)(2,1)}), bf16[4,128,256]{2,1,0:T(8,128)(2,1)S(1)}, u32[]{:S(2)}, u32[]{:S(2)}) async-start(bf16[4,128,256]{2,1,0:T(8,128)(2,1)} %sum_of_parts.2), calls=%async_computation.4 | async-start | bytes 524288 | tf_op jit(solution)/shard_map/all_to_all | solution.py:279
  85.9 17.6 %collective-permute-start.3 = (bf16[128,1024]{1,0:T(8,128)(2,1)S(1)}, bf16[128,1024]{1,0:T(8,128)(2,1)S(1)}, u32[]{:S(2)}, u32[]{:S(2)}) collective-permute-start(bf16[128,1024]{1,0:T(8,128)(2,1)S(1)} %get-tuple-element.29), channel_id=1, source_target_pairs={{0,4},{4,0},{8,12},{12,8},{16,20},{20,16},{24,28},{28,24},{32,36},... | collective-permute-start | bytes 786440 | tf_op jit(solution)/shard_map/ppermute | solution.py:283
  92.3 14.8 %all-to-all-start.5 = ((f32[4,32,256]{2,1,0:T(8,128)}), f32[4,32,256]{2,1,0:T(8,128)S(1)}, u32[]{:S(2)}, u32[]{:S(2)}) async-start(f32[4,32,256]{2,1,0:T(8,128)} %bitcast.4), calls=%async_computation.5 | async-start | bytes 262144 | tf_op jit(solution)/shard_map/all_to_all | solution.py:320

commit v4 on v3

--- a/solution.py
+++ b/solution.py
@@ -82,22 +82,33 @@
         weighted = weighted * factor + jnp.sum(weight * slope, axis=0, keepdims=True)
         return higher, norm, weighted
 
+    def finish(carry):
+        width = stats_ref.shape[1]
+        for i, row in enumerate(step(slab, carry, True)):
+            for j in range(ROWS // width):
+                at = 8 * i + of_peer * (ROWS // width) + j
+                stats_ref[at : at + 1, :] = row[:, j * width : (j + 1) * width]
+
     zeros = jnp.zeros((1, ROWS), F32)
-    carry = lax.fori_loop(
-        0, slab, functools.partial(step, masked=False), (jnp.full((1, ROWS), LOWEST, F32), zeros, zeros)
-    )
-    width = stats_ref.shape[1]
-    for i, row in enumerate(step(slab, carry, True)):
-        for j in range(ROWS // width):
-            at = 8 * i + of_peer * (ROWS // width) + j
-            stats_ref[at : at + 1, :] = row[:, j * width : (j + 1) * width]
+    start = (jnp.full((1, ROWS), LOWEST, F32), zeros, zeros)
+
+    @pl.when(slab == SLABS - 1)
+    def _():
+        carry = start
+        for s in range(SLABS - 1):
+            carry = step(s, carry, False)
+        finish(carry)
+
+    @pl.when(slab < SLABS - 1)
+    def _():
+        finish(lax.fori_loop(0, slab, functools.partial(step, masked=False), start))
 
 
 def gradients_kernel(
     place_ref, own_q, own_do, peer_q, peer_do, kv_ref, stats_ref, other_ref,
     own_maxima, own_weights, own_slopes, peer_maxima, peer_weights, peer_slopes,
     dq_ref, dq_peer_ref, dkv_ref,
-    there_q, there_do, k_cols, total,
+    there_q, there_do,
 ):
     tokens, width = peer_q.shape
     heads = width // HEAD_SIZE
@@ -105,53 +116,55 @@
     slab = place_ref[0]
     rows_kernel(peer_q, peer_do, there_q, there_do)
 
-    @pl.loop(0, slab + 1)
-    def _(s):
-        k_cols[s] = keys_of(kv_ref, s, 0).T
-
+    rows = ((own_q, own_do), (there_q, there_do))
+    held = ((own_maxima, own_weights, own_slopes), (peer_maxima, peer_weights, peer_slopes))
+    norms = []
     for owner in range(PAIR):
-        q_rows, do_rows = (there_q, there_do) if owner else (own_q, own_do)
-        maxima = peer_maxima if owner else own_maxima
-        weights = peer_weights if owner else own_weights
-        slopes = peer_slopes if owner else own_slopes
         here_highest, there_highest = row_of(stats_ref, 0, owner), row_of(other_ref, 0, 1 - owner)
         highest = jnp.maximum(here_highest, there_highest)
         here_factor, there_factor = jnp.exp2(here_highest - highest), jnp.exp2(there_highest - highest)
         inverse = 1.0 / (row_of(stats_ref, 1, owner) * here_factor + row_of(other_ref, 1, 1 - owner) * there_factor)
         centre = row_of(stats_ref, 2, owner) * here_factor + row_of(other_ref, 2, 1 - owner) * there_factor
-        centre = centre * inverse
-
-        def step(s, dq_cols):
+        norms.append((highest, inverse, centre * inverse))
+
+    def step(s, dq_cols):
+        k_cols = keys_of(kv_ref, s, 0).T
+        dk = dv = 0.0
+        added = []
+        for owner in range(PAIR):
+            (q_rows, do_rows), (maxima, weights, slopes) = rows[owner], held[owner]
+            highest, inverse, centre = norms[owner]
             factor = jnp.exp2(maxima[pl.ds(s, 1), :] - highest) * inverse
             soft = weights[s].astype(F32) * factor
             score_grad = (soft * (slopes[s] - centre)).astype(BF16)
-            dk = product(score_grad, q_rows[...])
-            dv = product(soft.astype(BF16), do_rows[...])
-            if owner == 0:
-                total[s, :, 0:HEAD_SIZE] = dk
-                total[s, :, HEAD_SIZE:] = dv
-            else:
-                total[s, :, 0:HEAD_SIZE] += dk
-                total[s, :, HEAD_SIZE:] += dv
-            return dq_cols + product(k_cols[s], score_grad)
-
-        dq_cols = lax.fori_loop(0, slab + 1, step, jnp.zeros((HEAD_SIZE, ROWS), F32)) * SCALE
-        out = dq_peer_ref if owner else dq_ref
-        for h in range(heads):
-            part = dq_cols[:, h * tokens : (h + 1) * tokens].T
-            out[:, h * HEAD_SIZE : (h + 1) * HEAD_SIZE] = part.astype(out.dtype)
-
-    @pl.loop(0, SLABS)
-    def _(s):
-        @pl.when(s <= slab)
-        def _():
-            dk = (total[s, :, 0:HEAD_SIZE] * SCALE).astype(BF16)
-            dv = total[s, :, HEAD_SIZE:].astype(BF16)
-            dkv_ref[:, s, :, 0:HEAD_SIZE] = dk.reshape(along_y, tokens, HEAD_SIZE)
-            dkv_ref[:, s, :, HEAD_SIZE:] = dv.reshape(along_y, tokens, HEAD_SIZE)
-
-        @pl.when(s > slab)
-        def _():
+            dk += product(score_grad, q_rows[...])
+            dv += product(soft.astype(BF16), do_rows[...])
+            added.append(dq_cols[owner] + product(k_cols, score_grad))
+        dkv_ref[:, s, :, 0:HEAD_SIZE] = (dk * SCALE).astype(BF16).reshape(along_y, tokens, HEAD_SIZE)
+        dkv_ref[:, s, :, HEAD_SIZE:] = dv.astype(BF16).reshape(along_y, tokens, HEAD_SIZE)
+        return tuple(added)
+
+    def finish(dq_cols):
+        for cols, out in zip(dq_cols, (dq_ref, dq_peer_ref)):
+            for h in range(heads):
+                part = cols[:, h * tokens : (h + 1) * tokens].T * SCALE
+                out[:, h * HEAD_SIZE : (h + 1) * HEAD_SIZE] = part.astype(out.dtype)
+
+    start = (jnp.zeros((HEAD_SIZE, ROWS), F32),) * PAIR
+
+    @pl.when(slab == SLABS - 1)
+    def _():
+        dq_cols = start
+        for s in range(SLABS):
+            dq_cols = step(s, dq_cols)
+        finish(dq_cols)
+
+    @pl.when(slab < SLABS - 1)
+    def _():
+        finish(lax.fori_loop(0, slab + 1, step, start))
+
+        @pl.loop(slab + 1, SLABS)
+        def _(s):
             dkv_ref[:, s] = jnp.zeros((along_y, tokens, 2 * HEAD_SIZE), BF16)
 
 
@@ -245,8 +258,6 @@
         scratch_shapes=[
             pltpu.VMEM((ROWS, HEAD_SIZE), BF16),
             pltpu.VMEM((ROWS, HEAD_SIZE), BF16),
-            pltpu.VMEM((SLABS, HEAD_SIZE, keys), BF16),
-            pltpu.VMEM((SLABS, keys, 2 * HEAD_SIZE), F32),
         ],
         compiler_params=pltpu.CompilerParams(vmem_limit_bytes=18 * 2**20),
         cost_estimate=pl.CostEstimate(

time: 109 us -> 106 us (0.972)
  starting transfers between devices: 45.7 us -> 42.6 us
    all_to_all x2, starting transfers between devices: 21.2 us -> 18.2 us  [exchange(): lax.all_to_all(parts, AXES, 0, 0, axis_index_groups=lists, tiled=True)]
where the time goes in v4:
time: 106 us; the launch traced here: 105 us
  starting transfers between devices  42.6 us (40%)
  blocking collectives  35.4 us (33%)
  waiting for transfers between devices  11.7 us (11%)
  Pallas kernels  8.88 us (8%)
  local copies, waits for them, and re-layouts  4.51 us (4%)
    all_to_all x2, blocking collectives, exchange(): lax.all_to_all(parts, AXES, 0, 0, axis_index_groups=lists, tiled=True)  22.9 us
    all_to_all x2, starting transfers between devices, exchange(): lax.all_to_all(parts, AXES, 0, 0, axis_index_groups=lists, tiled=True)  18.2 us
    ppermute x4, starting transfers between devices, to_peer(): lax.ppermute(array, 'ctx', [(c, c ^ 1) for c in range(lax.axis_size('ctx'...  13.2 us
    all_to_all x1, blocking collectives, shards(): lax.all_to_all(both, 'tp', 0, 0, tiled=True).reshape(rows, 2 * HEAD_SIZE)  12.5 us
    all_to_all x1, starting transfers between devices, shards(): lax.all_to_all(mine.reshape(tp_count, here, 2 * HEAD_SIZE), 'tp', 0, 0, t...  11.2 us
    all_to_all x2, waiting for transfers between devices, exchange(): lax.all_to_all(parts, AXES, 0, 0, axis_index_groups=lists, tiled=True)  6.86 us
    pallas_call x1, Pallas kernels, attention_gradients(): pl.pallas_call(gradients_kernel, out_shape=(jax.ShapeDtypeStruct(q.shape,...  3.42 us
    unnamed x8, local copies, waits for them, and re-layouts  3.4 us
  transfers between devices with their start and end apart: 7, of which 5 were waited for; matrix products, arithmetic and copies ran while one was open for 1% of the time, Pallas kernels for 2%

profile of v4, /device:TPU:1, one launch (start us, length us, event | category | flops | bytes accessed | tf_op | source)
XLA Modules:
  0.0 105.0 jit_solution(219604076050730290)
XLA Ops:
  0.6 0.0 copy-start.2
  0.6 0.7 copy-done.2
  1.4 0.0 copy-start.3
  1.4 0.8 copy-done.3
  2.2 12.5 %all_to_all.30 = bf16[4,32,256]{2,1,0:T(8,128)(2,1)S(1)} all-to-all(bf16[4,32,256]{2,1,0:T(8,128)(2,1)S(1)} %keys_and_values_by_head.1), channel_id=1, replica_groups=mesh['ctx'=128,'tp'=4] {'tp'}, dimensions={0} | all-to-all | bytes 131072 | tf_op jit(solution)/shard_map/all_to_all | solution.py:320
  14.7 9.5 %all_to_all.31 = bf16[4,128,256]{2,1,0:T(8,128)(2,1)S(1)} all-to-all(bf16[4,128,256]{2,1,0:T(8,128)(2,1)S(1)} %broadcast_in_dim.6), channel_id=1, replica_groups={{0,32,64,96},{4,36,68,100},{8,40,72,104},{12,44,76,108},{16,48,80,112},..., dimensions={0} | all-to-all | bytes 524288 | tf_op jit(solution)/shard_map/all_to_all | solution.py:290
  24.2 1.1 %broadcast_in_dim.7 = bf16[4,4,128,256]{3,2,1,0:T(8,128)(2,1)} broadcast(bf16[4,128,256]{2,1,0:T(8,128)(2,1)S(1)} %all_to_all.31), dimensions={1,2,3} | broadcast | bytes 1310720 | tf_op jit(solution)/shard_map/broadcast_in_dim | solution.py:322
  25.3 3.5 %all-to-all-start.2 = ((bf16[4,4,128,256]{3,2,1,0:T(8,128)(2,1)}), bf16[4,4,128,256]{3,2,1,0:T(8,128)(2,1)S(1)}, u32[]{:S(2)}, u32[]{:S(2)}) async-start(bf16[4,4,128,256]{3,2,1,0:T(8,128)(2,1)} %broadcast_in_dim.7), calls=%async_computation.2 | async-start | bytes 2097152 | tf_op jit(solution)/shard_map/all_to_all | solution.py:290
  28.8 1.9 %collective-permute-start = (bf16[128,1024]{1,0:T(8,128)(2,1)}, bf16[128,1024]{1,0:T(8,128)(2,1)S(1)}, u32[]{:S(2)}, u32[]{:S(2)}) collective-permute-start(bf16[128,1024]{1,0:T(8,128)(2,1)} %q_ref.1), channel_id=1, source_target_pairs={{0,4},{4,0},{8,12},{12,8},{16,20},{20,16},{24,28},{28,24},{32,36},... | collective-permute-start | bytes 786440 | tf_op jit(solution)/shard_map/ppermute | solution.py:294
  30.7 4.9 %collective-permute-start.1 = (bf16[128,1024]{1,0:T(8,128)(2,1)}, bf16[128,1024]{1,0:T(8,128)(2,1)S(1)}, u32[]{:S(2)}, u32[]{:S(2)}) collective-permute-start(bf16[128,1024]{1,0:T(8,128)(2,1)} %do_ref.1), channel_id=1, source_target_pairs={{0,4},{4,0},{8,12},{12,8},{16,20},{20,16},{24,28},{28,24},{32,36},... | collective-permute-start | bytes 786440 | tf_op jit(solution)/shard_map/ppermute | solution.py:294
  35.7 0.0 copy-start
  35.7 0.9 copy-done
  36.6 0.0 copy-start.1
  36.6 0.9 copy-done.1
  37.6 0.1 queries_by_head.1
  37.7 0.1 pad_add_fusion.place_ref
  37.8 3.3 %all-to-all-done.2.refs_2_.kv_ref = bf16[4,4,128,256]{3,2,1,0:T(8,128)(2,1)S(1)} async-done(((bf16[4,4,128,256]{3,2,1,0:T(8,128)(2,1)}), bf16[4,4,128,256]{3,2,1,0:T(8,128)(2,1)S(1)}, u32[]{:S(2)}, u32[]{:S(2)}) %all-to-all-start.2) | async-done | bytes 1048608 | tf_op jit(solution)/shard_map/all_to_all | solution.py:290
  41.1 1.6 %row_statistics.2 = (f32[24,256]{1,0:T(8,128)S(1)}, f32[8,1024]{1,0:T(8,128)S(1)}, bf16[4,512,1024]{2,1,0:T(8,128)(2,1)S(1)}, f32[4,512,1024]{2,1,0:T(8,128)S(1)}) custom-call(s32[3]{0:T(128)S(1)} %pad_add_fusion.place_ref, bf16[1024,128]{1,0:T(8,128)(2,1)S(1)} %get-tuple-element.18.refs_0_.own_q, bf16[1024,128]{1,0:T(8,128)(2,1)S(1)} %get-tuple-element.19.refs_1_.own_do, ...), custom_call_target="tpu_custom_call" | custom-call | flops 1073741824 | bytes 1048576 | tf_op jit(solution)/shard_map/row_statistics/pallas_call | solution.py:227
  42.7 0.0 collective-permute-done.refs_0_.peer_q
  42.7 0.3 collective-permute-done.1.refs_1_.peer_do
  43.1 1.5 %row_statistics.3 = (f32[24,256]{1,0:T(8,128)S(1)}, f32[8,1024]{1,0:T(8,128)S(1)}, bf16[4,512,1024]{2,1,0:T(8,128)(2,1)S(1)}, f32[4,512,1024]{2,1,0:T(8,128)S(1)}) custom-call(s32[3]{0:T(128)S(1)} %pad_add_fusion.place_ref, bf16[128,1024]{1,0:T(8,128)(2,1)S(1)} %collective-permute-done.refs_0_.peer_q, ...), custom_call_target="tpu_custom_call" | custom-call | flops 1073741824 | bytes 1048576 | tf_op jit(solution)/shard_map/row_statistics/pallas_call | solution.py:227
  44.6 4.3 %collective-permute-start.2 = (f32[24,256]{1,0:T(8,128)S(1)}, f32[24,256]{1,0:T(8,128)S(1)}, u32[]{:S(2)}, u32[]{:S(2)}) collective-permute-start(f32[24,256]{1,0:T(8,128)S(1)} %get-tuple-element.21.stats_ref), channel_id=1, source_target_pairs={{0,4},{4,0},{8,12},{12,8},{16,20},{20,16},{24,28},{28,24},{32,36},... | collective-permute-start | bytes 73736 | tf_op jit(solution)/shard_map/ppermute | solution.py:294
  49.0 1.7 %collective-permute-done.2.other_ref = f32[24,256]{1,0:T(8,128)S(1)} collective-permute-done((f32[24,256]{1,0:T(8,128)S(1)}, f32[24,256]{1,0:T(8,128)S(1)}, u32[]{:S(2)}, u32[]{:S(2)}) %collective-permute-start.2) | collective-permute-done | bytes 24608 | tf_op jit(solution)/shard_map/ppermute | solution.py:294
  50.7 3.4 %attention_gradients.1 = (f32[128,1024]{1,0:T(8,128)S(1)}, bf16[128,1024]{1,0:T(8,128)(2,1)S(1)}, bf16[4,4,128,256]{3,2,1,0:T(8,128)(2,1)S(1)}) custom-call(s32[3]{0:T(128)S(1)} %pad_add_fusion.place_ref, bf16[1024,128]{1,0:T(8,128)(2,1)S(1)} %get-tuple-element.18.refs_0_.own_q, bf16[1024,128]{1,0:T(8,128)(2,1)S(1)} %get-tuple-element.19.refs_1_.own_do, ...), custom_call_target="tpu_custom_call" | custom-call | flops 3221225472 | bytes 4194304 | tf_op jit(solution)/shard_map/attention_gradients/pallas_call | solution.py:249
  54.1 13.5 %all_to_all.32.parts_ref = bf16[4,4,128,256]{3,2,1,0:T(8,128)(2,1)S(1)} all-to-all(bf16[4,4,128,256]{3,2,1,0:T(8,128)(2,1)S(1)} %get-tuple-element.30), channel_id=1, replica_groups={{0,8,16,24},{4,12,20,28},{32,40,48,56},{36,44,52,60},{64,72,80,88},{68,..., dimensions={0} | all-to-all | bytes 2097152 | tf_op jit(solution)/shard_map/all_to_all | solution.py:290
  67.6 0.8 sum_of_parts.2
  68.4 14.7 %all-to-all-start.4 = ((bf16[4,128,256]{2,1,0:T(8,128)(2,1)}), bf16[4,128,256]{2,1,0:T(8,128)(2,1)S(1)}, u32[]{:S(2)}, u32[]{:S(2)}) async-start(bf16[4,128,256]{2,1,0:T(8,128)(2,1)} %sum_of_parts.2), calls=%async_computation.4 | async-start | bytes 524288 | tf_op jit(solution)/shard_map/all_to_all | solution.py:290
  83.1 2.1 %collective-permute-start.3 = (bf16[128,1024]{1,0:T(8,128)(2,1)S(1)}, bf16[128,1024]{1,0:T(8,128)(2,1)S(1)}, u32[]{:S(2)}, u32[]{:S(2)}) collective-permute-start(bf16[128,1024]{1,0:T(8,128)(2,1)S(1)} %get-tuple-element.29), channel_id=1, source_target_pairs={{0,4},{4,0},{8,12},{12,8},{16,20},{20,16},{24,28},{28,24},{32,36},... | collective-permute-start | bytes 786440 | tf_op jit(solution)/shard_map/ppermute | solution.py:294
  85.2 3.5 %all-to-all-done.4.parts_ref = bf16[4,128,256]{2,1,0:T(8,128)(2,1)S(1)} async-done(((bf16[4,128,256]{2,1,0:T(8,128)(2,1)}), bf16[4,128,256]{2,1,0:T(8,128)(2,1)S(1)}, u32[]{:S(2)}, u32[]{:S(2)}) %all-to-all-start.4) | async-done | bytes 262176 | tf_op jit(solution)/shard_map/all_to_all | solution.py:290
  88.7 0.7 sum_of_parts.3
  89.4 11.2 %all-to-all-start.5 = ((f32[4,32,256]{2,1,0:T(8,128)}), f32[4,32,256]{2,1,0:T(8,128)S(1)}, u32[]{:S(2)}, u32[]{:S(2)}) async-start(f32[4,32,256]{2,1,0:T(8,128)} %bitcast.4), calls=%async_computation.5 | async-start | bytes 262144 | tf_op jit(solution)/shard_map/all_to_all | solution.py:331
  100.6 0.0 collective-permute-done.3
  100.6 0.8 convert_add_fusion
  101.4 2.7 %all-to-all-done.5.both_ref = f32[4,32,256]{2,1,0:T(8,128)S(1)} async-done(((f32[4,32,256]{2,1,0:T(8,128)}), f32[4,32,256]{2,1,0:T(8,128)S(1)}, u32[]{:S(2)}, u32[]{:S(2)}) %all-to-all-start.5) | async-done | bytes 131104 | tf_op jit(solution)/shard_map/all_to_all | solution.py:331
  104.2 0.7 gradients_by_token.1
  (2 shorter events, 0.0 us)
Async XLA Ops:
  0.6 0.8 copy-start.2
  1.4 0.8 copy-start.3
  25.3 15.9 %all-to-all-start.2 = ((bf16[4,4,128,256]{3,2,1,0:T(8,128)(2,1)}), bf16[4,4,128,256]{3,2,1,0:T(8,128)(2,1)S(1)}, u32[]{:S(2)}, u32[]{:S(2)}) async-start(bf16[4,4,128,256]{3,2,1,0:T(8,128)(2,1)} %broadcast_in_dim.7), calls=%async_computation.2 | async-start | bytes 2097152 | tf_op jit(solution)/shard_map/all_to_all | solution.py:290
  28.8 13.9 %collective-permute-start = (bf16[128,1024]{1,0:T(8,128)(2,1)}, bf16[128,1024]{1,0:T(8,128)(2,1)S(1)}, u32[]{:S(2)}, u32[]{:S(2)}) collective-permute-start(bf16[128,1024]{1,0:T(8,128)(2,1)} %q_ref.1), channel_id=1, source_target_pairs={{0,4},{4,0},{8,12},{12,8},{16,20},{20,16},{24,28},{28,24},{32,36},... | collective-permute-start | bytes 786440 | tf_op jit(solution)/shard_map/ppermute | solution.py:294
  30.7 12.4 %collective-permute-start.1 = (bf16[128,1024]{1,0:T(8,128)(2,1)}, bf16[128,1024]{1,0:T(8,128)(2,1)S(1)}, u32[]{:S(2)}, u32[]{:S(2)}) collective-permute-start(bf16[128,1024]{1,0:T(8,128)(2,1)} %do_ref.1), channel_id=1, source_target_pairs={{0,4},{4,0},{8,12},{12,8},{16,20},{20,16},{24,28},{28,24},{32,36},... | collective-permute-start | bytes 786440 | tf_op jit(solution)/shard_map/ppermute | solution.py:294
  35.7 1.0 copy-start
  36.6 0.9 copy-start.1
  44.6 6.1 %collective-permute-start.2 = (f32[24,256]{1,0:T(8,128)S(1)}, f32[24,256]{1,0:T(8,128)S(1)}, u32[]{:S(2)}, u32[]{:S(2)}) collective-permute-start(f32[24,256]{1,0:T(8,128)S(1)} %get-tuple-element.21.stats_ref), channel_id=1, source_target_pairs={{0,4},{4,0},{8,12},{12,8},{16,20},{20,16},{24,28},{28,24},{32,36},... | collective-permute-start | bytes 73736 | tf_op jit(solution)/shard_map/ppermute | solution.py:294
  68.4 20.3 %all-to-all-start.4 = ((bf16[4,128,256]{2,1,0:T(8,128)(2,1)}), bf16[4,128,256]{2,1,0:T(8,128)(2,1)S(1)}, u32[]{:S(2)}, u32[]{:S(2)}) async-start(bf16[4,128,256]{2,1,0:T(8,128)(2,1)} %sum_of_parts.2), calls=%async_computation.4 | async-start | bytes 524288 | tf_op jit(solution)/shard_map/all_to_all | solution.py:290
  83.1 17.5 %collective-permute-start.3 = (bf16[128,1024]{1,0:T(8,128)(2,1)S(1)}, bf16[128,1024]{1,0:T(8,128)(2,1)S(1)}, u32[]{:S(2)}, u32[]{:S(2)}) collective-permute-start(bf16[128,1024]{1,0:T(8,128)(2,1)S(1)} %get-tuple-element.29), channel_id=1, source_target_pairs={{0,4},{4,0},{8,12},{12,8},{16,20},{20,16},{24,28},{28,24},{32,36},... | collective-permute-start | bytes 786440 | tf_op jit(solution)/shard_map/ppermute | solution.py:294
  89.4 14.8 %all-to-all-start.5 = ((f32[4,32,256]{2,1,0:T(8,128)}), f32[4,32,256]{2,1,0:T(8,128)S(1)}, u32[]{:S(2)}, u32[]{:S(2)}) async-start(f32[4,32,256]{2,1,0:T(8,128)} %bitcast.4), calls=%async_computation.5 | async-start | bytes 262144 | tf_op jit(solution)/shard_map/all_to_all | solution.py:331

commit v5 on v4

--- a/solution.py
+++ b/solution.py
@@ -104,14 +104,26 @@
         finish(lax.fori_loop(0, slab, functools.partial(step, masked=False), start))
 
 
+def key_columns_kernel(kv_ref, k_cols):
+    for s in range(SLABS):
+        k_cols[s] = keys_of(kv_ref, s, 0).T
+
+
+def query_rows_kernel(cols_ref, dq_ref, dq_peer_ref):
+    tokens = dq_ref.shape[0]
+    for owner, out in enumerate((dq_ref, dq_peer_ref)):
+        for h in range(dq_ref.shape[1] // HEAD_SIZE):
+            part = cols_ref[owner, :, h * tokens : (h + 1) * tokens].T
+            out[:, h * HEAD_SIZE : (h + 1) * HEAD_SIZE] = part.astype(out.dtype)
+
+
 def gradients_kernel(
     place_ref, own_q, own_do, peer_q, peer_do, kv_ref, stats_ref, other_ref,
     own_maxima, own_weights, own_slopes, peer_maxima, peer_weights, peer_slopes,
-    dq_ref, dq_peer_ref, dkv_ref,
+    k_cols, dq_ref, dkv_ref,
     there_q, there_do,
 ):
-    tokens, width = peer_q.shape
-    heads = width // HEAD_SIZE
+    tokens = peer_q.shape[0]
     along_y = kv_ref.shape[0]
     slab = place_ref[0]
     rows_kernel(peer_q, peer_do, there_q, there_do)
@@ -128,7 +140,6 @@
         norms.append((highest, inverse, centre * inverse))
 
     def step(s, dq_cols):
-        k_cols = keys_of(kv_ref, s, 0).T
         dk = dv = 0.0
         added = []
         for owner in range(PAIR):
@@ -139,16 +150,14 @@
             score_grad = (soft * (slopes[s] - centre)).astype(BF16)
             dk += product(score_grad, q_rows[...])
             dv += product(soft.astype(BF16), do_rows[...])
-            added.append(dq_cols[owner] + product(k_cols, score_grad))
+            added.append(dq_cols[owner] + product(k_cols[s], score_grad))
         dkv_ref[:, s, :, 0:HEAD_SIZE] = (dk * SCALE).astype(BF16).reshape(along_y, tokens, HEAD_SIZE)
         dkv_ref[:, s, :, HEAD_SIZE:] = dv.astype(BF16).reshape(along_y, tokens, HEAD_SIZE)
         return tuple(added)
 
     def finish(dq_cols):
-        for cols, out in zip(dq_cols, (dq_ref, dq_peer_ref)):
-            for h in range(heads):
-                part = cols[:, h * tokens : (h + 1) * tokens].T * SCALE
-                out[:, h * HEAD_SIZE : (h + 1) * HEAD_SIZE] = part.astype(out.dtype)
+        for owner in range(PAIR):
+            dq_ref[owner] = dq_cols[owner] * SCALE
 
     start = (jnp.zeros((HEAD_SIZE, ROWS), F32),) * PAIR
 
@@ -168,14 +177,14 @@
             dkv_ref[:, s] = jnp.zeros((along_y, tokens, 2 * HEAD_SIZE), BF16)
 
 
-def pack_kernel(key_ref, value_ref, out_ref):
+def pack_kernel(both_ref, out_ref):
     for h in range(out_ref.shape[0]):
-        across = slice(h * HEAD_SIZE, (h + 1) * HEAD_SIZE)
-        out_ref[h, :, 0:HEAD_SIZE] = key_ref[:, across]
-        out_ref[h, :, HEAD_SIZE:] = value_ref[:, across]
-
-
-def unpack_kernel(both_ref, key_ref, value_ref, sems):
+        for i in range(2):
+            out_ref[h, :, i * HEAD_SIZE : (i + 1) * HEAD_SIZE] = both_ref[i, :, h * HEAD_SIZE : (h + 1) * HEAD_SIZE]
+
+
+def finish_kernel(both_ref, dq_ref, peer_ref, key_ref, value_ref, query_ref, total, sems):
+    heads = both_ref.shape[0]
     copies = [
         pltpu.make_async_copy(
             both_ref.at[h, :, i * HEAD_SIZE : (i + 1) * HEAD_SIZE],
@@ -183,10 +192,16 @@
             sems.at[i, h],
         )
         for i, ref in enumerate((key_ref, value_ref))
-        for h in range(both_ref.shape[0])
+        for h in range(heads)
     ]
     for copy in copies:
         copy.start()
+    tokens = total.shape[0] // heads
+    for h in range(heads):
+        down = slice(h * tokens, (h + 1) * tokens)
+        total[down, :] = dq_ref[down, :] + peer_ref[down, :].astype(F32)
+        copies.append(pltpu.make_async_copy(total.at[down, :], query_ref.at[down, :], sems.at[2, h]))
+        copies[-1].start()
     for copy in copies:
         copy.wait()
 
@@ -244,17 +259,16 @@
 
 
 def attention_gradients(place, *args):
-    q, kv = args[2], args[4]
+    kv = args[4]
     keys = kv.shape[0] * kv.shape[2]
     return pl.pallas_call(
         gradients_kernel,
         out_shape=(
-            jax.ShapeDtypeStruct(q.shape, F32),
-            jax.ShapeDtypeStruct(q.shape, BF16),
+            jax.ShapeDtypeStruct((PAIR, HEAD_SIZE, ROWS), F32),
             jax.ShapeDtypeStruct(kv.shape, BF16),
         ),
         in_specs=[SCALARS] + [WHOLE] * len(args),
-        out_specs=(WHOLE, WHOLE, WHOLE),
+        out_specs=(WHOLE, WHOLE),
         scratch_shapes=[
             pltpu.VMEM((ROWS, HEAD_SIZE), BF16),
             pltpu.VMEM((ROWS, HEAD_SIZE), BF16),
@@ -313,26 +327,37 @@
     own_q, own_do = small(
         rows_kernel, "queries_by_head", (shape, shape), [WHOLE] * 2, (WHOLE, WHOLE), [], 4, query_heads, grad_output
     )
+    is_value = lax.broadcasted_iota(jnp.int32, (2,) + key_heads_wide.shape, 0) == 1
     both = small(
         pack_kernel, "keys_and_values_by_head", jax.ShapeDtypeStruct((tp_count, here, 2 * HEAD_SIZE), BF16),
-        [WHOLE, WHOLE], WHOLE, [], 4, key_heads_wide, value_heads_wide,
+        [WHOLE], WHOLE, [], 4, jnp.where(is_value, value_heads_wide, key_heads_wide),
     )
     own = lax.all_to_all(both, "tp", 0, 0, tiled=True).reshape(rows, 2 * HEAD_SIZE)
     column = exchange(jnp.broadcast_to(own, (SLABS,) + own.shape), along_z)
     kv = exchange(jnp.broadcast_to(column, (lines,) + column.shape), along_y)
     own_stats, *own_held = row_statistics(False, place, own_q, own_do, kv)
     stats, *peer_held = row_statistics(True, place, peer_q, peer_do, kv, own_stats)
-    dq, dq_peer, dkv = attention_gradients(
-        place, own_q, own_do, peer_q, peer_do, kv, stats, to_peer(stats), *own_held, *peer_held
-    )
-    grad_query = dq + to_peer(dq_peer).astype(F32)
+    k_cols = small(
+        key_columns_kernel, "keys_by_column",
+        jax.ShapeDtypeStruct((SLABS, HEAD_SIZE, kv.shape[0] * rows), BF16), [WHOLE], WHOLE, [], 4, kv,
+    )
+    dq_cols, dkv = attention_gradients(
+        place, own_q, own_do, peer_q, peer_do, kv, stats, to_peer(stats), *own_held, *peer_held, k_cols
+    )
+    shape = query_heads.shape
+    dq, dq_peer = small(
+        query_rows_kernel, "query_gradients_by_token",
+        (jax.ShapeDtypeStruct(shape, F32), jax.ShapeDtypeStruct(shape, BF16)), [WHOLE], (WHOLE, WHOLE), [], 8, dq_cols,
+    )
+    dq_there = to_peer(dq_peer)
     partial = summed(exchange(dkv, along_y), BF16)
     mine = summed(exchange(partial, along_z), F32)
     back = lax.all_to_all(mine.reshape(tp_count, here, 2 * HEAD_SIZE), "tp", 0, 0, tiled=True)
     shape = jax.ShapeDtypeStruct(key_heads_wide.shape, F32)
-    key_gradient, value_gradient = small(
-        unpack_kernel, "gradients_by_token", (shape, shape), [WHOLE], (IN_HBM, IN_HBM),
-        [pltpu.SemaphoreType.DMA((2, tp_count))], 4, back
+    key_gradient, value_gradient, grad_query = small(
+        finish_kernel, "gradients_by_token", (shape, shape, jax.ShapeDtypeStruct(dq.shape, F32)),
+        [WHOLE] * 3, (IN_HBM,) * 3,
+        [pltpu.VMEM(dq.shape, F32), pltpu.SemaphoreType.DMA((3, tp_count))], 4, back, dq, dq_there,
     )
     return grad_query, key_gradient, value_gradient
 

time: 106 us -> 105 us (level)
  local copies, waits for them, and re-layouts: 4.51 us -> 3 us
    unnamed x8 -> x4, local copies, waits for them, and re-layouts: 3.4 us -> 1.89 us
    pallas_call x5 -> x7, Pallas kernels: 2.35 us -> 3.01 us  [small(): pl.pallas_call(kernel, out_shape=out, in_specs=in_specs, out_specs=out_sp...]
  transfers between devices with their start and end apart: 7 -> 7, of which waited for: 5 -> 5; matrix products, arithmetic and copies ran while one was open for 1% -> 0% of each run, Pallas kernels for 2% -> 3%
where the time goes in v5:
time: 105 us; the launch traced here: 104 us
  starting transfers between devices  42.7 us (41%)
  blocking collectives  35.4 us (34%)
  waiting for transfers between devices  12 us (11%)
  Pallas kernels  9.27 us (9%)
  local copies, waits for them, and re-layouts  3 us (3%)
    all_to_all x2, blocking collectives, exchange(): lax.all_to_all(parts, AXES, 0, 0, axis_index_groups=lists, tiled=True)  22.9 us
    all_to_all x2, starting transfers between devices, exchange(): lax.all_to_all(parts, AXES, 0, 0, axis_index_groups=lists, tiled=True)  18.2 us
    ppermute x4, starting transfers between devices, to_peer(): lax.ppermute(array, 'ctx', [(c, c ^ 1) for c in range(lax.axis_size('ctx'...  13.3 us
    all_to_all x1, blocking collectives, shards(): lax.all_to_all(both, 'tp', 0, 0, tiled=True).reshape(rows, 2 * HEAD_SIZE)  12.5 us
    all_to_all x1, starting transfers between devices, shards(): lax.all_to_all(mine.reshape(tp_count, here, 2 * HEAD_SIZE), 'tp', 0, 0, t...  11.2 us
    all_to_all x2, waiting for transfers between devices, exchange(): lax.all_to_all(parts, AXES, 0, 0, axis_index_groups=lists, tiled=True)  6.53 us
    all_to_all x1, waiting for transfers between devices, shards(): lax.all_to_all(mine.reshape(tp_count, here, 2 * HEAD_SIZE), 'tp', 0, 0, t...  3.59 us
    pallas_call x1, Pallas kernels, attention_gradients(): pl.pallas_call(gradients_kernel, out_shape=(jax.ShapeDtypeStruct((PAIR, H...  3.16 us
  transfers between devices with their start and end apart: 7, of which 5 were waited for; matrix products, arithmetic and copies ran while one was open for 0% of the time, Pallas kernels for 3%

profile of v5, /device:TPU:1, one launch (start us, length us, event | category | flops | bytes accessed | tf_op | source)
XLA Modules:
  0.0 104.4 jit_solution(11662289847231481760)
XLA Ops:
  0.6 0.9 broadcast_select_fusion.both_ref
  1.5 12.5 %all_to_all.30 = bf16[4,32,256]{2,1,0:T(8,128)(2,1)S(1)} all-to-all(bf16[4,32,256]{2,1,0:T(8,128)(2,1)S(1)} %keys_and_values_by_head.1), channel_id=1, replica_groups=mesh['ctx'=128,'tp'=4] {'tp'}, dimensions={0} | all-to-all | bytes 131072 | tf_op jit(solution)/shard_map/all_to_all | solution.py:335
  14.0 9.5 %all_to_all.31 = bf16[4,128,256]{2,1,0:T(8,128)(2,1)S(1)} all-to-all(bf16[4,128,256]{2,1,0:T(8,128)(2,1)S(1)} %broadcast_in_dim.16), channel_id=1, replica_groups={{0,32,64,96},{4,36,68,100},{8,40,72,104},{12,44,76,108},{16,48,80,112},..., dimensions={0} | all-to-all | bytes 524288 | tf_op jit(solution)/shard_map/all_to_all | solution.py:304
  23.5 1.1 %broadcast_in_dim.17 = bf16[4,4,128,256]{3,2,1,0:T(8,128)(2,1)} broadcast(bf16[4,128,256]{2,1,0:T(8,128)(2,1)S(1)} %all_to_all.31), dimensions={1,2,3} | broadcast | bytes 1310720 | tf_op jit(solution)/shard_map/broadcast_in_dim | solution.py:337
  24.6 3.5 %all-to-all-start.2 = ((bf16[4,4,128,256]{3,2,1,0:T(8,128)(2,1)}), bf16[4,4,128,256]{3,2,1,0:T(8,128)(2,1)S(1)}, u32[]{:S(2)}, u32[]{:S(2)}) async-start(bf16[4,4,128,256]{3,2,1,0:T(8,128)(2,1)} %broadcast_in_dim.17), calls=%async_computation.2 | async-start | bytes 2097152 | tf_op jit(solution)/shard_map/all_to_all | solution.py:304
  28.1 1.9 %collective-permute-start = (bf16[128,1024]{1,0:T(8,128)(2,1)}, bf16[128,1024]{1,0:T(8,128)(2,1)S(1)}, u32[]{:S(2)}, u32[]{:S(2)}) collective-permute-start(bf16[128,1024]{1,0:T(8,128)(2,1)} %q_ref.1), channel_id=1, source_target_pairs={{0,4},{4,0},{8,12},{12,8},{16,20},{20,16},{24,28},{28,24},{32,36},... | collective-permute-start | bytes 786440 | tf_op jit(solution)/shard_map/ppermute | solution.py:308
  30.1 4.9 %collective-permute-start.1 = (bf16[128,1024]{1,0:T(8,128)(2,1)}, bf16[128,1024]{1,0:T(8,128)(2,1)S(1)}, u32[]{:S(2)}, u32[]{:S(2)}) collective-permute-start(bf16[128,1024]{1,0:T(8,128)(2,1)} %do_ref.1), channel_id=1, source_target_pairs={{0,4},{4,0},{8,12},{12,8},{16,20},{20,16},{24,28},{28,24},{32,36},... | collective-permute-start | bytes 786440 | tf_op jit(solution)/shard_map/ppermute | solution.py:308
  35.0 0.0 copy-start
  35.0 0.9 copy-done
  36.0 0.0 copy-start.1
  36.0 0.9 copy-done.1
  36.9 0.1 queries_by_head.1
  37.1 0.1 pad_add_fusion.place_ref
  37.1 3.3 %all-to-all-done.2.refs_2_.kv_ref = bf16[4,4,128,256]{3,2,1,0:T(8,128)(2,1)S(1)} async-done(((bf16[4,4,128,256]{3,2,1,0:T(8,128)(2,1)}), bf16[4,4,128,256]{3,2,1,0:T(8,128)(2,1)S(1)}, u32[]{:S(2)}, u32[]{:S(2)}) %all-to-all-start.2) | async-done | bytes 1048608 | tf_op jit(solution)/shard_map/all_to_all | solution.py:304
  40.5 1.6 %row_statistics.2 = (f32[24,256]{1,0:T(8,128)S(1)}, f32[8,1024]{1,0:T(8,128)S(1)}, bf16[4,512,1024]{2,1,0:T(8,128)(2,1)S(1)}, f32[4,512,1024]{2,1,0:T(8,128)S(1)}) custom-call(s32[3]{0:T(128)S(1)} %pad_add_fusion.place_ref, bf16[1024,128]{1,0:T(8,128)(2,1)S(1)} %get-tuple-element.20.refs_0_.own_q, bf16[1024,128]{1,0:T(8,128)(2,1)S(1)} %get-tuple-element.21.refs_1_.own_do, ...), custom_call_target="tpu_custom_call" | custom-call | flops 1073741824 | bytes 1048576 | tf_op jit(solution)/shard_map/row_statistics/pallas_call | solution.py:242
  42.1 0.0 collective-permute-done.refs_0_.peer_q
  42.1 0.4 collective-permute-done.1.refs_1_.peer_do
  42.4 1.5 %row_statistics.3 = (f32[24,256]{1,0:T(8,128)S(1)}, f32[8,1024]{1,0:T(8,128)S(1)}, bf16[4,512,1024]{2,1,0:T(8,128)(2,1)S(1)}, f32[4,512,1024]{2,1,0:T(8,128)S(1)}) custom-call(s32[3]{0:T(128)S(1)} %pad_add_fusion.place_ref, bf16[128,1024]{1,0:T(8,128)(2,1)S(1)} %collective-permute-done.refs_0_.peer_q, ...), custom_call_target="tpu_custom_call" | custom-call | flops 1073741824 | bytes 1048576 | tf_op jit(solution)/shard_map/row_statistics/pallas_call | solution.py:242
  44.0 4.3 %collective-permute-start.2 = (f32[24,256]{1,0:T(8,128)S(1)}, f32[24,256]{1,0:T(8,128)S(1)}, u32[]{:S(2)}, u32[]{:S(2)}) collective-permute-start(f32[24,256]{1,0:T(8,128)S(1)} %get-tuple-element.23.stats_ref), channel_id=1, source_target_pairs={{0,4},{4,0},{8,12},{12,8},{16,20},{20,16},{24,28},{28,24},{32,36},... | collective-permute-start | bytes 73736 | tf_op jit(solution)/shard_map/ppermute | solution.py:308
  48.3 0.2 keys_by_column.1.k_cols
  48.5 1.5 %collective-permute-done.2.other_ref = f32[24,256]{1,0:T(8,128)S(1)} collective-permute-done((f32[24,256]{1,0:T(8,128)S(1)}, f32[24,256]{1,0:T(8,128)S(1)}, u32[]{:S(2)}, u32[]{:S(2)}) %collective-permute-start.2) | collective-permute-done | bytes 24608 | tf_op jit(solution)/shard_map/ppermute | solution.py:308
  50.0 3.2 %attention_gradients.1 = (f32[2,128,1024]{2,1,0:T(8,128)S(1)}, bf16[4,4,128,256]{3,2,1,0:T(8,128)(2,1)S(1)}) custom-call(s32[3]{0:T(128)S(1)} %pad_add_fusion.place_ref, bf16[1024,128]{1,0:T(8,128)(2,1)S(1)} %get-tuple-element.20.refs_0_.own_q, bf16[1024,128]{1,0:T(8,128)(2,1)S(1)} %get-tuple-element.21.refs_1_.own_do, ...), custom_call_target="tpu_custom_call" | custom-call | flops 3221225472 | bytes 4194304 | tf_op jit(solution)/shard_map/attention_gradients/pallas_call | solution.py:264
  53.2 13.5 %all_to_all.32.parts_ref = bf16[4,4,128,256]{3,2,1,0:T(8,128)(2,1)S(1)} all-to-all(bf16[4,4,128,256]{3,2,1,0:T(8,128)(2,1)S(1)} %get-tuple-element.30), channel_id=1, replica_groups={{0,8,16,24},{4,12,20,28},{32,40,48,56},{36,44,52,60},{64,72,80,88},{68,..., dimensions={0} | all-to-all | bytes 2097152 | tf_op jit(solution)/shard_map/all_to_all | solution.py:304
  66.7 0.8 sum_of_parts.2
  67.5 14.7 %all-to-all-start.4 = ((bf16[4,128,256]{2,1,0:T(8,128)(2,1)}), bf16[4,128,256]{2,1,0:T(8,128)(2,1)S(1)}, u32[]{:S(2)}, u32[]{:S(2)}) async-start(bf16[4,128,256]{2,1,0:T(8,128)(2,1)} %sum_of_parts.2), calls=%async_computation.4 | async-start | bytes 524288 | tf_op jit(solution)/shard_map/all_to_all | solution.py:304
  82.2 0.3 query_gradients_by_token.1
  82.5 2.2 %collective-permute-start.3 = (bf16[128,1024]{1,0:T(8,128)(2,1)S(1)}, bf16[128,1024]{1,0:T(8,128)(2,1)S(1)}, u32[]{:S(2)}, u32[]{:S(2)}) collective-permute-start(bf16[128,1024]{1,0:T(8,128)(2,1)S(1)} %get-tuple-element.33), channel_id=1, source_target_pairs={{0,4},{4,0},{8,12},{12,8},{16,20},{20,16},{24,28},{28,24},{32,36},... | collective-permute-start | bytes 786440 | tf_op jit(solution)/shard_map/ppermute | solution.py:308
  84.7 3.2 %all-to-all-done.4.parts_ref = bf16[4,128,256]{2,1,0:T(8,128)(2,1)S(1)} async-done(((bf16[4,128,256]{2,1,0:T(8,128)(2,1)}), bf16[4,128,256]{2,1,0:T(8,128)(2,1)S(1)}, u32[]{:S(2)}, u32[]{:S(2)}) %all-to-all-start.4) | async-done | bytes 262176 | tf_op jit(solution)/shard_map/all_to_all | solution.py:304
  87.8 0.7 sum_of_parts.3
  88.5 11.2 %all-to-all-start.5 = ((f32[4,32,256]{2,1,0:T(8,128)}), f32[4,32,256]{2,1,0:T(8,128)S(1)}, u32[]{:S(2)}, u32[]{:S(2)}) async-start(f32[4,32,256]{2,1,0:T(8,128)} %bitcast.4), calls=%async_computation.5 | async-start | bytes 262144 | tf_op jit(solution)/shard_map/all_to_all | solution.py:355
  99.7 0.0 collective-permute-done.3.peer_ref
  99.7 3.6 %all-to-all-done.5.both_ref = f32[4,32,256]{2,1,0:T(8,128)S(1)} async-done(((f32[4,32,256]{2,1,0:T(8,128)}), f32[4,32,256]{2,1,0:T(8,128)S(1)}, u32[]{:S(2)}, u32[]{:S(2)}) %all-to-all-start.5) | async-done | bytes 131104 | tf_op jit(solution)/shard_map/all_to_all | solution.py:355
  103.3 0.9 gradients_by_token.1
  (3 shorter events, 0.0 us)
Async XLA Ops:
  24.6 15.9 %all-to-all-start.2 = ((bf16[4,4,128,256]{3,2,1,0:T(8,128)(2,1)}), bf16[4,4,128,256]{3,2,1,0:T(8,128)(2,1)S(1)}, u32[]{:S(2)}, u32[]{:S(2)}) async-start(bf16[4,4,128,256]{3,2,1,0:T(8,128)(2,1)} %broadcast_in_dim.17), calls=%async_computation.2 | async-start | bytes 2097152 | tf_op jit(solution)/shard_map/all_to_all | solution.py:304
  28.1 13.9 %collective-permute-start = (bf16[128,1024]{1,0:T(8,128)(2,1)}, bf16[128,1024]{1,0:T(8,128)(2,1)S(1)}, u32[]{:S(2)}, u32[]{:S(2)}) collective-permute-start(bf16[128,1024]{1,0:T(8,128)(2,1)} %q_ref.1), channel_id=1, source_target_pairs={{0,4},{4,0},{8,12},{12,8},{16,20},{20,16},{24,28},{28,24},{32,36},... | collective-permute-start | bytes 786440 | tf_op jit(solution)/shard_map/ppermute | solution.py:308
  30.1 12.4 %collective-permute-start.1 = (bf16[128,1024]{1,0:T(8,128)(2,1)}, bf16[128,1024]{1,0:T(8,128)(2,1)S(1)}, u32[]{:S(2)}, u32[]{:S(2)}) collective-permute-start(bf16[128,1024]{1,0:T(8,128)(2,1)} %do_ref.1), channel_id=1, source_target_pairs={{0,4},{4,0},{8,12},{12,8},{16,20},{20,16},{24,28},{28,24},{32,36},... | collective-permute-start | bytes 786440 | tf_op jit(solution)/shard_map/ppermute | solution.py:308
  35.0 1.0 copy-start
  36.0 0.9 copy-start.1
  44.0 6.1 %collective-permute-start.2 = (f32[24,256]{1,0:T(8,128)S(1)}, f32[24,256]{1,0:T(8,128)S(1)}, u32[]{:S(2)}, u32[]{:S(2)}) collective-permute-start(f32[24,256]{1,0:T(8,128)S(1)} %get-tuple-element.23.stats_ref), channel_id=1, source_target_pairs={{0,4},{4,0},{8,12},{12,8},{16,20},{20,16},{24,28},{28,24},{32,36},... | collective-permute-start | bytes 73736 | tf_op jit(solution)/shard_map/ppermute | solution.py:308
  67.5 20.3 %all-to-all-start.4 = ((bf16[4,128,256]{2,1,0:T(8,128)(2,1)}), bf16[4,128,256]{2,1,0:T(8,128)(2,1)S(1)}, u32[]{:S(2)}, u32[]{:S(2)}) async-start(bf16[4,128,256]{2,1,0:T(8,128)(2,1)} %sum_of_parts.2), calls=%async_computation.4 | async-start | bytes 524288 | tf_op jit(solution)/shard_map/all_to_all | solution.py:304
  82.5 17.3 %collective-permute-start.3 = (bf16[128,1024]{1,0:T(8,128)(2,1)S(1)}, bf16[128,1024]{1,0:T(8,128)(2,1)S(1)}, u32[]{:S(2)}, u32[]{:S(2)}) collective-permute-start(bf16[128,1024]{1,0:T(8,128)(2,1)S(1)} %get-tuple-element.33), channel_id=1, source_target_pairs={{0,4},{4,0},{8,12},{12,8},{16,20},{20,16},{24,28},{28,24},{32,36},... | collective-permute-start | bytes 786440 | tf_op jit(solution)/shard_map/ppermute | solution.py:308
  88.5 14.8 %all-to-all-start.5 = ((f32[4,32,256]{2,1,0:T(8,128)}), f32[4,32,256]{2,1,0:T(8,128)S(1)}, u32[]{:S(2)}, u32[]{:S(2)}) async-start(f32[4,32,256]{2,1,0:T(8,128)} %bitcast.4), calls=%async_computation.5 | async-start | bytes 262144 | tf_op jit(solution)/shard_map/all_to_all | solution.py:355

commit v6 on v5

--- a/solution.py
+++ b/solution.py
@@ -120,8 +120,8 @@
 def gradients_kernel(
     place_ref, own_q, own_do, peer_q, peer_do, kv_ref, stats_ref, other_ref,
     own_maxima, own_weights, own_slopes, peer_maxima, peer_weights, peer_slopes,
-    k_cols, dq_ref, dkv_ref,
-    there_q, there_do,
+    k_cols, dq_ref, dkv_out,
+    there_q, there_do, dkv_ref, sems,
 ):
     tokens = peer_q.shape[0]
     along_y = kv_ref.shape[0]
@@ -138,6 +138,9 @@
         inverse = 1.0 / (row_of(stats_ref, 1, owner) * here_factor + row_of(other_ref, 1, 1 - owner) * there_factor)
         centre = row_of(stats_ref, 2, owner) * here_factor + row_of(other_ref, 2, 1 - owner) * there_factor
         norms.append((highest, inverse, centre * inverse))
+
+    def leaving(s):
+        return pltpu.make_async_copy(dkv_ref.at[:, s], dkv_out.at[:, s], sems.at[s])
 
     def step(s, dq_cols):
         dk = dv = 0.0
@@ -153,6 +156,7 @@
             added.append(dq_cols[owner] + product(k_cols[s], score_grad))
         dkv_ref[:, s, :, 0:HEAD_SIZE] = (dk * SCALE).astype(BF16).reshape(along_y, tokens, HEAD_SIZE)
         dkv_ref[:, s, :, HEAD_SIZE:] = dv.astype(BF16).reshape(along_y, tokens, HEAD_SIZE)
+        leaving(s).start()
         return tuple(added)
 
     def finish(dq_cols):
@@ -175,6 +179,10 @@
         @pl.loop(slab + 1, SLABS)
         def _(s):
             dkv_ref[:, s] = jnp.zeros((along_y, tokens, 2 * HEAD_SIZE), BF16)
+            leaving(s).start()
+
+    for s in range(SLABS):
+        leaving(s).wait()
 
 
 def pack_kernel(both_ref, out_ref):
@@ -268,12 +276,14 @@
             jax.ShapeDtypeStruct(kv.shape, BF16),
         ),
         in_specs=[SCALARS] + [WHOLE] * len(args),
-        out_specs=(WHOLE, WHOLE),
+        out_specs=(WHOLE, IN_HBM),
         scratch_shapes=[
             pltpu.VMEM((ROWS, HEAD_SIZE), BF16),
             pltpu.VMEM((ROWS, HEAD_SIZE), BF16),
+            pltpu.VMEM(kv.shape, BF16),
+            pltpu.SemaphoreType.DMA((SLABS,)),
         ],
-        compiler_params=pltpu.CompilerParams(vmem_limit_bytes=18 * 2**20),
+        compiler_params=pltpu.CompilerParams(vmem_limit_bytes=19 * 2**20),
         cost_estimate=pl.CostEstimate(
             flops=12 * ROWS * SLABS * keys * HEAD_SIZE, bytes_accessed=4 * 2**20, transcendentals=ROWS
         ),
@@ -351,6 +361,7 @@
     )
     dq_there = to_peer(dq_peer)
     partial = summed(exchange(dkv, along_y), BF16)
+    partial, dq_there = lax.optimization_barrier((partial, dq_there))
     mine = summed(exchange(partial, along_z), F32)
     back = lax.all_to_all(mine.reshape(tp_count, here, 2 * HEAD_SIZE), "tp", 0, 0, tiled=True)
     shape = jax.ShapeDtypeStruct(key_heads_wide.shape, F32)

time: 105 us -> 105 us (level)
  blocking collectives: 35.4 us -> 57.7 us
  starting transfers between devices: 42.7 us -> 23.3 us
  waiting for transfers between devices: 12 us -> 10 us
    all_to_all x0 -> x1, blocking collectives: none -> 14.6 us  [shards(): lax.all_to_all(mine.reshape(tp_count, here, 2 * HEAD_SIZE), 'tp', 0, 0, t...]
    all_to_all x1 -> x0, starting transfers between devices: 11.2 us -> none  [shards(): lax.all_to_all(mine.reshape(tp_count, here, 2 * HEAD_SIZE), 'tp', 0, 0, t...]
    all_to_all x2, starting transfers between devices: 18.2 us -> 7.44 us  [exchange(): lax.all_to_all(parts, AXES, 0, 0, axis_index_groups=lists, tiled=True)]
    all_to_all x2, blocking collectives: 22.9 us -> 30.5 us  [exchange(): lax.all_to_all(parts, AXES, 0, 0, axis_index_groups=lists, tiled=True)]
    all_to_all x1 -> x0, waiting for transfers between devices: 3.59 us -> none  [shards(): lax.all_to_all(mine.reshape(tp_count, here, 2 * HEAD_SIZE), 'tp', 0, 0, t...]
    ppermute x4, starting transfers between devices: 13.3 us -> 15.8 us  [to_peer(): lax.ppermute(array, 'ctx', [(c, c ^ 1) for c in range(lax.axis_size('ctx'...]
    all_to_all x2, waiting for transfers between devices: 6.53 us -> 8.1 us  [exchange(): lax.all_to_all(parts, AXES, 0, 0, axis_index_groups=lists, tiled=True)]
    pallas_call x7, Pallas kernels: 3.01 us -> 1.66 us  [small(): pl.pallas_call(kernel, out_shape=out, in_specs=in_specs, out_specs=out_sp...]
  transfers between devices with their start and end apart: 7 -> 6, of which waited for: 5 -> 4; matrix products, arithmetic and copies ran while one was open for 0% -> 0% of each run, Pallas kernels for 3% -> 2%
where the time goes in v6:
time: 105 us
  blocking collectives  57.7 us (55%)
  starting transfers between devices  23.3 us (22%)
  waiting for transfers between devices  10 us (10%)
  Pallas kernels  8.81 us (8%)
  local copies, waits for them, and re-layouts  3 us (3%)
    all_to_all x2, blocking collectives, exchange(): lax.all_to_all(parts, AXES, 0, 0, axis_index_groups=lists, tiled=True)  30.5 us
    ppermute x4, starting transfers between devices, to_peer(): lax.ppermute(array, 'ctx', [(c, c ^ 1) for c in range(lax.axis_size('ctx'...  15.8 us
    all_to_all x1, blocking collectives, shards(): lax.all_to_all(mine.reshape(tp_count, here, 2 * HEAD_SIZE), 'tp', 0, 0, t...  14.6 us
    all_to_all x1, blocking collectives, shards(): lax.all_to_all(both, 'tp', 0, 0, tiled=True).reshape(rows, 2 * HEAD_SIZE)  12.5 us
    all_to_all x2, waiting for transfers between devices, exchange(): lax.all_to_all(parts, AXES, 0, 0, axis_index_groups=lists, tiled=True)  8.1 us
    all_to_all x2, starting transfers between devices, exchange(): lax.all_to_all(parts, AXES, 0, 0, axis_index_groups=lists, tiled=True)  7.44 us
    pallas_call x1, Pallas kernels, attention_gradients(): pl.pallas_call(gradients_kernel, out_shape=(jax.ShapeDtypeStruct((PAIR, H...  4.07 us
    pallas_call x2, Pallas kernels, row_statistics(): pl.pallas_call(functools.partial(statistics_kernel, of_peer), out_shape=(...  3.09 us
  transfers between devices with their start and end apart: 6, of which 4 were waited for; matrix products, arithmetic and copies ran while one was open for 0% of the time, Pallas kernels for 2%

profile of v6, /device:TPU:1, one launch (start us, length us, event | category | flops | bytes accessed | tf_op | source)
XLA Modules:
  0.0 104.7 jit_solution(11614678603675613586)
XLA Ops:
  0.6 0.9 broadcast_select_fusion.both_ref
  1.5 12.5 %all_to_all.30 = bf16[4,32,256]{2,1,0:T(8,128)(2,1)S(1)} all-to-all(bf16[4,32,256]{2,1,0:T(8,128)(2,1)S(1)} %keys_and_values_by_head.1), channel_id=1, replica_groups=mesh['ctx'=128,'tp'=4] {'tp'}, dimensions={0} | all-to-all | bytes 131072 | tf_op jit(solution)/shard_map/all_to_all | solution.py:345
  14.0 9.5 %all_to_all.31 = bf16[4,128,256]{2,1,0:T(8,128)(2,1)S(1)} all-to-all(bf16[4,128,256]{2,1,0:T(8,128)(2,1)S(1)} %broadcast_in_dim.16), channel_id=1, replica_groups={{0,32,64,96},{4,36,68,100},{8,40,72,104},{12,44,76,108},{16,48,80,112},..., dimensions={0} | all-to-all | bytes 524288 | tf_op jit(solution)/shard_map/all_to_all | solution.py:314
  23.5 1.1 %broadcast_in_dim.17 = bf16[4,4,128,256]{3,2,1,0:T(8,128)(2,1)} broadcast(bf16[4,128,256]{2,1,0:T(8,128)(2,1)S(1)} %all_to_all.31), dimensions={1,2,3} | broadcast | bytes 1310720 | tf_op jit(solution)/shard_map/broadcast_in_dim | solution.py:347
  24.6 3.5 %all-to-all-start.2 = ((bf16[4,4,128,256]{3,2,1,0:T(8,128)(2,1)}), bf16[4,4,128,256]{3,2,1,0:T(8,128)(2,1)S(1)}, u32[]{:S(2)}, u32[]{:S(2)}) async-start(bf16[4,4,128,256]{3,2,1,0:T(8,128)(2,1)} %broadcast_in_dim.17), calls=%async_computation.2 | async-start | bytes 2097152 | tf_op jit(solution)/shard_map/all_to_all | solution.py:314
  28.1 1.9 %collective-permute-start = (bf16[128,1024]{1,0:T(8,128)(2,1)}, bf16[128,1024]{1,0:T(8,128)(2,1)S(1)}, u32[]{:S(2)}, u32[]{:S(2)}) collective-permute-start(bf16[128,1024]{1,0:T(8,128)(2,1)} %q_ref.1), channel_id=1, source_target_pairs={{0,4},{4,0},{8,12},{12,8},{16,20},{20,16},{24,28},{28,24},{32,36},... | collective-permute-start | bytes 786440 | tf_op jit(solution)/shard_map/ppermute | solution.py:318
  30.1 4.9 %collective-permute-start.1 = (bf16[128,1024]{1,0:T(8,128)(2,1)}, bf16[128,1024]{1,0:T(8,128)(2,1)S(1)}, u32[]{:S(2)}, u32[]{:S(2)}) collective-permute-start(bf16[128,1024]{1,0:T(8,128)(2,1)} %do_ref.1), channel_id=1, source_target_pairs={{0,4},{4,0},{8,12},{12,8},{16,20},{20,16},{24,28},{28,24},{32,36},... | collective-permute-start | bytes 786440 | tf_op jit(solution)/shard_map/ppermute | solution.py:318
  35.0 0.0 copy-start
  35.0 0.9 copy-done
  36.0 0.0 copy-start.1
  36.0 0.9 copy-done.1
  36.9 0.1 queries_by_head.1
  37.1 0.1 pad_add_fusion.place_ref
  37.1 3.3 %all-to-all-done.2.refs_2_.kv_ref = bf16[4,4,128,256]{3,2,1,0:T(8,128)(2,1)S(1)} async-done(((bf16[4,4,128,256]{3,2,1,0:T(8,128)(2,1)}), bf16[4,4,128,256]{3,2,1,0:T(8,128)(2,1)S(1)}, u32[]{:S(2)}, u32[]{:S(2)}) %all-to-all-start.2) | async-done | bytes 1048608 | tf_op jit(solution)/shard_map/all_to_all | solution.py:314
  40.5 1.6 %row_statistics.2 = (f32[24,256]{1,0:T(8,128)S(1)}, f32[8,1024]{1,0:T(8,128)S(1)}, bf16[4,512,1024]{2,1,0:T(8,128)(2,1)S(1)}, f32[4,512,1024]{2,1,0:T(8,128)S(1)}) custom-call(s32[3]{0:T(128)S(1)} %pad_add_fusion.place_ref, bf16[1024,128]{1,0:T(8,128)(2,1)S(1)} %get-tuple-element.22.refs_0_.own_q, bf16[1024,128]{1,0:T(8,128)(2,1)S(1)} %get-tuple-element.23.refs_1_.own_do, ...), custom_call_target="tpu_custom_call" | custom-call | flops 1073741824 | bytes 1048576 | tf_op jit(solution)/shard_map/row_statistics/pallas_call | solution.py:250
  42.1 0.0 collective-permute-done.refs_0_.peer_q
  42.1 0.4 collective-permute-done.1.refs_1_.peer_do
  42.4 1.5 %row_statistics.3 = (f32[24,256]{1,0:T(8,128)S(1)}, f32[8,1024]{1,0:T(8,128)S(1)}, bf16[4,512,1024]{2,1,0:T(8,128)(2,1)S(1)}, f32[4,512,1024]{2,1,0:T(8,128)S(1)}) custom-call(s32[3]{0:T(128)S(1)} %pad_add_fusion.place_ref, bf16[128,1024]{1,0:T(8,128)(2,1)S(1)} %collective-permute-done.refs_0_.peer_q, ...), custom_call_target="tpu_custom_call" | custom-call | flops 1073741824 | bytes 1048576 | tf_op jit(solution)/shard_map/row_statistics/pallas_call | solution.py:250
  44.0 4.3 %collective-permute-start.2 = (f32[24,256]{1,0:T(8,128)S(1)}, f32[24,256]{1,0:T(8,128)S(1)}, u32[]{:S(2)}, u32[]{:S(2)}) collective-permute-start(f32[24,256]{1,0:T(8,128)S(1)} %get-tuple-element.25.stats_ref), channel_id=1, source_target_pairs={{0,4},{4,0},{8,12},{12,8},{16,20},{20,16},{24,28},{28,24},{32,36},... | collective-permute-start | bytes 73736 | tf_op jit(solution)/shard_map/ppermute | solution.py:318
  48.3 0.2 keys_by_column.1.k_cols
  48.5 1.5 %collective-permute-done.2.other_ref = f32[24,256]{1,0:T(8,128)S(1)} collective-permute-done((f32[24,256]{1,0:T(8,128)S(1)}, f32[24,256]{1,0:T(8,128)S(1)}, u32[]{:S(2)}, u32[]{:S(2)}) %collective-permute-start.2) | collective-permute-done | bytes 24608 | tf_op jit(solution)/shard_map/ppermute | solution.py:318
  50.0 4.1 %attention_gradients.1 = (f32[2,128,1024]{2,1,0:T(8,128)S(1)}, bf16[4,4,128,256]{3,2,1,0:T(8,128)(2,1)}) custom-call(s32[3]{0:T(128)S(1)} %pad_add_fusion.place_ref, bf16[1024,128]{1,0:T(8,128)(2,1)S(1)} %get-tuple-element.22.refs_0_.own_q, bf16[1024,128]{1,0:T(8,128)(2,1)S(1)} %get-tuple-element.23.refs_1_.own_do, ...), custom_call_target="tpu_custom_call" | custom-call | flops 3221225472 | bytes 4194304 | tf_op jit(solution)/shard_map/attention_gradients/pallas_call | solution.py:272
  54.1 3.9 %all-to-all-start.3 = ((bf16[4,4,128,256]{3,2,1,0:T(8,128)(2,1)}), bf16[4,4,128,256]{3,2,1,0:T(8,128)(2,1)S(1)}, u32[]{:S(2)}, u32[]{:S(2)}) async-start(bf16[4,4,128,256]{3,2,1,0:T(8,128)(2,1)} %get-tuple-element.32), calls=%async_computation.3 | async-start | bytes 2097152 | tf_op jit(solution)/shard_map/all_to_all | solution.py:314
  58.0 0.3 query_gradients_by_token.1
  58.3 4.7 %collective-permute-start.3 = (bf16[128,1024]{1,0:T(8,128)(2,1)S(1)}, bf16[128,1024]{1,0:T(8,128)(2,1)S(1)}, u32[]{:S(2)}, u32[]{:S(2)}) collective-permute-start(bf16[128,1024]{1,0:T(8,128)(2,1)S(1)} %get-tuple-element.34), channel_id=1, source_target_pairs={{0,4},{4,0},{8,12},{12,8},{16,20},{20,16},{24,28},{28,24},{32,36},... | collective-permute-start | bytes 786440 | tf_op jit(solution)/shard_map/ppermute | solution.py:318
  63.0 4.8 %all-to-all-done.3.parts_ref = bf16[4,4,128,256]{3,2,1,0:T(8,128)(2,1)S(1)} async-done(((bf16[4,4,128,256]{3,2,1,0:T(8,128)(2,1)}), bf16[4,4,128,256]{3,2,1,0:T(8,128)(2,1)S(1)}, u32[]{:S(2)}, u32[]{:S(2)}) %all-to-all-start.3) | async-done | bytes 1048608 | tf_op jit(solution)/shard_map/all_to_all | solution.py:314
  67.8 0.1 sum_of_parts.2
  67.9 0.0 collective-permute-done.3.peer_ref
  67.9 21.0 %all_to_all.32.parts_ref = bf16[4,128,256]{2,1,0:T(8,128)(2,1)S(1)} all-to-all(bf16[4,128,256]{2,1,0:T(8,128)(2,1)S(1)} %sum_of_parts.2), channel_id=1, replica_groups={{0,32,64,96},{4,36,68,100},{8,40,72,104},{12,44,76,108},{16,48,80,112},..., dimensions={0} | all-to-all | bytes 524288 | tf_op jit(solution)/shard_map/all_to_all | solution.py:314
  89.0 14.6 %all_to_all.33.both_ref = f32[4,32,256]{2,1,0:T(8,128)S(1)} all-to-all(f32[4,32,256]{2,1,0:T(8,128)S(1)} %bitcast.5), channel_id=1, replica_groups=mesh['ctx'=128,'tp'=4] {'tp'}, dimensions={0} | all-to-all | bytes 262144 | tf_op jit(solution)/shard_map/all_to_all | solution.py:366
  103.6 0.9 gradients_by_token.1
  (4 shorter events, 0.1 us)
Async XLA Ops:
  24.6 15.9 %all-to-all-start.2 = ((bf16[4,4,128,256]{3,2,1,0:T(8,128)(2,1)}), bf16[4,4,128,256]{3,2,1,0:T(8,128)(2,1)S(1)}, u32[]{:S(2)}, u32[]{:S(2)}) async-start(bf16[4,4,128,256]{3,2,1,0:T(8,128)(2,1)} %broadcast_in_dim.17), calls=%async_computation.2 | async-start | bytes 2097152 | tf_op jit(solution)/shard_map/all_to_all | solution.py:314
  28.1 13.9 %collective-permute-start = (bf16[128,1024]{1,0:T(8,128)(2,1)}, bf16[128,1024]{1,0:T(8,128)(2,1)S(1)}, u32[]{:S(2)}, u32[]{:S(2)}) collective-permute-start(bf16[128,1024]{1,0:T(8,128)(2,1)} %q_ref.1), channel_id=1, source_target_pairs={{0,4},{4,0},{8,12},{12,8},{16,20},{20,16},{24,28},{28,24},{32,36},... | collective-permute-start | bytes 786440 | tf_op jit(solution)/shard_map/ppermute | solution.py:318
  30.1 12.4 %collective-permute-start.1 = (bf16[128,1024]{1,0:T(8,128)(2,1)}, bf16[128,1024]{1,0:T(8,128)(2,1)S(1)}, u32[]{:S(2)}, u32[]{:S(2)}) collective-permute-start(bf16[128,1024]{1,0:T(8,128)(2,1)} %do_ref.1), channel_id=1, source_target_pairs={{0,4},{4,0},{8,12},{12,8},{16,20},{20,16},{24,28},{28,24},{32,36},... | collective-permute-start | bytes 786440 | tf_op jit(solution)/shard_map/ppermute | solution.py:318
  35.0 1.0 copy-start
  36.0 0.9 copy-start.1
  44.0 6.1 %collective-permute-start.2 = (f32[24,256]{1,0:T(8,128)S(1)}, f32[24,256]{1,0:T(8,128)S(1)}, u32[]{:S(2)}, u32[]{:S(2)}) collective-permute-start(f32[24,256]{1,0:T(8,128)S(1)} %get-tuple-element.25.stats_ref), channel_id=1, source_target_pairs={{0,4},{4,0},{8,12},{12,8},{16,20},{20,16},{24,28},{28,24},{32,36},... | collective-permute-start | bytes 73736 | tf_op jit(solution)/shard_map/ppermute | solution.py:318
  54.1 13.7 %all-to-all-start.3 = ((bf16[4,4,128,256]{3,2,1,0:T(8,128)(2,1)}), bf16[4,4,128,256]{3,2,1,0:T(8,128)(2,1)S(1)}, u32[]{:S(2)}, u32[]{:S(2)}) async-start(bf16[4,4,128,256]{3,2,1,0:T(8,128)(2,1)} %get-tuple-element.32), calls=%async_computation.3 | async-start | bytes 2097152 | tf_op jit(solution)/shard_map/all_to_all | solution.py:314
  58.3 9.6 %collective-permute-start.3 = (bf16[128,1024]{1,0:T(8,128)(2,1)S(1)}, bf16[128,1024]{1,0:T(8,128)(2,1)S(1)}, u32[]{:S(2)}, u32[]{:S(2)}) collective-permute-start(bf16[128,1024]{1,0:T(8,128)(2,1)S(1)} %get-tuple-element.34), channel_id=1, source_target_pairs={{0,4},{4,0},{8,12},{12,8},{16,20},{20,16},{24,28},{28,24},{32,36},... | collective-permute-start | bytes 786440 | tf_op jit(solution)/shard_map/ppermute | solution.py:318

commit v7 on v5

--- a/solution.py
+++ b/solution.py
@@ -183,19 +183,15 @@
             out_ref[h, :, i * HEAD_SIZE : (i + 1) * HEAD_SIZE] = both_ref[i, :, h * HEAD_SIZE : (h + 1) * HEAD_SIZE]
 
 
-def finish_kernel(both_ref, dq_ref, peer_ref, key_ref, value_ref, query_ref, total, sems):
+def finish_kernel(both_ref, dq_ref, peer_ref, key_ref, value_ref, query_ref, wide, total, sems):
     heads = both_ref.shape[0]
-    copies = [
-        pltpu.make_async_copy(
-            both_ref.at[h, :, i * HEAD_SIZE : (i + 1) * HEAD_SIZE],
-            ref.at[:, h * HEAD_SIZE : (h + 1) * HEAD_SIZE],
-            sems.at[i, h],
-        )
-        for i, ref in enumerate((key_ref, value_ref))
-        for h in range(heads)
-    ]
-    for copy in copies:
-        copy.start()
+    copies = []
+    for i, ref in enumerate((key_ref, value_ref)):
+        for h in range(heads):
+            part = both_ref[h, :, i * HEAD_SIZE : (i + 1) * HEAD_SIZE]
+            wide[i, :, h * HEAD_SIZE : (h + 1) * HEAD_SIZE] = part.astype(F32)
+        copies.append(pltpu.make_async_copy(wide.at[i], ref, sems.at[i, 0]))
+        copies[-1].start()
     tokens = total.shape[0] // heads
     for h in range(heads):
         down = slice(h * tokens, (h + 1) * tokens)
@@ -351,13 +347,14 @@
     )
     dq_there = to_peer(dq_peer)
     partial = summed(exchange(dkv, along_y), BF16)
-    mine = summed(exchange(partial, along_z), F32)
+    mine = summed(exchange(partial, along_z), BF16)
     back = lax.all_to_all(mine.reshape(tp_count, here, 2 * HEAD_SIZE), "tp", 0, 0, tiled=True)
     shape = jax.ShapeDtypeStruct(key_heads_wide.shape, F32)
     key_gradient, value_gradient, grad_query = small(
         finish_kernel, "gradients_by_token", (shape, shape, jax.ShapeDtypeStruct(dq.shape, F32)),
         [WHOLE] * 3, (IN_HBM,) * 3,
-        [pltpu.VMEM(dq.shape, F32), pltpu.SemaphoreType.DMA((3, tp_count))], 4, back, dq, dq_there,
+        [pltpu.VMEM((2,) + shape.shape, F32), pltpu.VMEM(dq.shape, F32), pltpu.SemaphoreType.DMA((3, tp_count))], 4,
+        back, dq, dq_there,
     )
     return grad_query, key_gradient, value_gradient
 

time: 105 us -> 105 us (level)
  no operation moved by 1% of the time
where the time goes in v7:
time: 105 us; the launch traced here: 104 us
  starting transfers between devices  42.7 us (41%)
  blocking collectives  35.4 us (34%)
  waiting for transfers between devices  11.7 us (11%)
  Pallas kernels  9.25 us (9%)
  local copies, waits for them, and re-layouts  3 us (3%)
    all_to_all x2, blocking collectives, exchange(): lax.all_to_all(parts, AXES, 0, 0, axis_index_groups=lists, tiled=True)  22.9 us
    all_to_all x2, starting transfers between devices, exchange(): lax.all_to_all(parts, AXES, 0, 0, axis_index_groups=lists, tiled=True)  18.2 us
    ppermute x4, starting transfers between devices, to_peer(): lax.ppermute(array, 'ctx', [(c, c ^ 1) for c in range(lax.axis_size('ctx'...  13.3 us
    all_to_all x1, blocking collectives, shards(): lax.all_to_all(both, 'tp', 0, 0, tiled=True).reshape(rows, 2 * HEAD_SIZE)  12.5 us
    all_to_all x1, starting transfers between devices, shards(): lax.all_to_all(mine.reshape(tp_count, here, 2 * HEAD_SIZE), 'tp', 0, 0, t...  11.2 us
    all_to_all x2, waiting for transfers between devices, exchange(): lax.all_to_all(parts, AXES, 0, 0, axis_index_groups=lists, tiled=True)  6.53 us
    all_to_all x1, waiting for transfers between devices, shards(): lax.all_to_all(mine.reshape(tp_count, here, 2 * HEAD_SIZE), 'tp', 0, 0, t...  3.26 us
    pallas_call x1, Pallas kernels, attention_gradients(): pl.pallas_call(gradients_kernel, out_shape=(jax.ShapeDtypeStruct((PAIR, H...  3.16 us
  transfers between devices with their start and end apart: 7, of which 5 were waited for; matrix products, arithmetic and copies ran while one was open for 0% of the time, Pallas kernels for 3%

profile of v7, /device:TPU:1, one launch (start us, length us, event | category | flops | bytes accessed | tf_op | source)
XLA Modules:
  0.0 104.1 jit_solution(451619061200254133)
XLA Ops:
  0.6 0.9 broadcast_select_fusion.both_ref
  1.5 12.5 %all_to_all.30 = bf16[4,32,256]{2,1,0:T(8,128)(2,1)S(1)} all-to-all(bf16[4,32,256]{2,1,0:T(8,128)(2,1)S(1)} %keys_and_values_by_head.1), channel_id=1, replica_groups=mesh['ctx'=128,'tp'=4] {'tp'}, dimensions={0} | all-to-all | bytes 131072 | tf_op jit(solution)/shard_map/all_to_all | solution.py:331
  14.0 9.5 %all_to_all.31 = bf16[4,128,256]{2,1,0:T(8,128)(2,1)S(1)} all-to-all(bf16[4,128,256]{2,1,0:T(8,128)(2,1)S(1)} %broadcast_in_dim.16), channel_id=1, replica_groups={{0,32,64,96},{4,36,68,100},{8,40,72,104},{12,44,76,108},{16,48,80,112},..., dimensions={0} | all-to-all | bytes 524288 | tf_op jit(solution)/shard_map/all_to_all | solution.py:300
  23.5 1.1 %broadcast_in_dim.17 = bf16[4,4,128,256]{3,2,1,0:T(8,128)(2,1)} broadcast(bf16[4,128,256]{2,1,0:T(8,128)(2,1)S(1)} %all_to_all.31), dimensions={1,2,3} | broadcast | bytes 1310720 | tf_op jit(solution)/shard_map/broadcast_in_dim | solution.py:333
  24.6 3.5 %all-to-all-start.2 = ((bf16[4,4,128,256]{3,2,1,0:T(8,128)(2,1)}), bf16[4,4,128,256]{3,2,1,0:T(8,128)(2,1)S(1)}, u32[]{:S(2)}, u32[]{:S(2)}) async-start(bf16[4,4,128,256]{3,2,1,0:T(8,128)(2,1)} %broadcast_in_dim.17), calls=%async_computation.2 | async-start | bytes 2097152 | tf_op jit(solution)/shard_map/all_to_all | solution.py:300
  28.1 1.9 %collective-permute-start = (bf16[128,1024]{1,0:T(8,128)(2,1)}, bf16[128,1024]{1,0:T(8,128)(2,1)S(1)}, u32[]{:S(2)}, u32[]{:S(2)}) collective-permute-start(bf16[128,1024]{1,0:T(8,128)(2,1)} %q_ref.1), channel_id=1, source_target_pairs={{0,4},{4,0},{8,12},{12,8},{16,20},{20,16},{24,28},{28,24},{32,36},... | collective-permute-start | bytes 786440 | tf_op jit(solution)/shard_map/ppermute | solution.py:304
  30.1 4.9 %collective-permute-start.1 = (bf16[128,1024]{1,0:T(8,128)(2,1)}, bf16[128,1024]{1,0:T(8,128)(2,1)S(1)}, u32[]{:S(2)}, u32[]{:S(2)}) collective-permute-start(bf16[128,1024]{1,0:T(8,128)(2,1)} %do_ref.1), channel_id=1, source_target_pairs={{0,4},{4,0},{8,12},{12,8},{16,20},{20,16},{24,28},{28,24},{32,36},... | collective-permute-start | bytes 786440 | tf_op jit(solution)/shard_map/ppermute | solution.py:304
  35.0 0.0 copy-start
  35.0 0.9 copy-done
  36.0 0.0 copy-start.1
  36.0 0.9 copy-done.1
  36.9 0.1 queries_by_head.1
  37.1 0.1 pad_add_fusion.place_ref
  37.1 3.3 %all-to-all-done.2.refs_2_.kv_ref = bf16[4,4,128,256]{3,2,1,0:T(8,128)(2,1)S(1)} async-done(((bf16[4,4,128,256]{3,2,1,0:T(8,128)(2,1)}), bf16[4,4,128,256]{3,2,1,0:T(8,128)(2,1)S(1)}, u32[]{:S(2)}, u32[]{:S(2)}) %all-to-all-start.2) | async-done | bytes 1048608 | tf_op jit(solution)/shard_map/all_to_all | solution.py:300
  40.5 1.6 %row_statistics.2 = (f32[24,256]{1,0:T(8,128)S(1)}, f32[8,1024]{1,0:T(8,128)S(1)}, bf16[4,512,1024]{2,1,0:T(8,128)(2,1)S(1)}, f32[4,512,1024]{2,1,0:T(8,128)S(1)}) custom-call(s32[3]{0:T(128)S(1)} %pad_add_fusion.place_ref, bf16[1024,128]{1,0:T(8,128)(2,1)S(1)} %get-tuple-element.20.refs_0_.own_q, bf16[1024,128]{1,0:T(8,128)(2,1)S(1)} %get-tuple-element.21.refs_1_.own_do, ...), custom_call_target="tpu_custom_call" | custom-call | flops 1073741824 | bytes 1048576 | tf_op jit(solution)/shard_map/row_statistics/pallas_call | solution.py:238
  42.1 0.0 collective-permute-done.refs_0_.peer_q
  42.1 0.4 collective-permute-done.1.refs_1_.peer_do
  42.4 1.5 %row_statistics.3 = (f32[24,256]{1,0:T(8,128)S(1)}, f32[8,1024]{1,0:T(8,128)S(1)}, bf16[4,512,1024]{2,1,0:T(8,128)(2,1)S(1)}, f32[4,512,1024]{2,1,0:T(8,128)S(1)}) custom-call(s32[3]{0:T(128)S(1)} %pad_add_fusion.place_ref, bf16[128,1024]{1,0:T(8,128)(2,1)S(1)} %collective-permute-done.refs_0_.peer_q, ...), custom_call_target="tpu_custom_call" | custom-call | flops 1073741824 | bytes 1048576 | tf_op jit(solution)/shard_map/row_statistics/pallas_call | solution.py:238
  44.0 4.3 %collective-permute-start.2 = (f32[24,256]{1,0:T(8,128)S(1)}, f32[24,256]{1,0:T(8,128)S(1)}, u32[]{:S(2)}, u32[]{:S(2)}) collective-permute-start(f32[24,256]{1,0:T(8,128)S(1)} %get-tuple-element.23.stats_ref), channel_id=1, source_target_pairs={{0,4},{4,0},{8,12},{12,8},{16,20},{20,16},{24,28},{28,24},{32,36},... | collective-permute-start | bytes 73736 | tf_op jit(solution)/shard_map/ppermute | solution.py:304
  48.3 0.2 keys_by_column.1.k_cols
  48.5 1.5 %collective-permute-done.2.other_ref = f32[24,256]{1,0:T(8,128)S(1)} collective-permute-done((f32[24,256]{1,0:T(8,128)S(1)}, f32[24,256]{1,0:T(8,128)S(1)}, u32[]{:S(2)}, u32[]{:S(2)}) %collective-permute-start.2) | collective-permute-done | bytes 24608 | tf_op jit(solution)/shard_map/ppermute | solution.py:304
  50.0 3.2 %attention_gradients.1 = (f32[2,128,1024]{2,1,0:T(8,128)S(1)}, bf16[4,4,128,256]{3,2,1,0:T(8,128)(2,1)S(1)}) custom-call(s32[3]{0:T(128)S(1)} %pad_add_fusion.place_ref, bf16[1024,128]{1,0:T(8,128)(2,1)S(1)} %get-tuple-element.20.refs_0_.own_q, bf16[1024,128]{1,0:T(8,128)(2,1)S(1)} %get-tuple-element.21.refs_1_.own_do, ...), custom_call_target="tpu_custom_call" | custom-call | flops 3221225472 | bytes 4194304 | tf_op jit(solution)/shard_map/attention_gradients/pallas_call | solution.py:260
  53.2 13.5 %all_to_all.32.parts_ref = bf16[4,4,128,256]{3,2,1,0:T(8,128)(2,1)S(1)} all-to-all(bf16[4,4,128,256]{3,2,1,0:T(8,128)(2,1)S(1)} %get-tuple-element.30), channel_id=1, replica_groups={{0,8,16,24},{4,12,20,28},{32,40,48,56},{36,44,52,60},{64,72,80,88},{68,..., dimensions={0} | all-to-all | bytes 2097152 | tf_op jit(solution)/shard_map/all_to_all | solution.py:300
  66.7 0.8 sum_of_parts.2
  67.5 14.7 %all-to-all-start.4 = ((bf16[4,128,256]{2,1,0:T(8,128)(2,1)}), bf16[4,128,256]{2,1,0:T(8,128)(2,1)S(1)}, u32[]{:S(2)}, u32[]{:S(2)}) async-start(bf16[4,128,256]{2,1,0:T(8,128)(2,1)} %sum_of_parts.2), calls=%async_computation.4 | async-start | bytes 524288 | tf_op jit(solution)/shard_map/all_to_all | solution.py:300
  82.2 0.3 query_gradients_by_token.1
  82.5 2.2 %collective-permute-start.3 = (bf16[128,1024]{1,0:T(8,128)(2,1)S(1)}, bf16[128,1024]{1,0:T(8,128)(2,1)S(1)}, u32[]{:S(2)}, u32[]{:S(2)}) collective-permute-start(bf16[128,1024]{1,0:T(8,128)(2,1)S(1)} %get-tuple-element.33), channel_id=1, source_target_pairs={{0,4},{4,0},{8,12},{12,8},{16,20},{20,16},{24,28},{28,24},{32,36},... | collective-permute-start | bytes 786440 | tf_op jit(solution)/shard_map/ppermute | solution.py:304
  84.7 3.2 %all-to-all-done.4.parts_ref = bf16[4,128,256]{2,1,0:T(8,128)(2,1)S(1)} async-done(((bf16[4,128,256]{2,1,0:T(8,128)(2,1)}), bf16[4,128,256]{2,1,0:T(8,128)(2,1)S(1)}, u32[]{:S(2)}, u32[]{:S(2)}) %all-to-all-start.4) | async-done | bytes 262176 | tf_op jit(solution)/shard_map/all_to_all | solution.py:300
  87.8 0.7 sum_of_parts.3
  88.5 11.2 %all-to-all-start.5 = ((bf16[4,32,256]{2,1,0:T(8,128)(2,1)}), bf16[4,32,256]{2,1,0:T(8,128)(2,1)S(1)}, u32[]{:S(2)}, u32[]{:S(2)}) async-start(bf16[4,32,256]{2,1,0:T(8,128)(2,1)} %bitcast.4), calls=%async_computation.5 | async-start | bytes 131072 | tf_op jit(solution)/shard_map/all_to_all | solution.py:351
  99.7 0.0 collective-permute-done.3.peer_ref
  99.7 3.3 %all-to-all-done.5.both_ref = bf16[4,32,256]{2,1,0:T(8,128)(2,1)S(1)} async-done(((bf16[4,32,256]{2,1,0:T(8,128)(2,1)}), bf16[4,32,256]{2,1,0:T(8,128)(2,1)S(1)}, u32[]{:S(2)}, u32[]{:S(2)}) %all-to-all-start.5) | async-done | bytes 65568 | tf_op jit(solution)/shard_map/all_to_all | solution.py:351
  103.0 0.9 gradients_by_token.1
  (3 shorter events, 0.0 us)
Async XLA Ops:
  24.6 15.9 %all-to-all-start.2 = ((bf16[4,4,128,256]{3,2,1,0:T(8,128)(2,1)}), bf16[4,4,128,256]{3,2,1,0:T(8,128)(2,1)S(1)}, u32[]{:S(2)}, u32[]{:S(2)}) async-start(bf16[4,4,128,256]{3,2,1,0:T(8,128)(2,1)} %broadcast_in_dim.17), calls=%async_computation.2 | async-start | bytes 2097152 | tf_op jit(solution)/shard_map/all_to_all | solution.py:300
  28.1 13.9 %collective-permute-start = (bf16[128,1024]{1,0:T(8,128)(2,1)}, bf16[128,1024]{1,0:T(8,128)(2,1)S(1)}, u32[]{:S(2)}, u32[]{:S(2)}) collective-permute-start(bf16[128,1024]{1,0:T(8,128)(2,1)} %q_ref.1), channel_id=1, source_target_pairs={{0,4},{4,0},{8,12},{12,8},{16,20},{20,16},{24,28},{28,24},{32,36},... | collective-permute-start | bytes 786440 | tf_op jit(solution)/shard_map/ppermute | solution.py:304
  30.1 12.4 %collective-permute-start.1 = (bf16[128,1024]{1,0:T(8,128)(2,1)}, bf16[128,1024]{1,0:T(8,128)(2,1)S(1)}, u32[]{:S(2)}, u32[]{:S(2)}) collective-permute-start(bf16[128,1024]{1,0:T(8,128)(2,1)} %do_ref.1), channel_id=1, source_target_pairs={{0,4},{4,0},{8,12},{12,8},{16,20},{20,16},{24,28},{28,24},{32,36},... | collective-permute-start | bytes 786440 | tf_op jit(solution)/shard_map/ppermute | solution.py:304
  35.0 1.0 copy-start
  36.0 0.9 copy-start.1
  44.0 6.1 %collective-permute-start.2 = (f32[24,256]{1,0:T(8,128)S(1)}, f32[24,256]{1,0:T(8,128)S(1)}, u32[]{:S(2)}, u32[]{:S(2)}) collective-permute-start(f32[24,256]{1,0:T(8,128)S(1)} %get-tuple-element.23.stats_ref), channel_id=1, source_target_pairs={{0,4},{4,0},{8,12},{12,8},{16,20},{20,16},{24,28},{28,24},{32,36},... | collective-permute-start | bytes 73736 | tf_op jit(solution)/shard_map/ppermute | solution.py:304
  67.5 20.3 %all-to-all-start.4 = ((bf16[4,128,256]{2,1,0:T(8,128)(2,1)}), bf16[4,128,256]{2,1,0:T(8,128)(2,1)S(1)}, u32[]{:S(2)}, u32[]{:S(2)}) async-start(bf16[4,128,256]{2,1,0:T(8,128)(2,1)} %sum_of_parts.2), calls=%async_computation.4 | async-start | bytes 524288 | tf_op jit(solution)/shard_map/all_to_all | solution.py:300
  82.5 17.2 %collective-permute-start.3 = (bf16[128,1024]{1,0:T(8,128)(2,1)S(1)}, bf16[128,1024]{1,0:T(8,128)(2,1)S(1)}, u32[]{:S(2)}, u32[]{:S(2)}) collective-permute-start(bf16[128,1024]{1,0:T(8,128)(2,1)S(1)} %get-tuple-element.33), channel_id=1, source_target_pairs={{0,4},{4,0},{8,12},{12,8},{16,20},{20,16},{24,28},{28,24},{32,36},... | collective-permute-start | bytes 786440 | tf_op jit(solution)/shard_map/ppermute | solution.py:304
  88.5 14.5 %all-to-all-start.5 = ((bf16[4,32,256]{2,1,0:T(8,128)(2,1)}), bf16[4,32,256]{2,1,0:T(8,128)(2,1)S(1)}, u32[]{:S(2)}, u32[]{:S(2)}) async-start(bf16[4,32,256]{2,1,0:T(8,128)(2,1)} %bitcast.4), calls=%async_computation.5 | async-start | bytes 131072 | tf_op jit(solution)/shard_map/all_to_all | solution.py:351
